TPU v7x, 32 devices: a whole 2x2x4 slice. The times are simulated.
32 devices in a mesh: ctx: 8 (over z, core), fsdp: 4 (over y, x).
Axes of the slice: x: 2, y: 2, z: 4, core: 2. Of those that a mesh axis runs over, the one named last changes fastest.
Arguments:
- inputs: bfloat16 [2, 4, 1024, 1536], P(None, 'fsdp', 'ctx'), may hold values from -6 to 6
- cotangent: bfloat16 [2, 4, 1024, 1536], P(None, 'fsdp', 'ctx'), may hold values from -6 to 6
- lengths: int32 [2, 4, 4], P(None, 'fsdp'), may hold values from 1 to 512, 1024 in all within a row
- deal: int32 [2, 8], replicated, may hold values from 0 to 7, each once within a row
- norm1_gain: bfloat16 [1536], P(('ctx', 'fsdp')), may hold values from 0.5 to 1.5
- w_query: bfloat16 [1536, 1536], P(('ctx', 'fsdp')), may hold values from -0.15625 to 0.15625
- w_key: bfloat16 [1536, 1536], P(('ctx', 'fsdp')), may hold values from -0.15625 to 0.15625
- w_value: bfloat16 [1536, 1536], P(('ctx', 'fsdp')), may hold values from -0.15625 to 0.15625
- w_outgate: bfloat16 [1536, 1536], P(('ctx', 'fsdp')), may hold values from -0.15625 to 0.15625
- w_out: bfloat16 [1536, 1536], P(('ctx', 'fsdp')), may hold values from -1.25 to 1.25
- forget_weight: bfloat16 [1536, 24], P(('ctx', 'fsdp')), may hold values from -0.15625 to 0.15625
- forget_bias: float32 [24], replicated, may hold values from 2 to 9
- norm2_gain: bfloat16 [1536], P(('ctx', 'fsdp')), may hold values from 0.5 to 1.5
- w_gate: bfloat16 [1536, 4096], P(('ctx', 'fsdp')), may hold values from -0.15625 to 0.15625
- w_up: bfloat16 [1536, 4096], P(('ctx', 'fsdp')), may hold values from -0.15625 to 0.15625
- w_down: bfloat16 [4096, 1536], P(('ctx', 'fsdp')), may hold values from -0.09375 to 0.09375
Outputs:
- output: bfloat16 [2, 4, 1024, 1536], P(None, 'fsdp', 'ctx')
- grad_inputs: float32 [2, 4, 1024, 1536], P(None, 'fsdp', 'ctx')
- grad_norm1_gain: float32 [1536], P(('ctx', 'fsdp'))
- grad_w_query: float32 [1536, 1536], P(('ctx', 'fsdp'))
- grad_w_key: float32 [1536, 1536], P(('ctx', 'fsdp'))
- grad_w_value: float32 [1536, 1536], P(('ctx', 'fsdp'))
- grad_w_outgate: float32 [1536, 1536], P(('ctx', 'fsdp'))
- grad_w_out: float32 [1536, 1536], P(('ctx', 'fsdp'))
- grad_forget_weight: float32 [1536, 24], P(('ctx', 'fsdp'))
- grad_forget_bias: float32 [24], replicated
- grad_norm2_gain: float32 [1536], P(('ctx', 'fsdp'))
- grad_w_gate: float32 [1536, 4096], P(('ctx', 'fsdp'))
- grad_w_up: float32 [1536, 4096], P(('ctx', 'fsdp'))
- grad_w_down: float32 [4096, 1536], P(('ctx', 'fsdp'))
Inputs may be any that keep to these rules, and one draw needn't show every extreme that they name: Each row of lengths holds the 4 document lengths of one stream, summing to 1024, the longest exactly 512. Each row of deal is a permutation of the block pairs.
All inputs are finite; a program needn't handle non-finite values.
Results may differ from a plain program's by a relative error of at most 0.025.
Values may be sent and summed in bfloat16 or wider, within the bound.
No kernel may reach another device: no remote copies, remote signals or barrier semaphores. Data moves between devices by JAX's collectives and lax.ppermute only.
A program may use at most 384 MiB of HBM per device.

v0:
```python
import jax
import jax.numpy as jnp
from jax import lax
from jax.sharding import PartitionSpec as P

KEY_TILE = 512


norm_eps = 1e-06
very_low = -1e30
highest = lax.Precision.HIGHEST


def product(left, right):
    return jnp.dot(left, right, preferred_element_type=jnp.float32)


def product_left(left, right):
    return lax.dot_general(
        left, right, (((0,), (0,)), ((), ())), preferred_element_type=jnp.float32
    )


def product_right(left, right):
    return lax.dot_general(
        left, right, (((1,), (1,)), ((), ())), preferred_element_type=jnp.float32
    )


def doc_begins(lengths_row, total):
    ends = jnp.cumsum(lengths_row)
    begins = ends - lengths_row
    place = jnp.arange(total, dtype=jnp.int32)
    inside = (place[:, None] >= begins[None, :]) & (place[:, None] < ends[None, :])
    return jnp.sum(jnp.where(inside, begins[None, :], 0), axis=1)


def slot_order(deal_row, count):
    return jnp.stack([deal_row, 2 * count - 1 - deal_row], axis=1).reshape(-1)


def into_natural(array, order):
    count = order.shape[0]
    numbers = jnp.arange(count, dtype=jnp.int32)
    source = jnp.sum(jnp.where(order[None, :] == numbers[:, None], numbers[None, :], 0), axis=1)
    blocks = array.reshape((count, array.shape[0] // count) + array.shape[1:])
    return jnp.take(blocks, source, axis=0).reshape(array.shape)


def into_slots(array, order):
    count = order.shape[0]
    blocks = array.reshape((count, array.shape[0] // count) + array.shape[1:])
    return jnp.take(blocks, order, axis=0).reshape(array.shape)


def add_rows(whole, part, first):
    current = lax.dynamic_slice_in_dim(whole, first, part.shape[0], 0)
    return lax.dynamic_update_slice_in_dim(whole, current + part, first, 0)


def tile_scores(
    query_block, query_cumul, query_place, query_begin, keys_nat, cumul_nat, number, scale
):
    first = number * KEY_TILE
    key_tile = lax.dynamic_slice_in_dim(keys_nat, first, KEY_TILE, 0)
    cumul_tile = lax.dynamic_slice_in_dim(cumul_nat, first, KEY_TILE, 0)
    place_tile = first + jnp.arange(KEY_TILE, dtype=jnp.int32)
    scores = (
        jnp.einsum("rhd,thd->hrt", query_block, key_tile, preferred_element_type=jnp.float32)
        * scale
    )
    scores = scores + query_cumul.T[:, :, None] - cumul_tile.T[:, None, :]
    mask = (place_tile[None, :] <= query_place[:, None]) & (
        place_tile[None, :] >= query_begin[:, None]
    )
    return (scores, mask)


def tile_range(query_place, query_begin):
    rows = query_place.shape[0]
    return (query_begin[0] // KEY_TILE, query_place[rows - 1] // KEY_TILE + 1)


def attend(
    query_block, query_cumul, query_place, query_begin, keys_nat, values_nat, cumul_nat, scale
):
    rows, heads, depth = query_block.shape
    first_tile, last_tile = tile_range(query_place, query_begin)

    def first_pass(number, carry):
        peak, weight_sum = carry
        scores, mask = tile_scores(
            query_block, query_cumul, query_place, query_begin, keys_nat, cumul_nat, number, scale
        )
        masked = jnp.where(mask[None], scores, very_low)
        new_peak = jnp.maximum(peak, jnp.max(masked, axis=2))
        fresh = jnp.where(mask[None], jnp.exp(masked - new_peak[:, :, None]), 0.0)
        return (new_peak, weight_sum * jnp.exp(peak - new_peak) + jnp.sum(fresh, axis=2))

    start = (jnp.full((heads, rows), very_low, jnp.float32), jnp.zeros((heads, rows), jnp.float32))
    peak, weight_sum = lax.fori_loop(first_tile, last_tile, first_pass, start)
    log_total = peak + jnp.log(weight_sum)

    def second_pass(number, output):
        scores, mask = tile_scores(
            query_block, query_cumul, query_place, query_begin, keys_nat, cumul_nat, number, scale
        )
        probs = jnp.where(mask[None], jnp.exp(scores - log_total[:, :, None]), 0.0).astype(
            jnp.bfloat16
        )
        value_tile = lax.dynamic_slice_in_dim(values_nat, number * KEY_TILE, KEY_TILE, 0)
        return output + jnp.einsum(
            "hrt,thd->rhd", probs, value_tile, preferred_element_type=jnp.float32
        )

    output = lax.fori_loop(
        first_tile, last_tile, second_pass, jnp.zeros((rows, heads, depth), jnp.float32)
    )
    return (output, log_total)


def attend_back(
    query_block,
    query_cumul,
    query_place,
    query_begin,
    output_grad,
    delta,
    log_total,
    keys_nat,
    values_nat,
    cumul_nat,
    scale,
    sums,
):
    rows, heads, depth = query_block.shape
    first_tile, last_tile = tile_range(query_place, query_begin)

    def back_step(number, state):
        query_grad, key_grad, value_grad, cumul_grad, query_cumul_grad = state
        first = number * KEY_TILE
        scores, mask = tile_scores(
            query_block, query_cumul, query_place, query_begin, keys_nat, cumul_nat, number, scale
        )
        key_tile = lax.dynamic_slice_in_dim(keys_nat, first, KEY_TILE, 0)
        value_tile = lax.dynamic_slice_in_dim(values_nat, first, KEY_TILE, 0)
        probs = jnp.where(mask[None], jnp.exp(scores - log_total[:, :, None]), 0.0)
        prob_grad = jnp.einsum(
            "rhd,thd->hrt", output_grad, value_tile, preferred_element_type=jnp.float32
        )
        score_grad = (probs * (prob_grad - delta.T[:, :, None])).astype(jnp.bfloat16)
        query_grad = (
            query_grad
            + jnp.einsum("hrt,thd->rhd", score_grad, key_tile, preferred_element_type=jnp.float32)
            * scale
        )
        key_part = (
            jnp.einsum("hrt,rhd->thd", score_grad, query_block, preferred_element_type=jnp.float32)
            * scale
        )
        value_part = jnp.einsum(
            "hrt,rhd->thd",
            probs.astype(jnp.bfloat16),
            output_grad,
            preferred_element_type=jnp.float32,
        )
        wide_grad = score_grad.astype(jnp.float32)
        query_cumul_grad = query_cumul_grad + jnp.sum(wide_grad, axis=2)
        cumul_part = -jnp.sum(wide_grad, axis=1).T
        key_grad = add_rows(key_grad, key_part, first)
        value_grad = add_rows(value_grad, value_part, first)
        cumul_grad = add_rows(cumul_grad, cumul_part, first)
        return (query_grad, key_grad, value_grad, cumul_grad, query_cumul_grad)

    start = (
        jnp.zeros((rows, heads, depth), jnp.float32),
        sums[0],
        sums[1],
        sums[2],
        jnp.zeros((heads, rows), jnp.float32),
    )
    query_grad, key_grad, value_grad, cumul_grad, query_cumul_grad = lax.fori_loop(
        first_tile, last_tile, back_step, start
    )
    cumul_grad = add_rows(cumul_grad, query_cumul_grad.T, query_place[0])
    return (query_grad, (key_grad, value_grad, cumul_grad))


def reduce_weight_grads(kept):
    (
        normed,
        gated,
        normed_two,
        activ,
        attn_right,
        branch_grad,
        ffn_right,
        upstream,
        normed_wide,
        logit_grad,
        gain_one_rows,
        gain_two_rows,
        bias_rows,
    ) = kept
    wide = lax.psum_scatter(
        jnp.concatenate(
            [
                product_left(normed, attn_right),
                product_left(gated, branch_grad),
                product_left(normed_two, ffn_right),
            ],
            axis=1,
        ),
        ("ctx", "fsdp"),
        scatter_dimension=0,
        tiled=True,
    )
    down = lax.psum_scatter(
        product_left(activ, upstream), ("ctx", "fsdp"), scatter_dimension=0, tiled=True
    )
    forget_part = jnp.dot(normed_wide.T, logit_grad, precision=highest)
    first_gain = jnp.sum(gain_one_rows, axis=0)
    second_gain = jnp.sum(gain_two_rows, axis=0)
    small = lax.psum_scatter(
        jnp.concatenate([forget_part, first_gain[:, None], second_gain[:, None]], axis=1),
        ("ctx", "fsdp"),
        scatter_dimension=0,
        tiled=True,
    )
    bias = lax.psum(jnp.sum(bias_rows, axis=0), ("ctx", "fsdp"))
    return (wide, down, small, bias)


def per_device(
    inputs,
    cotangent,
    lengths,
    deal,
    norm1_gain,
    w_query,
    w_key,
    w_value,
    w_outgate,
    w_out,
    forget_weight,
    forget_bias,
    norm2_gain,
    w_gate,
    w_up,
    w_down,
):
    ctx_count = lax.axis_size("ctx")
    ctx_place = lax.axis_index("ctx")
    micro = inputs.shape[0]
    tokens = inputs.shape[2]
    width = inputs.shape[3]
    block = tokens // 2
    total = tokens * ctx_count
    heads = forget_bias.shape[0]
    depth = width // heads
    scale = depth ** (-0.5)

    def fetch_weights():
        return (
            lax.all_gather(norm1_gain, ("ctx", "fsdp"), axis=0, tiled=True),
            lax.all_gather(w_query, ("ctx", "fsdp"), axis=0, tiled=True),
            lax.all_gather(w_key, ("ctx", "fsdp"), axis=0, tiled=True),
            lax.all_gather(w_value, ("ctx", "fsdp"), axis=0, tiled=True),
            lax.all_gather(w_outgate, ("ctx", "fsdp"), axis=0, tiled=True),
            lax.all_gather(w_out, ("ctx", "fsdp"), axis=0, tiled=True),
            lax.all_gather(forget_weight, ("ctx", "fsdp"), axis=0, tiled=True),
            lax.all_gather(norm2_gain, ("ctx", "fsdp"), axis=0, tiled=True),
            lax.all_gather(w_gate, ("ctx", "fsdp"), axis=0, tiled=True),
            lax.all_gather(w_up, ("ctx", "fsdp"), axis=0, tiled=True),
            lax.all_gather(w_down, ("ctx", "fsdp"), axis=0, tiled=True),
        )

    def fetch_keys(keys_own, values_own, forget_own, order):
        keys_all, values_all, forget_all = (
            lax.all_gather(keys_own, "ctx", axis=0, tiled=True),
            lax.all_gather(values_own, "ctx", axis=0, tiled=True),
            lax.all_gather(forget_own, "ctx", axis=0, tiled=True),
        )
        keys_nat = into_natural(keys_all, order).reshape(total, heads, depth)
        values_nat = into_natural(values_all, order).reshape(total, heads, depth)
        cumul_nat = jnp.cumsum(into_natural(forget_all, order).astype(jnp.float32), axis=0)
        return (keys_nat, values_nat, cumul_nat)

    outputs = []
    input_grads = []
    kept_list = []
    grad_sums = None
    for index in range(micro):
        weights = fetch_weights()
        gain_one, wq, wk, wv, wog, wo, wf, gain_two, wgate, wup, wdown = weights
        stream = inputs[index, 0].astype(jnp.float32)
        order = slot_order(deal[index], ctx_count)
        own_blocks = lax.dynamic_slice_in_dim(order, 2 * ctx_place, 2, 0)
        own_place = (
            own_blocks[:, None] * block + jnp.arange(block, dtype=jnp.int32)[None, :]
        ).reshape(tokens)
        begins = doc_begins(lengths[index, 0], total)
        own_begin = jnp.take(begins, own_place)
        norm_one = lax.rsqrt(jnp.mean(stream * stream, axis=-1, keepdims=True) + norm_eps)
        normed = (stream * norm_one * gain_one.astype(jnp.float32)).astype(jnp.bfloat16)
        queries = product(normed, wq).astype(jnp.bfloat16)
        keys_own = product(normed, wk).astype(jnp.bfloat16)
        values_own = product(normed, wv).astype(jnp.bfloat16)
        outgate = product(normed, wog)
        normed_wide = normed.astype(jnp.float32)
        forget_wide = wf.astype(jnp.float32)
        forget_logit = jnp.dot(normed_wide, forget_wide, precision=highest) + forget_bias
        forget_own = jax.nn.log_sigmoid(forget_logit).astype(jnp.bfloat16)
        keys_nat, values_nat, cumul_nat = fetch_keys(keys_own, values_own, forget_own, order)
        own_cumul = jnp.take(cumul_nat, own_place, axis=0)
        query_heads = queries.reshape(tokens, heads, depth)
        attended_parts = []
        log_totals = []
        for half in range(2):
            rows = slice(half * block, (half + 1) * block)
            part, log_total = attend(
                query_heads[rows],
                own_cumul[rows],
                own_place[rows],
                own_begin[rows],
                keys_nat,
                values_nat,
                cumul_nat,
                scale,
            )
            attended_parts.append(part)
            log_totals.append(log_total)
        attended = jnp.concatenate(attended_parts, axis=0).reshape(tokens, width)
        gate_open = jax.nn.sigmoid(outgate)
        gated = (attended * gate_open).astype(jnp.bfloat16)
        middle = stream + product(gated, wo)
        norm_two = lax.rsqrt(jnp.mean(middle * middle, axis=-1, keepdims=True) + norm_eps)
        normed_two = (middle * norm_two * gain_two.astype(jnp.float32)).astype(jnp.bfloat16)
        gate_pre = product(normed_two, wgate)
        up_pre = product(normed_two, wup)
        gate_sig = jax.nn.sigmoid(gate_pre)
        activ = (gate_pre * gate_sig * up_pre).astype(jnp.bfloat16)
        outputs.append((middle + product(activ, wdown)).astype(jnp.bfloat16))
        gain_one, wq, wk, wv, wog, wo, wf, gain_two, wgate, wup, wdown = fetch_weights()
        upstream = cotangent[index, 0]
        grad_activ = product_right(upstream, wdown)
        silu_grad = gate_sig * (1.0 + gate_pre * (1.0 - gate_sig))
        gate_grad = (grad_activ * up_pre * silu_grad).astype(jnp.bfloat16)
        up_grad = (grad_activ * gate_pre * gate_sig).astype(jnp.bfloat16)
        normed_two_grad = product_right(gate_grad, wgate) + product_right(up_grad, wup)
        unit_two = middle * norm_two
        gain_two_rows = normed_two_grad * unit_two
        scaled_two = normed_two_grad * gain_two.astype(jnp.float32)
        middle_grad = upstream.astype(jnp.float32) + norm_two * (
            scaled_two - unit_two * jnp.mean(scaled_two * unit_two, axis=-1, keepdims=True)
        )
        branch_grad = middle_grad.astype(jnp.bfloat16)
        gated_grad = product_right(branch_grad, wo)
        output_grad = (gated_grad * gate_open).astype(jnp.bfloat16)
        outgate_grad = (gated_grad * attended * gate_open * (1.0 - gate_open)).astype(jnp.bfloat16)
        output_heads = output_grad.reshape(tokens, heads, depth)
        delta = jnp.sum(
            output_heads.astype(jnp.float32) * attended.reshape(tokens, heads, depth), axis=2
        )
        keys_nat, values_nat, cumul_nat = fetch_keys(keys_own, values_own, forget_own, order)
        sums = (
            jnp.zeros((total, heads, depth), jnp.float32),
            jnp.zeros((total, heads, depth), jnp.float32),
            jnp.zeros((total, heads), jnp.float32),
        )
        query_parts = []
        for half in range(2):
            rows = slice(half * block, (half + 1) * block)
            query_part, sums = attend_back(
                query_heads[rows],
                own_cumul[rows],
                own_place[rows],
                own_begin[rows],
                output_heads[rows],
                delta[rows],
                log_totals[half],
                keys_nat,
                values_nat,
                cumul_nat,
                scale,
                sums,
            )
            query_parts.append(query_part)
        key_grad, value_grad, cumul_grad = sums
        forget_grad = jnp.cumsum(cumul_grad[::-1], axis=0)[::-1]
        slot_keys = into_slots(key_grad.reshape(total, width), order)
        slot_values = into_slots(value_grad.reshape(total, width), order)
        slot_forget = into_slots(forget_grad, order)
        own_key_grad, own_value_grad, own_forget_grad = (
            lax.psum_scatter(
                slot_keys.astype(jnp.bfloat16), "ctx", scatter_dimension=0, tiled=True
            ).astype(jnp.float32),
            lax.psum_scatter(
                slot_values.astype(jnp.bfloat16), "ctx", scatter_dimension=0, tiled=True
            ).astype(jnp.float32),
            lax.psum_scatter(
                slot_forget.astype(jnp.bfloat16), "ctx", scatter_dimension=0, tiled=True
            ).astype(jnp.float32),
        )
        query_grad_low = (
            jnp.concatenate(query_parts, axis=0).reshape(tokens, width).astype(jnp.bfloat16)
        )
        key_grad_low = own_key_grad.astype(jnp.bfloat16)
        value_grad_low = own_value_grad.astype(jnp.bfloat16)
        logit_grad = own_forget_grad * jax.nn.sigmoid(-forget_logit)
        normed_grad = (
            product_right(query_grad_low, wq)
            + product_right(key_grad_low, wk)
            + product_right(value_grad_low, wv)
            + product_right(outgate_grad, wog)
        )
        normed_grad = normed_grad + jnp.dot(logit_grad, forget_wide.T, precision=highest)
        unit_one = stream * norm_one
        gain_one_rows = normed_grad * unit_one
        scaled_one = normed_grad * gain_one.astype(jnp.float32)
        input_grads.append(
            middle_grad
            + norm_one
            * (scaled_one - unit_one * jnp.mean(scaled_one * unit_one, axis=-1, keepdims=True))
        )
        attn_right = jnp.concatenate(
            [query_grad_low, key_grad_low, value_grad_low, outgate_grad], axis=1
        )
        ffn_right = jnp.concatenate([gate_grad, up_grad], axis=1)
        bias_rows = jnp.sum(logit_grad, axis=0)[None, :]
        kept = (
            normed,
            gated,
            normed_two,
            activ,
            attn_right,
            branch_grad,
            ffn_right,
            upstream,
            normed_wide,
            logit_grad,
            gain_one_rows,
            gain_two_rows,
            bias_rows,
        )
        kept_list.append(kept)
    stacked = tuple(
        (jnp.concatenate([item[number] for item in kept_list], axis=0) for number in range(13))
    )
    grad_sums = reduce_weight_grads(stacked)
    wide, down, small, bias = grad_sums
    output = jnp.stack(outputs, axis=0)[:, None]
    grad_inputs = jnp.stack(input_grads, axis=0)[:, None]
    hidden = w_gate.shape[1]
    grad_query = wide[:, 0:width]
    grad_key = wide[:, width : 2 * width]
    grad_value = wide[:, 2 * width : 3 * width]
    grad_outgate = wide[:, 3 * width : 4 * width]
    grad_outw = wide[:, 4 * width : 5 * width]
    grad_gatew = wide[:, 5 * width : 5 * width + hidden]
    grad_upw = wide[:, 5 * width + hidden : 5 * width + 2 * hidden]
    grad_forgetw = small[:, 0:heads]
    grad_gain_one = small[:, heads]
    grad_gain_two = small[:, heads + 1]
    return (
        output,
        grad_inputs,
        grad_gain_one,
        grad_query,
        grad_key,
        grad_value,
        grad_outgate,
        grad_outw,
        grad_forgetw,
        bias,
        grad_gain_two,
        grad_gatew,
        grad_upw,
        down,
    )


def solution(mesh):
    return jax.shard_map(
        per_device,
        mesh=mesh,
        in_specs=(
            P(None, "fsdp", "ctx", None),
            P(None, "fsdp", "ctx", None),
            P(None, "fsdp", None),
            P(),
            P(("ctx", "fsdp")),
            P(("ctx", "fsdp"), None),
            P(("ctx", "fsdp"), None),
            P(("ctx", "fsdp"), None),
            P(("ctx", "fsdp"), None),
            P(("ctx", "fsdp"), None),
            P(("ctx", "fsdp"), None),
            P(),
            P(("ctx", "fsdp")),
            P(("ctx", "fsdp"), None),
            P(("ctx", "fsdp"), None),
            P(("ctx", "fsdp"), None),
        ),
        out_specs=(
            P(None, "fsdp", "ctx", None),
            P(None, "fsdp", "ctx", None),
            P(("ctx", "fsdp")),
            P(("ctx", "fsdp"), None),
            P(("ctx", "fsdp"), None),
            P(("ctx", "fsdp"), None),
            P(("ctx", "fsdp"), None),
            P(("ctx", "fsdp"), None),
            P(("ctx", "fsdp"), None),
            P(),
            P(("ctx", "fsdp")),
            P(("ctx", "fsdp"), None),
            P(("ctx", "fsdp"), None),
            P(("ctx", "fsdp"), None),
        ),
        check_vma=False,
    )
```

profile of v0, /device:TPU:0, one launch (start us, length us, event | category | flops | bytes accessed | tf_op | source)
XLA Modules:
  0.0 2435.7 jit_solution(1897634911836689856)
XLA Ops:
  11.2 42.2 %all-reduce.2 = (bf16[1536]{0:T(1024)(128)(2,1)S(1)}, bf16[1536]{0:T(1024)(128)(2,1)S(1)}) all-reduce(bf16[1536]{0:T(1024)(128)(2,1)S(1)} %dynamic-update-slice, bf16[1536]{0:T(1024)(128)(2,1)S(1)} %dynamic-update-slice.1), channel_id=1, replica_groups=mesh['ctx'=8,'fsdp'=4] {'ctx','fsdp'}, use_global_device_ids=true, to_apply=%add | all-reduce | flops 3072 | bytes 12288
  56.6 20.7 all-gather.18.cloned.1.call-done
  81.2 61.3 %all-gather.14.cloned.1.call-done = bf16[1536,1536]{1,0:T(8,128)(2,1)} async-done(((bf16[48,1536]{1,0:T(8,128)(2,1)}), bf16[1536,1536]{1,0:T(8,128)(2,1)}) %all-gather.14.cloned.1.call-update) | async-done | bytes 4718608 | tf_op jit(solution)/shard_map/all_gather | solution.py:268
  191.1 68.5 %all-gather = bf16[32,48,24]{1,2,0:T(8,128)(2,1)S(1)} all-gather(bf16[1,48,24]{1,2,0:T(8,128)(2,1)S(1)} %bitcast.784), channel_id=1, replica_groups=mesh['ctx'=8,'fsdp'=4] {'ctx','fsdp'}, dimensions={0}, use_global_device_ids=true | all-gather | bytes 76032 | tf_op jit(solution)/shard_map/all_gather | solution.py:271
  261.6 13.1 all_gather.41
  283.9 12.9 all_gather.50
  337.4 28.8 %all-gather.34.cloned.1.call-done = bf16[1024,1536]{1,0:T(8,128)(2,1)} async-done(((bf16[128,1536]{1,0:T(8,128)(2,1)}), bf16[1024,1536]{1,0:T(8,128)(2,1)}) %all-gather.34.cloned.1.call-update) | async-done | bytes 3145744 | tf_op jit(solution)/shard_map/all_gather | solution.py:281
  511.0 83.3 %all-gather.30.cloned.1.call-done = bf16[1536,4096]{1,0:T(8,128)(2,1)} async-done(((bf16[48,4096]{1,0:T(8,128)(2,1)}), bf16[1536,4096]{1,0:T(8,128)(2,1)}) %all-gather.30.cloned.1.call-update) | async-done | bytes 12582928 | tf_op jit(solution)/shard_map/all_gather | solution.py:274
  600.8 90.8 %all-gather.28.cloned.1.call-done = bf16[1536,4096]{1,0:T(8,128)(2,1)} async-done(((bf16[48,4096]{1,0:T(8,128)(2,1)}), bf16[1536,4096]{1,0:T(8,128)(2,1)}) %all-gather.28.cloned.1.call-update) | async-done | bytes 12582928 | tf_op jit(solution)/shard_map/all_gather | solution.py:273
  699.4 89.2 %all-gather.32.cloned.1.call-done = bf16[4096,1536]{1,0:T(8,128)(2,1)} async-done(((bf16[128,1536]{1,0:T(8,128)(2,1)}), bf16[4096,1536]{1,0:T(8,128)(2,1)}) %all-gather.32.cloned.1.call-update) | async-done | bytes 12582928 | tf_op jit(solution)/shard_map/all_gather | solution.py:275
  788.6 10.8 multiply_convert_fusion.2
  799.4 10.3 fusion.322
  809.7 11.4 multiply_reduce_fusion.1
  831.0 9.9 multiply_convert_fusion
  840.9 10.0 fusion.324
  892.5 15.1 while.170
  912.1 13.6 while.171
  950.6 15.2 while.168
  970.2 14.0 while.169
  1019.4 9.8 reshape.1314
  1049.0 9.8 reshape.1311
  1069.2 9.8 reshape.1312
  1114.6 20.0 fusion.204
  1143.0 37.1 %reduce-scatter.22.cloned.1.call-done = bf16[128,1536]{1,0:T(8,128)(2,1)} async-done(((bf16[1024,1536]{1,0:T(8,128)(2,1)}), bf16[128,1536]{1,0:T(8,128)(2,1)}) %reduce-scatter.22.cloned.1.call-update) | async-done | bytes 393232 | tf_op jit(solution)/shard_map/reduce_scatter | solution.py:398
  1188.8 32.9 %reduce-scatter.16.cloned.1.call-done = bf16[128,1536]{1,0:T(8,128)(2,1)} async-done(((bf16[1024,1536]{1,0:T(8,128)(2,1)}), bf16[128,1536]{1,0:T(8,128)(2,1)}) %reduce-scatter.16.cloned.1.call-update) | async-done | bytes 393232 | tf_op jit(solution)/shard_map/reduce_scatter | solution.py:395
  1226.0 37.3 %reduce-scatter.18.cloned.1.call-done = bf16[128,1536]{1,0:T(8,128)(2,1)} async-done(((bf16[1024,1536]{1,0:T(8,128)(2,1)}), bf16[128,1536]{1,0:T(8,128)(2,1)}) %reduce-scatter.18.cloned.1.call-update) | async-done | bytes 393232 | tf_op jit(solution)/shard_map/reduce_scatter | solution.py:398
  1275.3 20.2 fusion.212
  1295.5 63.8 %pad_maximum_fusion = f32[1536,15872]{1,0:T(8,128)} fusion(f32[1536,8192]{1,0:T(8,128)} %fusion.204, f32[1536,1536]{1,0:T(8,128)} %fusion.266, f32[1536,6144]{1,0:T(8,128)} %fusion.212), kind=kLoop, calls=%fused_computation.244 | loop fusion | flops 48758784 | bytes 195035136 | tf_op jit(solution)/shard_map/concatenate | solution.py:206
  1360.8 11.5 fusion.238
  1389.9 38.2 %psum.7 = f32[24]{0:T(128)} all-reduce(f32[24]{0:T(128)S(1)} %reduce_sum.375), channel_id=1, replica_groups=mesh['ctx'=8,'fsdp'=4] {'ctx','fsdp'}, use_global_device_ids=true, to_apply=%region_78.85 | all-reduce | flops 24 | bytes 192 | tf_op jit(solution)/shard_map/psum | solution.py:230
  1436.0 740.0 %reduce-scatter.24.cloned.1.call-done = f32[48,15872]{1,0:T(8,128)} async-done(((f32[1536,15872]{1,0:T(8,128)}), f32[48,15872]{1,0:T(8,128)}) %reduce-scatter.24.cloned.1.call-update) | async-done | bytes 3047440 | tf_op jit(solution)/shard_map/reduce_scatter | solution.py:205
  2181.1 247.6 %reduce-scatter.26.cloned.1.call-done = f32[128,1536]{1,0:T(8,128)} async-done(((f32[4096,1536]{1,0:T(8,128)}), f32[128,1536]{1,0:T(8,128)}) %reduce-scatter.26.cloned.1.call-update) | async-done | bytes 786448 | tf_op jit(solution)/shard_map/reduce_scatter | solution.py:218
  (863 shorter events, 579.9 us)
Async XLA Ops:
  7.2 70.1 %all-gather.18.cloned.1.call-start = ((), (), s32[]{:S(2)}) async-start(), calls=%async_computation.11 | async-start | bytes 4866048 | tf_op jit(solution)/shard_map/all_gather | solution.py:267
  7.9 134.6 %all-gather.14.cloned.1.call-start = ((), (), s32[]{:S(2)}) async-start(), calls=%async_computation.9 | async-start | bytes 4866048 | tf_op jit(solution)/shard_map/all_gather | solution.py:268
  8.7 302.4 %all-gather.22.cloned.1.call-start = ((), (), s32[]{:S(2)}) async-start(), calls=%async_computation.13 | async-start | bytes 4866048 | tf_op jit(solution)/shard_map/all_gather | solution.py:266
  9.4 316.6 %all-gather.20.cloned.1.call-start = ((), (), s32[]{:S(2)}) async-start(), calls=%async_computation.12 | async-start | bytes 3538944 | tf_op jit(solution)/shard_map/all_gather | solution.py:280
  56.6 254.4 %copy-start.39 = (bf16[128,1536]{1,0:T(8,128)(2,1)}, bf16[128,1536]{1,0:T(8,128)(2,1)S(1)}, u32[]{:S(2)}) copy-start(bf16[128,1536]{1,0:T(8,128)(2,1)S(1)} %get-tuple-element.2395) | copy-start | bytes 1179652
  56.6 261.9 %copy-start.42 = (bf16[128,1536]{1,0:T(8,128)(2,1)}, bf16[128,1536]{1,0:T(8,128)(2,1)S(1)}, u32[]{:S(2)}) copy-start(bf16[128,1536]{1,0:T(8,128)(2,1)S(1)} %get-tuple-element.2396) | copy-start | bytes 1179652
  81.2 249.2 %all-gather.16.cloned.1.call-start = ((), (), s32[]{:S(2)}) async-start(), calls=%async_computation.10 | async-start | bytes 3538944 | tf_op jit(solution)/shard_map/all_gather | solution.py:281
  146.5 188.1 %all-gather.36.cloned.1.call-start = ((), (), s32[]{:S(2)}) async-start(), calls=%async_computation.20 | async-start | bytes 3538944 | tf_op jit(solution)/shard_map/all_gather | solution.py:280
  150.4 215.8 %all-gather.34.cloned.1.call-start = ((), (), s32[]{:S(2)}) async-start(), calls=%async_computation.19 | async-start | bytes 3538944 | tf_op jit(solution)/shard_map/all_gather | solution.py:281
  154.4 105.5 %copy-start.167 = (f32[24]{0:T(128)S(1)}, f32[24]{0:T(128)}, u32[]{:S(2)}) copy-start(f32[24]{0:T(128)} %param.63) | copy-start | bytes 292
  154.5 340.8 %all-gather.24.cloned.1.call-start = ((), (), s32[]{:S(2)}) async-start(), calls=%async_computation.14 | async-start | bytes 4866048 | tf_op jit(solution)/shard_map/all_gather | solution.py:269
  155.2 344.9 %all-gather.26.cloned.1.call-start = ((), (), s32[]{:S(2)}) async-start(), calls=%async_computation.15 | async-start | bytes 4866048 | tf_op jit(solution)/shard_map/all_gather | solution.py:270
  155.9 438.4 %all-gather.30.cloned.1.call-start = ((), (), s32[]{:S(2)}) async-start(), calls=%async_computation.17 | async-start | bytes 12976128 | tf_op jit(solution)/shard_map/all_gather | solution.py:274
  156.5 535.0 %all-gather.28.cloned.1.call-start = ((), (), s32[]{:S(2)}) async-start(), calls=%async_computation.16 | async-start | bytes 12976128 | tf_op jit(solution)/shard_map/all_gather | solution.py:273
  157.3 631.3 %all-gather.32.cloned.1.call-start = ((), (), s32[]{:S(2)}) async-start(), calls=%async_computation.18 | async-start | bytes 12976128 | tf_op jit(solution)/shard_map/all_gather | solution.py:275
  157.8 976.7 %reduce-scatter.30.cloned.1.call-start = ((), (), s32[]{:S(2)}) async-start(), calls=%async_computation.28 | async-start | bytes 294912
  504.5 356.2 %copy-start.154 = (f32[128]{0:T(128)}, f32[128]{0:T(128)S(1)}, u32[]{:S(2)}) copy-start(f32[128]{0:T(128)S(1)} %add_rsqrt_fusion) | copy-start | bytes 1540
  510.0 350.7 %copy-start.156 = (f32[128]{0:T(128)}, f32[128]{0:T(128)S(1)}, u32[]{:S(2)}) copy-start(f32[128]{0:T(128)S(1)} %add_rsqrt_fusion.2) | copy-start | bytes 1540
  511.0 180.5 %copy-start.46 = (bf16[128,1536]{1,0:T(8,128)(2,1)}, bf16[128,1536]{1,0:T(8,128)(2,1)S(1)}, u32[]{:S(2)}) copy-start(bf16[128,1536]{1,0:T(8,128)(2,1)S(1)} %multiply_convert_fusion.12) | copy-start | bytes 1179652
  600.8 187.8 %copy-start.53 = (bf16[2,1,128,1536]{3,2,1,0:T(8,128)(2,1)S(1)}, bf16[2,1,128,1536]{3,2,1,0:T(8,128)(2,1)}, u32[]{:S(2)}) copy-start(bf16[2,1,128,1536]{3,2,1,0:T(8,128)(2,1)} %param.53) | copy-start | bytes 2359300
  941.4 194.0 %reduce-scatter.28.cloned.1.call-start = ((), (), s32[]{:S(2)}) async-start(), calls=%async_computation.27 | async-start | bytes 294912
  1042.1 96.5 %reduce-scatter.20.cloned.1.call-start = ((), (), s32[]{:S(2)}) async-start(), calls=%async_computation.23 | async-start | bytes 3538944 | tf_op jit(solution)/shard_map/reduce_scatter | solution.py:395
  1048.4 131.7 %reduce-scatter.22.cloned.1.call-start = ((), (), s32[]{:S(2)}) async-start(), calls=%async_computation.24 | async-start | bytes 3538944 | tf_op jit(solution)/shard_map/reduce_scatter | solution.py:398
  1048.9 172.8 %reduce-scatter.16.cloned.1.call-start = ((), (), s32[]{:S(2)}) async-start(), calls=%async_computation.21 | async-start | bytes 3538944 | tf_op jit(solution)/shard_map/reduce_scatter | solution.py:395
  1097.3 166.0 %reduce-scatter.18.cloned.1.call-start = ((), (), s32[]{:S(2)}) async-start(), calls=%async_computation.22 | async-start | bytes 3538944 | tf_op jit(solution)/shard_map/reduce_scatter | solution.py:398
  1100.8 331.7 %reduce-scatter.32.cloned.1.call-start = ((), (), s32[]{:S(2)}) async-start(), calls=%async_computation.29 | async-start | bytes 811008
  1188.8 82.8 %copy-start.84 = (f32[128,1536]{1,0:T(8,128)}, f32[128,1536]{1,0:T(8,128)S(1)}, u32[]{:S(2)}) copy-start(f32[128,1536]{1,0:T(8,128)S(1)} %convolution_add_fusion) | copy-start | bytes 2359300
  1275.2 900.8 %reduce-scatter.24.cloned.1.call-start = ((), (), s32[]{:S(2)}) async-start(), calls=%async_computation.25 | async-start | bytes 100564992 | tf_op jit(solution)/shard_map/reduce_scatter | solution.py:205
  1359.3 1069.3 %reduce-scatter.26.cloned.1.call-start = ((), (), s32[]{:S(2)}) async-start(), calls=%async_computation.26 | async-start | bytes 25952256 | tf_op jit(solution)/shard_map/reduce_scatter | solution.py:218
  1380.0 48.1 %copy-start.130 = (f32[1536]{0:T(1024)S(1)}, f32[1536]{0:T(1024)}, u32[]{:S(2)}) copy-start(f32[1536]{0:T(1024)} %convert_element_type.256) | copy-start | bytes 18436
  1380.0 48.1 %copy-start.155 = (f32[128]{0:T(128)S(1)}, f32[128]{0:T(128)}, u32[]{:S(2)}) copy-start(f32[128]{0:T(128)} %copy-done.154) | copy-start | bytes 1540
  1380.0 48.1 %copy-start.164 = (f32[128]{0:T(128)S(1)}, f32[128]{0:T(128)}, u32[]{:S(2)}) copy-start(f32[128]{0:T(128)} %copy-done.162) | copy-start | bytes 1540
  (192 other events, 1474.2 us)
Sparse Core Ops, SparseCore 0:
  10.9 66.3 all-gather.17
  80.2 62.3 all-gather.13
  145.5 62.8 all-gather.21
  210.4 37.7 all-gather.19
  249.7 37.5 all-gather.15
  289.4 37.3 all-gather.35
  329.0 37.1 all-gather.33
  369.1 62.3 all-gather.23
  434.4 62.3 all-gather.25
  499.6 94.7 all-gather.29
  597.3 94.2 all-gather.27
  694.3 94.2 all-gather.31
  941.5 42.0 reduce-scatter.29
  1042.2 55.5 reduce-scatter.27
  1100.0 38.4 reduce-scatter.19
  1140.6 39.4 reduce-scatter.21
  1182.2 39.4 reduce-scatter.15
  1223.8 39.4 reduce-scatter.17
  1275.3 94.5 reduce-scatter.31
  1376.2 799.7 reduce-scatter.23
  2184.2 244.4 reduce-scatter.25
where the time goes:
time: 2450 us; the launch traced here: 2440 us
  waiting for transfers between devices  1480 us (60%)
  local copies, waits for them, and re-layouts  289 us (12%)
  matrix products  289 us (12%)
  blocking collectives  175 us (7%)
  other arithmetic  159 us (6%)
  between operations  45.4 us (2%)
    reduce_scatter x1, waiting for transfers between devices, reduce_weight_grads(): lax.psum_scatter(jnp.concatenate([product_left(normed, attn_right), produ...  740 us
    reduce_scatter x1, waiting for transfers between devices, reduce_weight_grads(): lax.psum_scatter(product_left(activ, upstream), ('ctx', 'fsdp'), scatter_...  248 us
    dot_general x16, matrix products, product_right(): lax.dot_general(left, right, (((1,), (1,)), ((), ())), preferred_element_...  99.3 us
    all_gather x1, waiting for transfers between devices, fetch_weights(): lax.all_gather(w_gate, ('ctx', 'fsdp'), axis=0, tiled=True)  90.8 us
    all_gather x1, waiting for transfers between devices, fetch_weights(): lax.all_gather(w_down, ('ctx', 'fsdp'), axis=0, tiled=True)  89.2 us
    all_gather x1, waiting for transfers between devices, fetch_weights(): lax.all_gather(w_up, ('ctx', 'fsdp'), axis=0, tiled=True)  83.3 us
    dot_general x16, matrix products, product(): return jnp.dot(left, right, preferred_element_type=jnp.float32)  75.6 us
    reduce_scatter x2, waiting for transfers between devices, per_device(): lax.psum_scatter(slot_values.astype(jnp.bfloat16), 'ctx', scatter_dimensi...  74.4 us
  transfers between devices with their start and end apart: 21, of which 11 were waited for; matrix products, arithmetic and copies ran while one was open for 23% of the time, Pallas kernels for 0%

commit v1 on v0

v1 whole, which is shorter than its diff:
```python
import functools

import jax
import jax.numpy as jnp
from jax import lax
from jax.experimental import pallas as pl
from jax.experimental.pallas import tpu as pltpu
from jax.sharding import Mesh, PartitionSpec as P

EPS = 1e-06
LOW = -1e30
BQ = 256
F32 = jnp.float32
BF16 = jnp.bfloat16
VMEM_LIMIT = 56 * 1024 * 1024


def dot(left, right, contract=((1,), (0,)), out=F32):
    return lax.dot_general(left, right, (contract, ((), ())), preferred_element_type=out)


def xor_permute(x, axis, step):
    n = lax.axis_size(axis)
    return lax.ppermute(x, axis, [(i, i ^ step) for i in range(n)])


def pick(stacked, index):
    return lax.dynamic_index_in_dim(stacked, index, 0, keepdims=False)


def rows_to_group(x):
    np_, nz = lax.axis_size("p"), lax.axis_size("z")
    p, z = lax.axis_index("p"), lax.axis_index("z")
    micro, tokens, width = x.shape
    rp = tokens // np_
    parts = x.reshape(micro, np_, rp, width).transpose(1, 0, 2, 3)
    got = [pick(parts, p)]
    for k in range(1, np_):
        got.append(xor_permute(pick(parts, p ^ k), "p", k))
    got = jnp.stack(got).reshape(np_ * micro, rp, width)

    def for_layer(target):
        m, ps = target // np_, target % np_
        return pick(got, (p ^ ps) * micro + m)

    rows = [for_layer(z)]
    for k in range(1, nz):
        rows.append(xor_permute(for_layer(z ^ k), "z", k))
    return jnp.concatenate(rows, axis=0)


def rows_from_group(y, micro):
    np_, nz = lax.axis_size("p"), lax.axis_size("z")
    p, z = lax.axis_index("p"), lax.axis_index("z")
    width = y.shape[1]
    rp = y.shape[0] // nz
    parts = y.reshape(nz, rp, width)
    got = [parts[0]]
    for k in range(1, nz):
        got.append(xor_permute(parts[k], "z", k))
    got = jnp.stack(got)

    def for_place(target):
        return jnp.stack([pick(got, z ^ (m * np_ + target)) for m in range(micro)])

    back = [for_place(p)]
    for k in range(1, np_):
        back.append(xor_permute(for_place(p ^ k), "p", k))
    back = jnp.stack(back)
    return jnp.stack([pick(back, p ^ c) for c in range(np_)], axis=1).reshape(micro, np_ * rp, width)


def gather_heads(x):
    np_ = lax.axis_size("p")
    own = [x] + [xor_permute(x, "p", k) for k in range(1, np_)]
    other = [xor_permute(block, "core", 1) for block in own]
    return jnp.concatenate(own + other, axis=0)


def scatter_heads(partial):
    np_ = lax.axis_size("p")
    rows = partial.shape[0] // 2
    low = partial.astype(BF16)
    got = xor_permute(low[rows:], "core", 1)
    total = partial[:rows] + got.astype(F32)
    total = total.reshape(np_, rows // np_, -1)
    out = total[0]
    for k in range(1, np_):
        out = out + xor_permute(total[k].astype(BF16), "p", k).astype(F32)
    return out


def gather_plane(x):
    np_ = lax.axis_size("p")
    half = x.shape[0] // 2
    over_q = xor_permute(x, "q", 1)
    if np_ == 2:
        over_p = xor_permute(x, "p", 1)
        diagonal = [xor_permute(over_q[:half], "p", 1), xor_permute(over_p[half:], "q", 1)]
        own = [x, over_q, over_p, jnp.concatenate(diagonal, axis=0)]
    else:
        own = [x, over_q]
        for k in range(1, np_):
            own += [xor_permute(x, "p", k), xor_permute(over_q, "p", k)]
    other = [xor_permute(block, "core", 1) for block in own]
    return jnp.concatenate(own + other, axis=0)


def scatter_plane(partial):
    np_ = lax.axis_size("p")
    rows = partial.shape[0] // 2
    low = partial.astype(BF16)
    got = xor_permute(low[rows:], "core", 1)
    total = partial[:rows] + got.astype(F32)
    total = total.reshape(np_, 2, rows // np_ // 2, -1)
    if np_ == 2:
        half = total.shape[2] // 2
        diagonal = total[1, 1].astype(BF16)
        into_q = xor_permute(diagonal[:half], "p", 1)
        into_p = xor_permute(diagonal[half:], "q", 1)
        to_q = jnp.concatenate([total[0, 1, :half] + into_q.astype(F32), total[0, 1, half:]], axis=0)
        to_p = jnp.concatenate([total[1, 0, :half], total[1, 0, half:] + into_p.astype(F32)], axis=0)
        over_q = xor_permute(to_q.astype(BF16), "q", 1)
        over_p = xor_permute(to_p.astype(BF16), "p", 1)
        return total[0, 0] + over_q.astype(F32) + over_p.astype(F32)
    pair = total[0]
    for k in range(1, np_):
        pair = pair + xor_permute(total[k].astype(BF16), "p", k).astype(F32)
    return pair[0] + xor_permute(pair[1].astype(BF16), "q", 1).astype(F32)


def lanes_of(rows, width, head, depth):
    lane = lax.broadcasted_iota(jnp.int32, (rows, width), 1)
    return (lane >= head * depth) & (lane < (head + 1) * depth)


def log_sigmoid(z):
    return jnp.minimum(z, 0.0) - jnp.log(1.0 + jnp.exp(-jnp.abs(z)))


def to_natural(table, source, target, chunk):
    for n in range(target.shape[0] // chunk):
        place = pl.multiple_of(table[n] * chunk, chunk)
        target[pl.ds(n * chunk, chunk), :] = source[pl.ds(place, chunk), :].astype(target.dtype)


def from_natural(table, source, target, chunk):
    for n in range(source.shape[0] // chunk):
        place = pl.multiple_of(table[n] * chunk, chunk)
        target[pl.ds(place, chunk), :] = source[pl.ds(n * chunk, chunk), :].astype(target.dtype)


def attend_kernel(
    chunk, depth, table, q_ref, k_ref, v_ref, g_ref, z_ref, bias_ref, begin_ref,
    a_ref, b_ref, total_ref, cumul_ref,
    qn, kn, vn, an, cumul_rows,
):
    group = pl.program_id(0)
    total, width = q_ref.shape
    per_group = width // depth
    bq = min(BQ, total)
    window = total // 2

    @pl.when(group == 0)
    def _():
        logs = an
        lower = (
            lax.broadcasted_iota(jnp.int32, (bq, bq), 0) >= lax.broadcasted_iota(jnp.int32, (bq, bq), 1)
        ).astype(F32).astype(BF16)
        for n in range(total // chunk):
            place = pl.multiple_of(table[n] * chunk, chunk)
            logs[pl.ds(n * chunk, chunk), 0:128] = log_sigmoid(z_ref[pl.ds(place, chunk), :] + bias_ref[...])
        carry = jnp.zeros((1, 128), F32)
        for i in range(total // bq):
            part = dot(lower, logs[i * bq:(i + 1) * bq, 0:128].astype(BF16)) + carry
            cumul_ref[i * bq:(i + 1) * bq, :] = part
            carry = part[bq - 1:bq, :]
        cumul_rows[...] = jnp.transpose(cumul_ref[...])
        total_ref[...] = jnp.zeros_like(total_ref)

    to_natural(table, q_ref, qn, chunk)
    to_natural(table, k_ref, kn, chunk)
    to_natural(table, v_ref, vn, chunk)
    lane = lax.broadcasted_iota(jnp.int32, (bq, 128), 1)
    for i in range(total // bq):
        first = max(0, i * bq - window)
        span = (i + 1) * bq - first
        place = i * bq + lax.broadcasted_iota(jnp.int32, (bq, span), 0)
        other = first + lax.broadcasted_iota(jnp.int32, (bq, span), 1)
        begin = begin_ref[i * bq:(i + 1) * bq, :]
        bias = jnp.where((other <= place) & (other >= begin), 0.0, LOW)
        q_tile = qn[i * bq:(i + 1) * bq, :] * jnp.asarray(depth ** -0.5, BF16)
        keys = kn[first:first + span, :]
        values = jnp.concatenate([vn[first:first + span, :], jnp.ones((span, width), BF16)], axis=1)
        out = jnp.zeros((bq, width), F32)
        totals = total_ref[i * bq:(i + 1) * bq, :]
        for h in range(per_group):
            head = group * per_group + h
            mine = lanes_of(bq, width, h, depth)
            score = dot(jnp.where(mine, q_tile, jnp.zeros_like(q_tile)), keys, ((1,), (1,)))
            score = score - cumul_rows[pl.ds(head, 1), first:first + span] + bias
            peak = jnp.max(score, axis=1, keepdims=True)
            weight = jnp.exp(score - peak)
            both = dot(weight.astype(BF16), values)
            weight_sum = both[:, width:]
            out = jnp.where(mine, both[:, :width] / weight_sum, out)
            totals = jnp.where(lane == head, peak + jnp.log(weight_sum[:, 0:128]), totals)
        an[i * bq:(i + 1) * bq, 0:width] = out
        total_ref[i * bq:(i + 1) * bq, :] = totals
    for n in range(total // chunk):
        place = pl.multiple_of(table[n] * chunk, chunk)
        part = an[pl.ds(n * chunk, chunk), 0:width]
        a_ref[pl.ds(place, chunk), :] = part
        b_ref[pl.ds(place, chunk), :] = (part * jax.nn.sigmoid(g_ref[pl.ds(place, chunk), :])).astype(BF16)


def attend_back_kernel(
    chunk, depth, heads, table, q_ref, k_ref, v_ref, g_ref, a_ref, db_ref, total_ref, cumul_ref, z_ref,
    bias_ref, begin_ref,
    dq_ref, dk_ref, dv_ref, dg_ref, dz_ref, dbias_ref,
    qn, kn, vn, dan, delta, rows, total_rows, dqn, dkn, dvn, dcumul,
):
    group = pl.program_id(0)
    total, width = q_ref.shape
    per_group = width // depth
    bq = min(BQ, total)
    window = total // 2
    lane = lax.broadcasted_iota(jnp.int32, (bq, 128), 1)

    @pl.when(group == 0)
    def _():
        total_rows[...] = jnp.transpose(total_ref[...])
        dcumul[...] = jnp.zeros_like(dcumul)

    to_natural(table, q_ref, qn, chunk)
    to_natural(table, k_ref, kn, chunk)
    to_natural(table, v_ref, vn, chunk)
    small = lax.broadcasted_iota(jnp.int32, (chunk, 128), 1)
    for n in range(total // chunk):
        place = pl.multiple_of(table[n] * chunk, chunk)
        opened = jax.nn.sigmoid(g_ref[pl.ds(place, chunk), :])
        attended = a_ref[pl.ds(place, chunk), :]
        grad = db_ref[pl.ds(place, chunk), :]
        below = (grad * opened).astype(BF16)
        dan[pl.ds(n * chunk, chunk), :] = below
        dg_ref[pl.ds(place, chunk), :] = (grad * attended * opened * (1.0 - opened)).astype(BF16)
        both = below.astype(F32) * attended
        sums = jnp.zeros((chunk, 128), F32)
        for h in range(per_group):
            own = jnp.where(lanes_of(chunk, width, h, depth), both, 0.0)
            sums = jnp.where(small == h, jnp.sum(own, axis=1, keepdims=True), sums)
        delta[pl.ds(n * chunk, chunk), :] = sums
    rows[...] = jnp.transpose(delta[...])
    dkn[...] = jnp.zeros_like(dkn)
    dvn[...] = jnp.zeros_like(dvn)
    for i in range(total // bq):
        first = max(0, i * bq - window)
        span = (i + 1) * bq - first
        window_rows = pl.ds(first, span)
        place = i * bq + lax.broadcasted_iota(jnp.int32, (span, bq), 1)
        other = first + lax.broadcasted_iota(jnp.int32, (span, bq), 0)
        begin = begin_ref[:, i * bq:(i + 1) * bq]
        bias = jnp.where((other <= place) & (other >= begin), 0.0, LOW)
        q_tile = qn[i * bq:(i + 1) * bq, :] * jnp.asarray(depth ** -0.5, BF16)
        a_tile = dan[i * bq:(i + 1) * bq, :]
        keys = kn[window_rows, :]
        values = vn[window_rows, :]
        cumul = cumul_ref[window_rows, :]
        wide_lane = lax.broadcasted_iota(jnp.int32, (span, 128), 1)
        query_grad = jnp.zeros((bq, width + 128), F32)
        for h in range(per_group):
            head = group * per_group + h
            mine = lanes_of(bq, width, h, depth)
            q_mine = jnp.where(mine, q_tile, jnp.zeros_like(q_tile))
            a_mine = jnp.where(mine, a_tile, jnp.zeros_like(a_tile))
            column = jnp.sum(jnp.where(wide_lane == head, cumul, 0.0), axis=1, keepdims=True)
            score = dot(keys, q_mine, ((1,), (1,)))
            score = score - total_rows[pl.ds(head, 1), i * bq:(i + 1) * bq] - column + bias
            weight = jnp.exp(score)
            weight_grad = dot(values, a_mine, ((1,), (1,)))
            score_grad = (weight * (weight_grad - rows[h:h + 1, i * bq:(i + 1) * bq])).astype(BF16)
            mark = ((lane == head) | (lane == head + heads)).astype(F32).astype(BF16)
            mark_keys = ((wide_lane == head) | (wide_lane == head + heads)).astype(F32).astype(BF16)
            key_part = dot(score_grad, jnp.concatenate([q_mine, mark], axis=1))
            dvn[window_rows, :] += dot(weight.astype(BF16), a_mine)
            dkn[window_rows, :] += key_part[:, :width]
            dcumul[window_rows, :] -= key_part[:, width:]
            k_mine = jnp.where(lanes_of(span, width, h, depth), keys, jnp.zeros_like(keys))
            query_grad += dot(score_grad, jnp.concatenate([k_mine, mark_keys], axis=1), ((0,), (0,)))
        dqn[i * bq:(i + 1) * bq, :] = query_grad[:, :width] * depth ** -0.5
        dcumul[i * bq:(i + 1) * bq, :] += query_grad[:, width:]
    from_natural(table, dqn, dq_ref, chunk)
    from_natural(table, dkn, dk_ref, chunk)
    from_natural(table, dvn, dv_ref, chunk)

    @pl.when(group == pl.num_programs(0) - 1)
    def _():
        upper = (
            lax.broadcasted_iota(jnp.int32, (bq, bq), 0) <= lax.broadcasted_iota(jnp.int32, (bq, bq), 1)
        ).astype(F32)
        carry = jnp.zeros((1, 128), F32)
        for i in reversed(range(total // bq)):
            part = (
                jnp.dot(
                    upper, dcumul[i * bq:(i + 1) * bq, :], precision=lax.Precision.HIGHEST,
                    preferred_element_type=F32,
                )
                + carry
            )
            delta[i * bq:(i + 1) * bq, :] = part
            carry = part[0:1, :]
        sums = jnp.zeros((1, 128), F32)
        for n in range(total // chunk):
            place = pl.multiple_of(table[n] * chunk, chunk)
            logit = z_ref[pl.ds(place, chunk), :] + bias_ref[...]
            grad = delta[pl.ds(n * chunk, chunk), :] * jax.nn.sigmoid(-logit)
            sums = sums + jnp.sum(grad, axis=0, keepdims=True)
            high = grad.astype(BF16)
            rest = grad - high.astype(F32)
            dz_ref[pl.ds(place, chunk), :] = jnp.where(
                small < heads, high.astype(F32), jnp.where(small < 2 * heads, rest, 0.0)
            ).astype(BF16)
        dbias_ref[...] = jnp.broadcast_to(sums, dbias_ref.shape)


def group_width(columns):
    return 128 if columns % 128 == 0 else columns


def attend(table, qkv, gate, logit, bias, begin, chunk, depth):
    total = qkv[0].shape[0]
    columns = qkv[0].shape[1]
    width = group_width(columns)
    block = pl.BlockSpec((total, width), lambda g, t: (0, g))
    whole = pl.BlockSpec((total, 128), lambda g, t: (0, 0))
    wide = max(width, 128)
    return pl.pallas_call(
        functools.partial(attend_kernel, chunk, depth),
        grid_spec=pltpu.PrefetchScalarGridSpec(
            num_scalar_prefetch=1,
            grid=(columns // width,),
            in_specs=[
                block, block, block, block, whole,
                pl.BlockSpec((1, 128), lambda g, t: (0, 0)),
                pl.BlockSpec((total, 1), lambda g, t: (0, 0)),
            ],
            out_specs=[block, block, whole, whole],
            scratch_shapes=[
                pltpu.VMEM((total, width), BF16),
                pltpu.VMEM((total, width), BF16),
                pltpu.VMEM((total, width), BF16),
                pltpu.VMEM((total, wide), F32),
                pltpu.VMEM((128, total), F32),
            ],
        ),
        out_shape=[
            jax.ShapeDtypeStruct((total, columns), F32),
            jax.ShapeDtypeStruct((total, columns), BF16),
            jax.ShapeDtypeStruct((total, 128), F32),
            jax.ShapeDtypeStruct((total, 128), F32),
        ],
        compiler_params=pltpu.CompilerParams(vmem_limit_bytes=VMEM_LIMIT),
        name="attend",
    )(table, *qkv, gate, logit, bias, begin[:, None])


def attend_back(table, qkv, gate, attended, grad, totals, cumul, logit, bias, begin, chunk, depth):
    total = qkv[0].shape[0]
    columns = qkv[0].shape[1]
    width = group_width(columns)
    block = pl.BlockSpec((total, width), lambda g, t: (0, g))
    whole = pl.BlockSpec((total, 128), lambda g, t: (0, 0))
    low = jax.ShapeDtypeStruct((total, columns), BF16)
    return pl.pallas_call(
        functools.partial(attend_back_kernel, chunk, depth, columns // depth),
        grid_spec=pltpu.PrefetchScalarGridSpec(
            num_scalar_prefetch=1,
            grid=(columns // width,),
            in_specs=[
                block, block, block, block, block, block, whole, whole, whole,
                pl.BlockSpec((1, 128), lambda g, t: (0, 0)),
                pl.BlockSpec((1, total), lambda g, t: (0, 0)),
            ],
            out_specs=[block, block, block, block, whole, pl.BlockSpec((8, 128), lambda g, t: (0, 0))],
            scratch_shapes=[
                pltpu.VMEM((total, width), BF16),
                pltpu.VMEM((total, width), BF16),
                pltpu.VMEM((total, width), BF16),
                pltpu.VMEM((total, width), BF16),
                pltpu.VMEM((total, 128), F32),
                pltpu.VMEM((128, total), F32),
                pltpu.VMEM((128, total), F32),
                pltpu.VMEM((total, width), F32),
                pltpu.VMEM((total, width), F32),
                pltpu.VMEM((total, width), F32),
                pltpu.VMEM((total, 128), F32),
            ],
        ),
        out_shape=[
            low, low, low, low,
            jax.ShapeDtypeStruct((total, 128), BF16),
            jax.ShapeDtypeStruct((8, 128), F32),
        ],
        compiler_params=pltpu.CompilerParams(vmem_limit_bytes=VMEM_LIMIT),
        name="attend_back",
    )(table, *qkv, gate, attended, grad, totals, cumul, logit, bias, begin[None, :])


def doc_begins(lengths_row, total):
    ends = jnp.cumsum(lengths_row)
    begins = ends - lengths_row
    place = jnp.arange(total, dtype=jnp.int32)
    inside = (place[:, None] >= begins[None, :]) & (place[:, None] < ends[None, :])
    return jnp.sum(jnp.where(inside, begins[None, :], 0), axis=1)


def per_device(
    inputs, cotangent, lengths, deal, norm1_gain, w_query, w_key, w_value, w_outgate, w_out,
    forget_weight, forget_bias, norm2_gain, w_gate, w_up, w_down,
):
    nz, np_, nq = lax.axis_size("z"), lax.axis_size("p"), lax.axis_size("q")
    z, core, p, q = (lax.axis_index(name) for name in ("z", "core", "p", "q"))
    n_ctx = 2 * nz
    nt = 2 * np_
    plane = nt * nq
    micro, _, tokens, width = inputs.shape
    heads = forget_bias.shape[0]
    depth = width // heads
    own_heads = heads // nt
    columns = width // nt
    total = tokens * n_ctx
    chunk = tokens // np_
    block = tokens // 2
    hidden = w_gate.shape[1]
    slab = w_query.shape[0]
    everywhere = ("z", "core", "p", "q")
    member = core * np_ + p
    place = ((z * 2 + core) * np_ + p) * nq + q

    gains = lax.all_gather(jnp.stack([norm1_gain, norm2_gain]), everywhere, axis=0)
    gains = gains.transpose(1, 0, 2).reshape(2, width).astype(F32)
    gain_one, gain_two = gains[0:1], gains[1:2]

    forget = forget_weight.reshape(slab, nt, own_heads)
    spare = jnp.zeros((slab, nt, 128 - 2 * own_heads), BF16)
    packed = jnp.concatenate(
        [item.reshape(slab, nt, columns) for item in (w_query, w_key, w_value, w_outgate)]
        + [forget, forget, spare],
        axis=2,
    ).transpose(1, 0, 2)
    packed = lax.all_to_all(packed, ("core", "p"), split_axis=0, concat_axis=0, tiled=True)
    packed = lax.all_gather(packed, ("z", "q"), axis=0)
    packed = packed.reshape(nz, nq, nt, slab, -1).transpose(0, 2, 1, 3, 4).reshape(width, -1)
    w_qkv, w_gf = packed[:, :3 * columns], packed[:, 3 * columns:]

    piece = width // nz
    out_w = w_out.reshape(slab, nz, piece).transpose(1, 0, 2)
    out_w = lax.all_to_all(out_w, "z", split_axis=0, concat_axis=0, tiled=True)
    out_w = lax.all_to_all(out_w, ("core", "p"), split_axis=0, concat_axis=0, tiled=True)
    out_w = lax.all_gather(out_w, ("z", "q"), axis=0)
    out_w = out_w.reshape(nz, nq, nt, slab, piece).transpose(2, 1, 3, 0, 4).reshape(columns, width)

    unit = hidden // (nz * plane)
    share = nz * unit
    ffn_w = jnp.stack(
        [item.reshape(slab, nz, plane, unit).transpose(2, 0, 1, 3).reshape(plane, slab, share) for item in (w_gate, w_up)],
        axis=2,
    ).reshape(plane, slab, 2 * share)
    ffn_w = lax.all_to_all(ffn_w, ("core", "p", "q"), split_axis=0, concat_axis=0, tiled=True)
    ffn_w = lax.all_gather(ffn_w, "z", axis=0).reshape(width, 2 * share)
    down_w = lax.all_gather(w_down, "z", axis=0, tiled=True)

    stream_m, stream_p = z // np_, z % np_
    lengths_all = jnp.stack([lengths[:, 0]] + [xor_permute(lengths[:, 0], "p", k) for k in range(1, np_)])
    lengths_row = pick(pick(lengths_all, p ^ stream_p), stream_m)
    begin = doc_begins(lengths_row, total)
    number = jnp.arange(total // chunk, dtype=jnp.int32)
    from_core = core ^ (number // (np_ * nz))
    from_p = p ^ (number // nz % np_)
    from_z = z ^ (number % nz)
    dealt = jnp.take(pick(deal, stream_m), from_z * 2 + from_core)
    inside = from_p * chunk
    natural = jnp.where(inside < block, dealt, 2 * n_ctx - 1 - dealt) * block + inside % block
    natural = natural // chunk
    table = jnp.sum(jnp.where(natural[None, :] == number[:, None], number[None, :], 0), axis=1).astype(jnp.int32)
    bias_row = jnp.zeros((1, 128), F32)
    own_bias = lax.dynamic_slice_in_dim(forget_bias, member * own_heads, own_heads, 0)[None]
    bias_row = jnp.concatenate([own_bias, own_bias, jnp.zeros((1, 128 - 2 * own_heads), F32)], axis=1)

    stream = rows_to_group(inputs[:, 0]).astype(F32)
    norm_one = lax.rsqrt(jnp.mean(stream * stream, axis=-1, keepdims=True) + EPS)
    normed = gather_heads((stream * norm_one * gain_one).astype(BF16))
    qkv = dot(normed, w_qkv, out=BF16)
    gate_logit = dot(normed, w_gf)
    queries, keys, values = (qkv[:, i * columns:(i + 1) * columns] for i in range(3))
    gate, logit = gate_logit[:, :columns], gate_logit[:, columns:]
    attended, gated, totals, cumul = attend(
        table, (queries, keys, values), gate, logit, bias_row, begin, chunk, depth
    )
    middle = stream + scatter_heads(dot(gated, out_w))
    norm_two = lax.rsqrt(jnp.mean(middle * middle, axis=-1, keepdims=True) + EPS)
    normed_two = gather_plane((middle * norm_two * gain_two).astype(BF16))
    pre = dot(normed_two, ffn_w)
    gate_pre, up_pre = pre[:, :share], pre[:, share:]
    gate_sig = jax.nn.sigmoid(gate_pre)
    activ = (gate_pre * gate_sig * up_pre).astype(BF16)
    result = (middle + scatter_plane(dot(activ, down_w))).astype(BF16)
    output = rows_from_group(result, micro)

    upstream_own = rows_to_group(cotangent[:, 0])
    upstream = gather_plane(upstream_own)
    grad_activ = dot(upstream, down_w, ((1,), (1,)))
    gate_grad = (grad_activ * up_pre * (gate_sig * (1.0 + gate_pre * (1.0 - gate_sig)))).astype(BF16)
    up_grad = (grad_activ * gate_pre * gate_sig).astype(BF16)
    ffn_grad = jnp.concatenate([gate_grad, up_grad], axis=1)
    normed_two_grad = scatter_plane(dot(ffn_grad, ffn_w, ((1,), (1,))))
    grad_ffn_w = dot(normed_two, ffn_grad, ((0,), (0,)), BF16)
    grad_down = dot(activ, upstream, ((0,), (0,)), BF16)

    unit_two = middle * norm_two
    gain_two_sum = jnp.sum(normed_two_grad * unit_two, axis=0)
    scaled_two = normed_two_grad * gain_two
    middle_grad = upstream_own.astype(F32) + norm_two * (
        scaled_two - unit_two * jnp.mean(scaled_two * unit_two, axis=-1, keepdims=True)
    )
    branch_grad = gather_heads(middle_grad.astype(BF16))
    gated_grad = dot(branch_grad, out_w, ((1,), (1,)))
    grad_out = dot(gated, branch_grad, ((0,), (0,)), BF16)
    dq, dk, dv, dg, dz, dbias = attend_back(
        table, (queries, keys, values), gate, attended, gated_grad, totals, cumul, logit, bias_row, begin, chunk, depth
    )
    right = jnp.concatenate([dq, dk, dv, dg, dz], axis=1)
    normed_grad = scatter_heads(dot(right, packed, ((1,), (1,))))
    grad_packed = dot(normed, right, ((0,), (0,)), BF16)
    unit_one = stream * norm_one
    gain_one_sum = jnp.sum(normed_grad * unit_one, axis=0)
    scaled_one = normed_grad * gain_one
    stream_grad = middle_grad + norm_one * (
        scaled_one - unit_one * jnp.mean(scaled_one * unit_one, axis=-1, keepdims=True)
    )
    input_grad = rows_from_group(stream_grad.astype(BF16), micro).astype(F32)

    grad_ffn_w = lax.psum_scatter(grad_ffn_w, "z", scatter_dimension=0, tiled=True)
    grad_ffn_w = lax.all_to_all(
        grad_ffn_w.reshape(plane, slab, 2 * share), ("core", "p", "q"), split_axis=0, concat_axis=0, tiled=True
    ).astype(F32)
    grad_gate, grad_up = (
        item.reshape(plane, slab, nz, unit).transpose(1, 2, 0, 3).reshape(slab, hidden)
        for item in (grad_ffn_w[:, :, :share], grad_ffn_w[:, :, share:])
    )
    grad_down = lax.psum_scatter(grad_down, "z", scatter_dimension=0, tiled=True).astype(F32)

    grad_out = grad_out.reshape(nt, nq, slab, nz, piece).transpose(3, 1, 0, 2, 4).reshape(nz * nq, nt, slab, piece)
    grad_out = lax.psum_scatter(grad_out, ("z", "q"), scatter_dimension=0, tiled=True)[0]
    grad_out = lax.all_to_all(grad_out, ("core", "p"), split_axis=0, concat_axis=0, tiled=True)
    grad_out = lax.all_to_all(grad_out, "z", split_axis=0, concat_axis=0, tiled=True)
    grad_out = grad_out.transpose(1, 0, 2).reshape(slab, width).astype(F32)

    grad_packed = grad_packed.reshape(nz, nt, nq, slab, -1).transpose(0, 2, 1, 3, 4).reshape(nz * nq, nt, slab, -1)
    grad_packed = lax.psum_scatter(grad_packed, ("z", "q"), scatter_dimension=0, tiled=True)[0]
    grad_packed = lax.all_to_all(grad_packed, ("core", "p"), split_axis=0, concat_axis=0, tiled=True).astype(F32)
    grad_query, grad_key, grad_value, grad_outgate = (
        grad_packed[:, :, i * columns:(i + 1) * columns].transpose(1, 0, 2).reshape(slab, width) for i in range(4)
    )
    tail = grad_packed[:, :, 4 * columns:]
    grad_forget = (tail[:, :, :own_heads] + tail[:, :, own_heads:2 * own_heads]).transpose(1, 0, 2).reshape(slab, heads)

    bias_sum = lax.dynamic_update_slice_in_dim(
        jnp.zeros((width,), F32), dbias[0, :own_heads], member * own_heads, 0
    )
    sums = lax.psum(jnp.stack([gain_one_sum, gain_two_sum, bias_sum]), everywhere)
    grad_gain_one = lax.dynamic_slice_in_dim(sums[0], place * slab, slab, 0)
    grad_gain_two = lax.dynamic_slice_in_dim(sums[1], place * slab, slab, 0)
    return (
        output[:, None], input_grad[:, None], grad_gain_one, grad_query, grad_key, grad_value, grad_outgate,
        grad_out, grad_forget, sums[2, :heads], grad_gain_two, grad_gate, grad_up, grad_down,
    )


def solution(mesh):
    n_ctx, n_fsdp = mesh.shape["ctx"], mesh.shape["fsdp"]
    fine = Mesh(mesh.devices.reshape(n_ctx // 2, 2, n_fsdp // 2, 2), ("z", "core", "p", "q"))
    ctx, fsdp, every = ("z", "core"), ("p", "q"), ("z", "core", "p", "q")
    rows = P(None, fsdp, ctx, None)
    vector, matrix = P(every), P(every, None)
    return jax.shard_map(
        per_device,
        mesh=fine,
        in_specs=(
            rows, rows, P(None, fsdp, None), P(), vector, matrix, matrix, matrix, matrix, matrix, matrix, P(),
            vector, matrix, matrix, matrix,
        ),
        out_specs=(
            rows, rows, vector, matrix, matrix, matrix, matrix, matrix, matrix, P(), vector, matrix, matrix, matrix,
        ),
        check_vma=False,
    )
```

time: 2450 us -> 719 us (0.29)
  waiting for transfers between devices: 1480 us -> 233 us
  local copies, waits for them, and re-layouts: 289 us -> 86.8 us
  matrix products: 289 us -> 91 us
  other arithmetic: 159 us -> 39.1 us
  starting transfers between devices: 1.01 us -> 70.9 us
  Pallas kernels: 0 us -> 30.2 us
  between operations: 45.4 us -> 15.8 us
  blocking collectives: 175 us -> 147 us
    reduce_scatter x6 -> x4, waiting for transfers between devices: 1090 us -> 10.1 us  [the longest x1 10.1 us: per_device(): lax.psum_scatter(grad_packed, ('z', 'q'), scatter_dimension=0, tiled=True)]
    all_gather x12 -> x4, waiting for transfers between devices: 374 us -> 0.03 us  [the longest x1 0.02 us: per_device(): packed = lax.all_gather(packed, ('z', 'q'), axis=0)]
    dot_general x69 -> x13, matrix products: 289 us -> 91 us  [dot(): lax.dot_general(left, right, (contract, ((), ())), preferred_element_type...]
    ppermute x0 -> x53, waiting for transfers between devices: none -> 197 us  [xor_permute(): return lax.ppermute(x, axis, [(i, i ^ step) for i in range(n)])]
    another operation x62 -> x4, local copies, waits for them, and re-layouts: 133 us -> 0.91 us  [the longest x2 0.6 us: per_device(): jnp.stack([gain_one_sum, gain_two_sum, bias_sum])]
    concatenate x6 -> x8, other arithmetic: 71.6 us -> 1.92 us  [the longest x1 1.01 us: rows_to_group(): return jnp.concatenate(rows, axis=0)]
    while x162 -> x0, local copies, waits for them, and re-layouts: 64.1 us -> none  [the longest x14 32.1 us: attend(): lax.fori_loop(first_tile, last_tile, second_pass, jnp.zeros((rows, heads,...]
    ppermute x0 -> x53, starting transfers between devices: none -> 51.1 us  [xor_permute(): return lax.ppermute(x, axis, [(i, i ^ step) for i in range(n)])]
  transfers between devices with their start and end apart: 21 -> 66, of which waited for: 11 -> 29; matrix products, arithmetic and copies ran while one was open for 23% -> 25% of each run, Pallas kernels for 0% -> 4%
where the time goes in v1:
time: 719 us; the launch traced here: 714 us
  waiting for transfers between devices  233 us (32%)
  blocking collectives  147 us (20%)
  matrix products  91 us (13%)
  local copies, waits for them, and re-layouts  86.8 us (12%)
  starting transfers between devices  70.9 us (10%)
  other arithmetic  39.1 us (5%)
  Pallas kernels  30.2 us (4%)
  between operations  15.8 us (2%)
    ppermute x53, waiting for transfers between devices, xor_permute(): return lax.ppermute(x, axis, [(i, i ^ step) for i in range(n)])  197 us
    dot_general x13, matrix products, dot(): lax.dot_general(left, right, (contract, ((), ())), preferred_element_type...  91 us
    all_gather x1, blocking collectives, per_device(): lax.all_gather(jnp.stack([norm1_gain, norm2_gain]), everywhere, axis=0)  73.3 us
    ppermute x53, starting transfers between devices, xor_permute(): return lax.ppermute(x, axis, [(i, i ^ step) for i in range(n)])  51.1 us
    psum x1, blocking collectives, per_device(): lax.psum(jnp.stack([gain_one_sum, gain_two_sum, bias_sum]), everywhere)  39.9 us
    unnamed x146, local copies, waits for them, and re-layouts  38.1 us
    pallas_call x1, Pallas kernels, attend_back(): pl.pallas_call(functools.partial(attend_back_kernel, chunk, depth, column...  18 us
  transfers between devices with their start and end apart: 66, of which 29 were waited for; matrix products, arithmetic and copies ran while one was open for 25% of the time, Pallas kernels for 4%

profile of v1, /device:TPU:0, one launch (start us, length us, event | category | flops | bytes accessed | tf_op | source)
XLA Modules:
  0.0 714.0 jit_solution(17004377294622847389)
XLA Ops:
  8.2 12.8 %all_to_all.40 = bf16[4,48,384]{2,1,0:T(8,128)(2,1)S(1)} all-to-all(bf16[4,48,384]{2,1,0:T(8,128)(2,1)S(1)} %copy.111), channel_id=1, replica_groups=mesh['z'=4,'core'=2,'p'=2,'q'=2] {'z'}, dimensions={0} | all-to-all | bytes 294912 | tf_op jit(solution)/shard_map/all_to_all | solution.py:458
  21.0 8.0 %all_to_all.41 = bf16[4,48,384]{2,1,0:T(8,128)(2,1)} all-to-all(bf16[4,48,384]{2,1,0:T(8,128)(2,1)S(1)} %all_to_all.40), channel_id=1, replica_groups=mesh['z'=4,'core'=2,'p'=2,'q'=2] {'core','p'}, dimensions={0} | all-to-all | bytes 294912 | tf_op jit(solution)/shard_map/all_to_all | solution.py:459
  34.6 13.3 %all_to_all.42 = bf16[4,48,1664]{2,1,0:T(8,128)(2,1)} all-to-all(bf16[4,48,1664]{2,1,0:T(8,128)(2,1)S(1)} %copy.108), channel_id=1, replica_groups=mesh['z'=4,'core'=2,'p'=2,'q'=2] {'core','p'}, dimensions={0} | all-to-all | bytes 1277952 | tf_op jit(solution)/shard_map/all_to_all | solution.py:451
  55.8 73.3 %all-gather.4 = bf16[32,2,48]{2,1,0:T(2,128)(2,1)S(1)} all-gather(bf16[1,2,48]{2,1,0:T(2,128)(2,1)S(1)} %maximum_bitcast_fusion.3), channel_id=2, replica_groups=mesh['z'=4,'core'=2,'p'=2,'q'=2] {'z','core','p','q'}, dimensions={0}, use_global_device_ids=true | all-gather | bytes 6336 | tf_op jit(solution)/shard_map/all_gather | solution.py:440
  134.4 8.6 %collective-permute-done.3 = bf16[64,1536]{1,0:T(8,128)(2,1)S(1)} collective-permute-done((bf16[64,1536]{1,0:T(8,128)(2,1)S(1)}, bf16[64,1536]{1,0:T(8,128)(2,1)S(1)}, u32[]{:S(2)}, u32[]{:S(2)}) %collective-permute-start.3) | collective-permute-done | bytes 196640 | tf_op jit(solution)/shard_map/ppermute | solution.py:24
  143.0 15.0 %collective-permute-done.2 = bf16[64,1536]{1,0:T(8,128)(2,1)S(1)} collective-permute-done((bf16[64,1536]{1,0:T(8,128)(2,1)S(1)}, bf16[64,1536]{1,0:T(8,128)(2,1)S(1)}, u32[]{:S(2)}, u32[]{:S(2)}) %collective-permute-start.2) | collective-permute-done | bytes 196640 | tf_op jit(solution)/shard_map/ppermute | solution.py:24
  164.6 15.6 %collective-permute-done.4 = bf16[256,1536]{1,0:T(8,128)(2,1)} collective-permute-done((bf16[256,1536]{1,0:T(8,128)(2,1)}, bf16[256,1536]{1,0:T(8,128)(2,1)}, u32[]{:S(2)}, u32[]{:S(2)}) %collective-permute-start.4) | collective-permute-done | bytes 786464 | tf_op jit(solution)/shard_map/ppermute | solution.py:24
  198.7 6.1 fusion
  206.3 12.2 %attend.1 = (f32[1024,384]{1,0:T(8,128)}, bf16[1024,384]{1,0:T(8,128)(2,1)}, f32[1024,128]{1,0:T(8,128)}, f32[1024,128]{1,0:T(8,128)}) custom-call(s32[16]{0:T(128)} %select_reduce_fusion.1.table, bf16[1024,384]{1,0:T(8,128)(2,1)} %get-tuple-element.67.q_ref, bf16[1024,384]{1,0:T(8,128)(2,1)} %get-tuple-element.66.k_ref, ...), custom_call_target="tpu_custom_call" | custom-call | tf_op jit(solution)/shard_map/attend/pallas_call | solution.py:337
  228.3 8.6 %collective-permute-done.30 = bf16[64,1536]{1,0:T(8,128)(2,1)S(1)} collective-permute-done((bf16[64,1536]{1,0:T(8,128)(2,1)S(1)}, bf16[64,1536]{1,0:T(8,128)(2,1)S(1)}, u32[]{:S(2)}, u32[]{:S(2)}) %collective-permute-start.30) | collective-permute-done | bytes 196640 | tf_op jit(solution)/shard_map/ppermute | solution.py:24
  237.0 14.3 %collective-permute-done.29 = bf16[64,1536]{1,0:T(8,128)(2,1)S(1)} collective-permute-done((bf16[64,1536]{1,0:T(8,128)(2,1)S(1)}, bf16[64,1536]{1,0:T(8,128)(2,1)S(1)}, u32[]{:S(2)}, u32[]{:S(2)}) %collective-permute-start.29) | collective-permute-done | bytes 196640 | tf_op jit(solution)/shard_map/ppermute | solution.py:24
  258.3 13.6 %collective-permute-done.32 = bf16[256,1536]{1,0:T(8,128)(2,1)} collective-permute-done((bf16[256,1536]{1,0:T(8,128)(2,1)}, bf16[256,1536]{1,0:T(8,128)(2,1)}, u32[]{:S(2)}, u32[]{:S(2)}) %collective-permute-start.32) | collective-permute-done | bytes 786464 | tf_op jit(solution)/shard_map/ppermute | solution.py:24
  287.2 15.0 %collective-permute-done.9 = bf16[256,1536]{1,0:T(8,128)(2,1)S(1)} collective-permute-done((bf16[256,1536]{1,0:T(8,128)(2,1)S(1)}, bf16[256,1536]{1,0:T(8,128)(2,1)S(1)}, u32[]{:S(2)}, u32[]{:S(2)}) %collective-permute-start.9) | collective-permute-done | bytes 786464 | tf_op jit(solution)/shard_map/ppermute | solution.py:24
  309.9 13.1 %collective-permute-done.11 = bf16[256,1536]{1,0:T(8,128)(2,1)S(1)} collective-permute-done((bf16[256,1536]{1,0:T(8,128)(2,1)S(1)}, bf16[256,1536]{1,0:T(8,128)(2,1)S(1)}, u32[]{:S(2)}, u32[]{:S(2)}) %collective-permute-start.11) | collective-permute-done | bytes 786464 | tf_op jit(solution)/shard_map/ppermute | solution.py:24
  339.1 11.7 %fusion.72 = f32[2048,1024]{0,1:T(8,128)} fusion(bf16[2048,1536]{1,0:T(8,128)(2,1)} %constant_dynamic-update-slice_fusion, bf16[1536,1024]{1,0:T(8,128)(2,1)} %bitcast.305), kind=kOutput, calls=%fused_computation.252 | convolution fusion | flops 6442450944 | bytes 17825792 | tf_op jit(solution)/shard_map/dot_general | solution.py:19
  350.8 12.4 %multiply_convert_fusion.1 = (bf16[2048,512]{0,1:T(8,128)(2,1)}, bf16[2048,512]{0,1:T(8,128)(2,1)}, bf16[2048,512]{0,1:T(8,128)(2,1)S(1)}) fusion(f32[2048,1024]{0,1:T(8,128)} %fusion.72, bf16[2048,1536]{1,0:T(8,128)(2,1)} %constant_dynamic-update-slice_fusion.9, bf16[512,1536]{1,0:T(8,128)(2,1)} %all-gather.10.cloned.1.call-done), kind=kOutput, calls=%fused_computation.7 | convolution fusion | flops 3238002688 | bytes 22544384 | tf_op jit(solution)/shard_map/dot_general | solution.py:19
  364.5 7.3 %fusion.75 = bf16[512,1536]{1,0:T(8,128)(2,1)} fusion(bf16[2048,512]{0,1:T(8,128)(2,1)S(1)} %get-tuple-element.52, bf16[2048,1536]{1,0:T(8,128)(2,1)} %constant_dynamic-update-slice_fusion.9), kind=kOutput, calls=%fused_computation.255 | convolution fusion | flops 3221225472 | bytes 9961472 | tf_op jit(solution)/shard_map/dot_general | solution.py:19
  371.9 9.7 %fusion.3 = f32[2048,1536]{1,0:T(8,128)S(1)} fusion(bf16[1536,1024]{1,0:T(8,128)(2,1)} %bitcast.306, bf16[2048,512]{0,1:T(8,128)(2,1)} %get-tuple-element.51, bf16[2048,512]{0,1:T(8,128)(2,1)} %get-tuple-element.50), kind=kOutput, calls=%fused_computation.19 | convolution fusion | flops 6450839552 | bytes 19922944 | tf_op jit(solution)/shard_map/dot_general | solution.py:19
  400.1 10.0 %fusion.2 = bf16[1536,1024]{1,0:T(8,128)(2,1)} fusion(bf16[2048,1536]{1,0:T(8,128)(2,1)} %constant_dynamic-update-slice_fusion, bf16[2048,512]{0,1:T(8,128)(2,1)S(1)} %copy-done.59, bf16[2048,512]{0,1:T(8,128)(2,1)S(1)} %copy-done.58), kind=kOutput, calls=%fused_computation.18 | convolution fusion | flops 6450839552 | bytes 13631488 | tf_op jit(solution)/shard_map/dot_general | solution.py:19
  440.2 13.4 %collective-permute-done.43 = bf16[256,1536]{1,0:T(8,128)(2,1)S(1)} collective-permute-done((bf16[256,1536]{1,0:T(8,128)(2,1)S(1)}, bf16[256,1536]{1,0:T(8,128)(2,1)S(1)}, u32[]{:S(2)}, u32[]{:S(2)}) %collective-permute-start.43) | collective-permute-done | bytes 786464 | tf_op jit(solution)/shard_map/ppermute | solution.py:24
  455.3 13.8 %collective-permute-done.22 = bf16[256,1536]{1,0:T(8,128)(2,1)S(1)} collective-permute-done((bf16[256,1536]{1,0:T(8,128)(2,1)S(1)}, bf16[256,1536]{1,0:T(8,128)(2,1)S(1)}, u32[]{:S(2)}, u32[]{:S(2)}) %collective-permute-start.22) | collective-permute-done | bytes 786464 | tf_op jit(solution)/shard_map/ppermute | solution.py:24
  473.7 17.0 %collective-permute-done.44 = bf16[256,1536]{1,0:T(8,128)(2,1)S(1)} collective-permute-done((bf16[256,1536]{1,0:T(8,128)(2,1)S(1)}, bf16[256,1536]{1,0:T(8,128)(2,1)S(1)}, u32[]{:S(2)}, u32[]{:S(2)}) %collective-permute-start.44) | collective-permute-done | bytes 786464 | tf_op jit(solution)/shard_map/ppermute | solution.py:24
  501.7 18.0 %attend_back.1 = (bf16[1024,384]{1,0:T(8,128)(2,1)}, bf16[1024,384]{1,0:T(8,128)(2,1)}, bf16[1024,384]{1,0:T(8,128)(2,1)}, bf16[1024,384]{1,0:T(8,128)(2,1)}, bf...) custom-call(s32[16]{0:T(128)} %select_reduce_fusion.1.table, bf16[1024,384]{1,0:T(8,128)(2,1)} %get-tuple-element.67.q_ref, ...), custom_call_target="tpu_custom_call" | custom-call | tf_op jit(solution)/shard_map/attend_back/pallas_call | solution.py:374
  522.9 7.6 %fusion.66 = bf16[1536,1664]{1,0:T(8,128)(2,1)S(1)} fusion(bf16[1024,1664]{1,0:T(8,128)(2,1)S(1)} %constant_dynamic-update-slice_fusion.21, bf16[256,1536]{1,0:T(8,128)(2,1)} %collective-permute-done.6, bf16[256,1536]{1,0:T(8,128)(2,1)} %collective-permute-done.5, bf16[256,1536]{1,0:T(8,128)(2,1)} %collective-permute-done.4, bf16[256,1536]{1,0:T(8,128)(2,1)} %fusion.8), kind=kOutput, calls=%fused_computation.246 | convolution fusion | flops 5247074304 | bytes 11665408 | tf_op jit(solution)/shard_map/dot_general | solution.py:19
  533.3 7.9 %fusion.74 = f32[1024,1536]{1,0:T(8,128)S(1)} fusion(bf16[1024,1664]{1,0:T(8,128)(2,1)S(1)} %constant_dynamic-update-slice_fusion.21, bf16[1536,1664]{1,0:T(8,128)(2,1)} %bitcast.256), kind=kOutput, calls=%fused_computation.254 | convolution fusion | flops 5234491392 | bytes 14811136 | tf_op jit(solution)/shard_map/dot_general | solution.py:19
  556.7 11.4 %collective-permute-done.24 = bf16[64,1536]{1,0:T(8,128)(2,1)S(1)} collective-permute-done((bf16[64,1536]{1,0:T(8,128)(2,1)S(1)}, bf16[64,1536]{1,0:T(8,128)(2,1)S(1)}, u32[]{:S(2)}, u32[]{:S(2)}) %collective-permute-start.24) | collective-permute-done | bytes 196640 | tf_op jit(solution)/shard_map/ppermute | solution.py:24
  577.0 8.7 %all-to-all-done.7 = bf16[8,48,1024]{2,1,0:T(8,128)(2,1)S(1)} async-done(((bf16[8,48,1024]{2,1,0:T(8,128)(2,1)}), bf16[8,48,1024]{2,1,0:T(8,128)(2,1)S(1)}, u32[]{:S(2)}, u32[]{:S(2)}) %all-to-all-start.7) | async-done | bytes 786464 | tf_op jit(solution)/shard_map/all_to_all | solution.py:544
  600.3 11.9 %collective-permute-done.48 = bf16[256,1536]{1,0:T(8,128)(2,1)} collective-permute-done((bf16[256,1536]{1,0:T(8,128)(2,1)}, bf16[256,1536]{1,0:T(8,128)(2,1)}, u32[]{:S(2)}, u32[]{:S(2)}) %collective-permute-start.48) | collective-permute-done | bytes 786464 | tf_op jit(solution)/shard_map/ppermute | solution.py:24
  620.6 39.9 %psum.7 = f32[3,1536]{1,0:T(4,128)S(1)} all-reduce(f32[3,1536]{1,0:T(4,128)S(1)} %pad_maximum_fusion.23), channel_id=1, replica_groups=mesh['z'=4,'core'=2,'p'=2,'q'=2] {'z','core','p','q'}, use_global_device_ids=true, to_apply=%region_9.10 | all-reduce | flops 4608 | bytes 36864 | tf_op jit(solution)/shard_map/psum | solution.py:571
  667.9 8.1 %all-to-all-done.6 = bf16[4,48,384]{2,1,0:T(8,128)(2,1)S(1)} async-done(((bf16[4,48,384]{2,1,0:T(8,128)(2,1)}), bf16[4,48,384]{2,1,0:T(8,128)(2,1)S(1)}, u32[]{:S(2)}, u32[]{:S(2)}) %all-to-all-start.6) | async-done | bytes 147488 | tf_op jit(solution)/shard_map/all_to_all | solution.py:556
  679.4 10.1 %reduce-scatter.5.cloned.1.call-done = bf16[1,4,48,1664]{3,2,1,0:T(8,128)(2,1)} async-done(((bf16[8,4,48,1664]{3,2,1,0:T(8,128)(2,1)}), bf16[1,4,48,1664]{3,2,1,0:T(8,128)(2,1)}) %reduce-scatter.5.cloned.1.call-update) | async-done | bytes 638992 | tf_op jit(solution)/shard_map/reduce_scatter | solution.py:560
  694.3 8.7 %all-to-all-done.4 = bf16[4,48,1664]{2,1,0:T(8,128)(2,1)S(1)} async-done(((bf16[4,48,1664]{2,1,0:T(8,128)(2,1)}), bf16[4,48,1664]{2,1,0:T(8,128)(2,1)S(1)}, u32[]{:S(2)}, u32[]{:S(2)}) %all-to-all-start.4) | async-done | bytes 639008 | tf_op jit(solution)/shard_map/all_to_all | solution.py:561
  (405 shorter events, 240.9 us)
Async XLA Ops:
  7.2 178.6 %all-gather.14.cloned.1.call-start = ((), (), s32[]{:S(2)}) async-start(), calls=%async_computation.18 | async-start | bytes 1327104 | tf_op jit(solution)/shard_map/all_gather | solution.py:460
  29.0 159.1 %all-gather.12.cloned.1.call-start = ((), (), s32[]{:S(2)}) async-start(), calls=%async_computation.17 | async-start | bytes 5750784 | tf_op jit(solution)/shard_map/all_gather | solution.py:452
  48.0 81.0 %collective-permute-start = (bf16[2,64,1536]{2,1,0:T(8,128)(2,1)S(1)}, bf16[2,64,1536]{2,1,0:T(8,128)(2,1)S(1)}, u32[]{:S(2)}, u32[]{:S(2)}) collective-permute-start(bf16[2,64,1536]{2,1,0:T(8,128)(2,1)S(1)} %get-tuple-element.105), channel_id=1, source_target_pairs={{0,2},{2,0},{1,3},{3,1},{4,6},{6,4},{5,7},{7,5},{8,10},{10,8},{9,1... | collective-permute-start | bytes 1179656 | tf_op jit(solution)/shard_map/ppermute | solution.py:24
  48.3 132.6 %collective-permute-start.7 = (s32[2,4]{1,0:T(2,128)S(1)}, s32[2,4]{1,0:T(2,128)S(1)}, u32[]{:S(2)}, u32[]{:S(2)}) collective-permute-start(s32[2,4]{1,0:T(2,128)S(1)} %bitcast.300), channel_id=1, source_target_pairs={{0,2},{2,0},{1,3},{3,1},{4,6},{6,4},{5,7},{7,5},{8,10},{10,8},{9,1... | collective-permute-start | bytes 104 | tf_op jit(solution)/shard_map/ppermute | solution.py:24
  52.0 107.5 %all-to-all-start.3 = ((bf16[8,48,1024]{2,1,0:T(8,128)(2,1)}), bf16[8,48,1024]{2,1,0:T(8,128)(2,1)S(1)}, u32[]{:S(2)}, u32[]{:S(2)}) async-start(bf16[8,48,1024]{2,1,0:T(8,128)(2,1)} %bitcast.103), calls=%async_computation.3 | async-start | bytes 1572864 | tf_op jit(solution)/shard_map/all_to_all | solution.py:469
  55.6 283.5 %all-gather.16.cloned.1.call-start = ((), (), s32[]{:S(2)}) async-start(), calls=%async_computation.19 | async-start | bytes 3932160 | tf_op jit(solution)/shard_map/all_gather | solution.py:470
  129.3 28.8 %collective-permute-start.2 = (bf16[64,1536]{1,0:T(8,128)(2,1)S(1)}, bf16[64,1536]{1,0:T(8,128)(2,1)S(1)}, u32[]{:S(2)}, u32[]{:S(2)}) collective-permute-start(bf16[64,1536]{1,0:T(8,128)(2,1)S(1)} %get-tuple-element.102), channel_id=1, source_target_pairs={{0,16},{8,24},{16,0},{24,8},{1,17},{9,25},{17,1},{25,9},{2,18},{10... | collective-permute-start | bytes 589832 | tf_op jit(solution)/shard_map/ppermute | solution.py:24
  129.4 28.7 %collective-permute-start.1 = (bf16[64,1536]{1,0:T(8,128)(2,1)S(1)}, bf16[64,1536]{1,0:T(8,128)(2,1)S(1)}, u32[]{:S(2)}, u32[]{:S(2)}) collective-permute-start(bf16[64,1536]{1,0:T(8,128)(2,1)S(1)} %get-tuple-element.103), channel_id=1, source_target_pairs={{0,8},{8,0},{16,24},{24,16},{1,9},{9,1},{17,25},{25,17},{2,10},{10... | collective-permute-start | bytes 589832 | tf_op jit(solution)/shard_map/ppermute | solution.py:24
  160.4 190.4 %all-gather.10.cloned.1.call-start = ((), (), s32[]{:S(2)}) async-start(), calls=%async_computation.12 | async-start | bytes 1966080 | tf_op jit(solution)/shard_map/all_gather | solution.py:471
  161.1 23.7 %collective-permute-start.27 = (bf16[2,64,1536]{2,1,0:T(8,128)(2,1)S(1)}, bf16[2,64,1536]{2,1,0:T(8,128)(2,1)S(1)}, u32[]{:S(2)}, u32[]{:S(2)}) collective-permute-start(bf16[2,64,1536]{2,1,0:T(8,128)(2,1)S(1)} %get-tuple-element.89), channel_id=1, source_target_pairs={{0,2},{2,0},{1,3},{3,1},{4,6},{6,4},{5,7},{7,5},{8,10},{10,8},{9,1... | collective-permute-start | bytes 1179656 | tf_op jit(solution)/shard_map/ppermute | solution.py:24
  164.6 26.4 %collective-permute-start.5 = (bf16[256,1536]{1,0:T(8,128)(2,1)}, bf16[256,1536]{1,0:T(8,128)(2,1)}, u32[]{:S(2)}, u32[]{:S(2)}) collective-permute-start(bf16[256,1536]{1,0:T(8,128)(2,1)} %fusion.8), channel_id=1, source_target_pairs={{0,4},{4,0},{1,5},{5,1},{2,6},{6,2},{3,7},{7,3},{8,12},{12,8},{9,1... | collective-permute-start | bytes 2359304 | tf_op jit(solution)/shard_map/ppermute | solution.py:24
  222.7 56.3 %collective-permute-start.8 = (bf16[512,1536]{1,0:T(8,128)(2,1)}, bf16[512,1536]{1,0:T(8,128)(2,1)}, u32[]{:S(2)}, u32[]{:S(2)}) collective-permute-start(bf16[512,1536]{1,0:T(8,128)(2,1)} %slice.452), channel_id=1, source_target_pairs={{0,4},{4,0},{1,5},{5,1},{2,6},{6,2},{3,7},{7,3},{8,12},{12,8},{9,1... | collective-permute-start | bytes 4718600 | tf_op jit(solution)/shard_map/ppermute | solution.py:24
  227.0 24.2 %collective-permute-start.29 = (bf16[64,1536]{1,0:T(8,128)(2,1)S(1)}, bf16[64,1536]{1,0:T(8,128)(2,1)S(1)}, u32[]{:S(2)}, u32[]{:S(2)}) collective-permute-start(bf16[64,1536]{1,0:T(8,128)(2,1)S(1)} %get-tuple-element.86), channel_id=1, source_target_pairs={{0,16},{8,24},{16,0},{24,8},{1,17},{9,25},{17,1},{25,9},{2,18},{10... | collective-permute-start | bytes 589832 | tf_op jit(solution)/shard_map/ppermute | solution.py:24
  227.0 24.2 %collective-permute-start.28 = (bf16[64,1536]{1,0:T(8,128)(2,1)S(1)}, bf16[64,1536]{1,0:T(8,128)(2,1)S(1)}, u32[]{:S(2)}, u32[]{:S(2)}) collective-permute-start(bf16[64,1536]{1,0:T(8,128)(2,1)S(1)} %get-tuple-element.87), channel_id=1, source_target_pairs={{0,8},{8,0},{16,24},{24,16},{1,9},{9,1},{17,25},{25,17},{2,10},{10... | collective-permute-start | bytes 589832 | tf_op jit(solution)/shard_map/ppermute | solution.py:24
  255.2 294.5 %reduce-scatter.11.cloned.1.call-start = ((), (), s32[]{:S(2)}) async-start(), calls=%async_computation.16 | async-start | bytes 1966080 | tf_op jit(solution)/shard_map/reduce_scatter | solution.py:551
  256.2 48.9 %collective-permute-start.35 = (bf16[256,1536]{1,0:T(8,128)(2,1)}, bf16[256,1536]{1,0:T(8,128)(2,1)S(1)}, u32[]{:S(2)}, u32[]{:S(2)}) collective-permute-start(bf16[256,1536]{1,0:T(8,128)(2,1)} %pad_maximum_fusion.13), channel_id=1, source_target_pairs={{0,4},{4,0},{1,5},{5,1},{2,6},{6,2},{3,7},{7,3},{8,12},{12,8},{9,1... | collective-permute-start | bytes 2359304 | tf_op jit(solution)/shard_map/ppermute | solution.py:24
  277.0 31.0 %collective-permute-start.37 = (bf16[256,1536]{1,0:T(8,128)(2,1)}, bf16[256,1536]{1,0:T(8,128)(2,1)S(1)}, u32[]{:S(2)}, u32[]{:S(2)}) collective-permute-start(bf16[256,1536]{1,0:T(8,128)(2,1)} %collective-permute-done.32), channel_id=1, source_target_pairs={{0,4},{4,0},{1,5},{5,1},{2,6},{6,2},{3,7},{7,3},{8,12},{12,8},{9,1... | collective-permute-start | bytes 2359304 | tf_op jit(solution)/shard_map/ppermute | solution.py:24
  285.5 23.4 %collective-permute-start.38 = (bf16[256,1536]{1,0:T(8,128)(2,1)S(1)}, bf16[256,1536]{1,0:T(8,128)(2,1)S(1)}, u32[]{:S(2)}, u32[]{:S(2)}) collective-permute-start(bf16[256,1536]{1,0:T(8,128)(2,1)S(1)} %pad_maximum_fusion.14), channel_id=1, source_target_pairs={{0,4},{4,0},{1,5},{5,1},{2,6},{6,2},{3,7},{7,3},{8,12},{12,8},{9,1... | collective-permute-start | bytes 2359304 | tf_op jit(solution)/shard_map/ppermute | solution.py:24
  309.9 25.3 %collective-permute-start.14 = (bf16[256,1536]{1,0:T(8,128)(2,1)S(1)}, bf16[256,1536]{1,0:T(8,128)(2,1)S(1)}, u32[]{:S(2)}, u32[]{:S(2)}) collective-permute-start(bf16[256,1536]{1,0:T(8,128)(2,1)S(1)} %get-tuple-element.47), channel_id=1, source_target_pairs={{0,4},{4,0},{1,5},{5,1},{2,6},{6,2},{3,7},{7,3},{8,12},{12,8},{9,1... | collective-permute-start | bytes 2359304 | tf_op jit(solution)/shard_map/ppermute | solution.py:24
  371.8 196.4 %reduce-scatter.9.cloned.1.call-start = ((), (), s32[]{:S(2)}) async-start(), calls=%async_computation.15 | async-start | bytes 3932160 | tf_op jit(solution)/shard_map/reduce_scatter | solution.py:543
  410.2 186.1 %reduce-scatter.7.cloned.1.call-start = ((), (), s32[]{:S(2)}) async-start(), calls=%async_computation.14 | async-start | bytes 1327104 | tf_op jit(solution)/shard_map/reduce_scatter | solution.py:554
  429.0 24.5 %collective-permute-start.43 = (bf16[256,1536]{1,0:T(8,128)(2,1)S(1)}, bf16[256,1536]{1,0:T(8,128)(2,1)S(1)}, u32[]{:S(2)}, u32[]{:S(2)}) collective-permute-start(bf16[256,1536]{1,0:T(8,128)(2,1)S(1)} %pad_maximum_fusion.16), channel_id=1, source_target_pairs={{0,2},{2,0},{1,3},{3,1},{4,6},{6,4},{5,7},{7,5},{8,10},{10,8},{9,1... | collective-permute-start | bytes 2359304 | tf_op jit(solution)/shard_map/ppermute | solution.py:24
  430.7 23.3 %collective-permute-start.41 = (bf16[256,1536]{1,0:T(8,128)(2,1)S(1)}, bf16[256,1536]{1,0:T(8,128)(2,1)S(1)}, u32[]{:S(2)}, u32[]{:S(2)}) collective-permute-start(bf16[256,1536]{1,0:T(8,128)(2,1)S(1)} %pad_maximum_fusion.15), channel_id=1, source_target_pairs={{0,1},{1,0},{2,3},{3,2},{4,5},{5,4},{6,7},{7,6},{8,9},{9,8},{10,11... | collective-permute-start | bytes 2359304 | tf_op jit(solution)/shard_map/ppermute | solution.py:24
  437.5 31.6 %collective-permute-start.22 = (bf16[256,1536]{1,0:T(8,128)(2,1)S(1)}, bf16[256,1536]{1,0:T(8,128)(2,1)S(1)}, u32[]{:S(2)}, u32[]{:S(2)}) collective-permute-start(bf16[256,1536]{1,0:T(8,128)(2,1)S(1)} %pad_maximum_fusion.9), channel_id=1, source_target_pairs={{0,2},{2,0},{1,3},{3,1},{4,6},{6,4},{5,7},{7,5},{8,10},{10,8},{9,1... | collective-permute-start | bytes 2359304 | tf_op jit(solution)/shard_map/ppermute | solution.py:24
  439.2 30.4 %collective-permute-start.20 = (bf16[256,1536]{1,0:T(8,128)(2,1)S(1)}, bf16[256,1536]{1,0:T(8,128)(2,1)S(1)}, u32[]{:S(2)}, u32[]{:S(2)}) collective-permute-start(bf16[256,1536]{1,0:T(8,128)(2,1)S(1)} %pad_maximum_fusion.8), channel_id=1, source_target_pairs={{0,1},{1,0},{2,3},{3,2},{4,5},{5,4},{6,7},{7,6},{8,9},{9,8},{10,11... | collective-permute-start | bytes 2359304 | tf_op jit(solution)/shard_map/ppermute | solution.py:24
  497.1 192.4 %reduce-scatter.5.cloned.1.call-start = ((), (), s32[]{:S(2)}) async-start(), calls=%async_computation.13 | async-start | bytes 5750784 | tf_op jit(solution)/shard_map/reduce_scatter | solution.py:560
  545.1 43.1 %collective-permute-start.47 = (bf16[512,1536]{1,0:T(8,128)(2,1)}, bf16[512,1536]{1,0:T(8,128)(2,1)}, u32[]{:S(2)}, u32[]{:S(2)}) collective-permute-start(bf16[512,1536]{1,0:T(8,128)(2,1)} %slice.451), channel_id=1, source_target_pairs={{0,4},{4,0},{1,5},{5,1},{2,6},{6,2},{3,7},{7,3},{8,12},{12,8},{9,1... | collective-permute-start | bytes 4718600 | tf_op jit(solution)/shard_map/ppermute | solution.py:24
  572.8 104.0 %collective-permute-start.26 = (bf16[2,64,1536]{2,1,0:T(8,128)(2,1)}, bf16[2,64,1536]{2,1,0:T(8,128)(2,1)}, u32[]{:S(2)}, u32[]{:S(2)}) collective-permute-start(bf16[2,64,1536]{2,1,0:T(8,128)(2,1)} %pad_maximum_fusion.21), channel_id=1, source_target_pairs={{0,2},{2,0},{1,3},{3,1},{4,6},{6,4},{5,7},{7,5},{8,10},{10,8},{9,1... | collective-permute-start | bytes 1179656 | tf_op jit(solution)/shard_map/ppermute | solution.py:24
  596.3 65.3 %all-to-all-start.5 = ((bf16[4,48,384]{2,1,0:T(8,128)(2,1)}), bf16[4,48,384]{2,1,0:T(8,128)(2,1)}, u32[]{:S(2)}, u32[]{:S(2)}) async-start(bf16[4,48,384]{2,1,0:T(8,128)(2,1)} %bitcast.297), calls=%async_computation.7 | async-start | bytes 294912 | tf_op jit(solution)/shard_map/all_to_all | solution.py:555
  616.1 49.1 %collective-permute-start.51 = (bf16[64,1536]{1,0:T(8,128)(2,1)S(1)}, bf16[64,1536]{1,0:T(8,128)(2,1)S(1)}, u32[]{:S(2)}, u32[]{:S(2)}) collective-permute-start(bf16[64,1536]{1,0:T(8,128)(2,1)S(1)} %get-tuple-element.82), channel_id=1, source_target_pairs={{0,24},{8,16},{16,8},{24,0},{1,25},{9,17},{17,9},{25,1},{2,26},{10... | collective-permute-start | bytes 589832 | tf_op jit(solution)/shard_map/ppermute | solution.py:24
  618.2 47.0 %collective-permute-start.50 = (bf16[64,1536]{1,0:T(8,128)(2,1)S(1)}, bf16[64,1536]{1,0:T(8,128)(2,1)S(1)}, u32[]{:S(2)}, u32[]{:S(2)}) collective-permute-start(bf16[64,1536]{1,0:T(8,128)(2,1)S(1)} %get-tuple-element.83), channel_id=1, source_target_pairs={{0,16},{8,24},{16,0},{24,8},{1,17},{9,25},{17,1},{25,9},{2,18},{10... | collective-permute-start | bytes 589832 | tf_op jit(solution)/shard_map/ppermute | solution.py:24
  618.3 47.0 %collective-permute-start.49 = (bf16[64,1536]{1,0:T(8,128)(2,1)S(1)}, bf16[64,1536]{1,0:T(8,128)(2,1)S(1)}, u32[]{:S(2)}, u32[]{:S(2)}) collective-permute-start(bf16[64,1536]{1,0:T(8,128)(2,1)S(1)} %get-tuple-element.84), channel_id=1, source_target_pairs={{0,8},{8,0},{16,24},{24,16},{1,9},{9,1},{17,25},{25,17},{2,10},{10... | collective-permute-start | bytes 589832 | tf_op jit(solution)/shard_map/ppermute | solution.py:24
  (94 other events, 2173.5 us)
Sparse Core Ops, SparseCore 0:
  29.1 41.7 all-gather.13
  73.1 97.5 all-gather.11
  172.3 76.7 all-gather.15
  255.3 33.7 all-gather.9
  371.9 32.9 reduce-scatter.10
  410.3 57.7 reduce-scatter.8
  497.2 71.2 reduce-scatter.6
  572.2 117.2 reduce-scatter.4

commit v2 on v1

v2 whole, which is shorter than its diff:
```python
import functools

import jax
import jax.numpy as jnp
from jax import lax
from jax.experimental import pallas as pl
from jax.experimental.pallas import tpu as pltpu
from jax.sharding import Mesh, PartitionSpec as P

EPS = 1e-06
LOW = -1e30
BQ = 256
F32 = jnp.float32
BF16 = jnp.bfloat16
VMEM_LIMIT = 56 * 1024 * 1024


def dot(left, right, contract=((1,), (0,)), out=F32):
    return lax.dot_general(left, right, (contract, ((), ())), preferred_element_type=out)


def xor_permute(x, axis, step):
    n = lax.axis_size(axis)
    return lax.ppermute(x, axis, [(i, i ^ step) for i in range(n)])


def pick(stacked, index):
    return lax.dynamic_index_in_dim(stacked, index, 0, keepdims=False)


def xor_plane(x, step):
    n = lax.axis_size("p") * lax.axis_size("q")
    return lax.ppermute(x, ("p", "q"), [(i, i ^ step) for i in range(n)])


def rows_to_plane(x):
    nf = lax.axis_size("p") * lax.axis_size("q")
    f = lax.axis_index(("p", "q"))
    micro, tokens, width = x.shape
    parts = x.reshape(micro, nf, tokens // nf, width).transpose(1, 0, 2, 3)
    return jnp.stack([pick(parts, f)] + [xor_plane(pick(parts, f ^ k), k) for k in range(1, nf)])


def rows_to_layer(got):
    nz = lax.axis_size("z")
    f, z = lax.axis_index(("p", "q")), lax.axis_index("z")
    return [pick(got, f ^ z)] + [xor_permute(pick(got, f ^ z ^ k), "z", k) for k in range(1, nz)]


def rows_from_layer(y):
    nz = lax.axis_size("z")
    micro, rows, width = y.shape
    rp = rows // nz
    return [y[:, :rp]] + [xor_permute(y[:, k * rp:(k + 1) * rp], "z", k) for k in range(1, nz)]


def rows_from_plane(got):
    nf = lax.axis_size("p") * lax.axis_size("q")
    f, z = lax.axis_index(("p", "q")), lax.axis_index("z")
    got = jnp.stack(got)
    back = [pick(got, z ^ f)] + [xor_plane(pick(got, z ^ f ^ k), k) for k in range(1, nf)]
    back = jnp.stack(back)
    return jnp.concatenate([pick(back, f ^ c) for c in range(nf)], axis=1)


def gather_first(x):
    np_ = lax.axis_size("p")
    return [x, xor_permute(x, "q", 1)] + [xor_permute(x, "p", k) for k in range(1, np_)]


def gather_rest(first):
    np_ = lax.axis_size("p")
    x, over_q = first[:2]
    half = x.shape[0] // 2
    if np_ == 2:
        over_p = first[2]
        own = [x, over_q, over_p, [xor_permute(over_q[:half], "p", 1), xor_permute(over_p[half:], "q", 1)]]
    else:
        own = [x, over_q]
        for k in range(1, np_):
            own += [first[1 + k], xor_permute(over_q, "p", k)]
    return own + jax.tree.map(lambda block: xor_permute(block, "core", 1), own)


def gather_plane(x):
    return gather_rest(gather_first(x))


def in_rows(blocks):
    return jnp.concatenate(jax.tree.leaves(blocks), axis=0)


def add_up(*parts):
    return sum(part.astype(F32) for part in parts)


def scatter_core(far, near):
    got = [xor_permute(item, "core", 1) for item in far]
    shape = (2 * lax.axis_size("p"), -1, near[0].shape[-1])
    near = [item.reshape(shape) for item in near]
    got = [item.reshape(shape) for item in got]
    return near, got, both_cores(near, got, shape[0] - 1).astype(BF16)


def both_cores(near, got, number):
    return jnp.concatenate([add_up(one[number], other[number]) for one, other in zip(near, got)], axis=0)


def scatter_diagonal(near, got, last, beside=None):
    np_ = lax.axis_size("p")
    near, got, last = lax.optimization_barrier((near, got, last))
    made = ()
    if np_ == 2:
        half = last.shape[0] // 2
        into_q = xor_permute(last[:half], "p", 1)
        into_p = xor_permute(last[half:], "q", 1)
        if beside is not None:
            into_q, into_p, made = lax.optimization_barrier((into_q, into_p, beside(last)))
        to_q, to_p = both_cores(near, got, 1), both_cores(near, got, 2)
        to_q = jnp.concatenate([add_up(to_q[:half], into_q), to_q[half:]], axis=0).astype(BF16)
        to_p = jnp.concatenate([to_p[:half], add_up(to_p[half:], into_p)], axis=0).astype(BF16)
        own = [side[0][0] if len(side) == 1 else jnp.concatenate([item[0] for item in side]) for side in (near, got)]
        return own, [(to_q, "q"), (to_p, "p")], made
    if beside is not None:
        made = beside(last)
    pair = [both_cores(near, got, 0), both_cores(near, got, 1)]
    for k in range(1, np_):
        for side in range(2):
            item = last if 2 * k + side == 2 * np_ - 1 else both_cores(near, got, 2 * k + side).astype(BF16)
            pair[side] = pair[side] + xor_permute(item, "p", k).astype(F32)
    return [pair[0]], [(pair[1].astype(BF16), "q")], made


def scatter_first(far, near, beside=None):
    return scatter_diagonal(*scatter_core(far, near), beside)


def sent(state):
    return [item for item, _ in state[1]]


def received(state, sends):
    return [xor_permute(item, axis, 1) for item, (_, axis) in zip(sends, state[1])]


def scatter_rest(state):
    return add_up(*state[0], *received(state, sent(state)))


def total_over(axis, x):
    step = 1
    while step < lax.axis_size(axis):
        x = x + xor_permute(x, axis, step)
        step *= 2
    return x


def log_sigmoid(z):
    return jnp.minimum(z, 0.0) - jnp.log(1.0 + jnp.exp(-jnp.abs(z)))


def window_of(i, bq, window):
    first = max(0, i * bq - window)
    return first, (i + 1) * bq - first


def pieces(members, rows, chunk):
    per = rows // chunk
    return [(j * per + k, j, k * chunk) for j in range(members) for k in range(per)]


def natural_rows(table, number, chunk):
    return pl.ds(pl.multiple_of(table[number] * chunk, chunk), chunk)


def spread_rows(table, source, far_ref, near_ref, chunk):
    half = near_ref.shape[0]
    for number, j, at in pieces(2 * half, near_ref.shape[1], chunk):
        target = near_ref if j < half else far_ref
        target[j % half, at:at + chunk, :] = source[natural_rows(table, number, chunk), :]


def attend_kernel(heads, depth, chunk, members, table, *refs):
    x_refs, refs = refs[:members], refs[members:]
    w_ref, bias_ref, begin_ref = refs[:3]
    h_ref, qkv_ref, g_ref, z_ref, a_ref, total_ref, cumul_ref, b_ref, gain_ref = refs[3:12]
    ka, va, rows, part = refs[12:]
    total = total_ref.shape[0]
    columns = heads * depth
    bq = min(BQ, total)
    window = total // 2
    scale = jnp.asarray(depth ** -0.5, BF16)
    for number, j, at in pieces(members, x_refs[0].shape[0], chunk):
        part[natural_rows(table, number, chunk), :] = x_refs[j][at:at + chunk, :]
    gains = jnp.transpose(w_ref[:, 0:128].astype(F32))[2 * heads:2 * heads + 2, :]
    gain_ref[...] = jnp.concatenate([gains, jnp.zeros((6, gains.shape[1]), F32)], axis=0)
    gain = gains[0:1, :]
    lower = (
        lax.broadcasted_iota(jnp.int32, (bq, bq), 0) >= lax.broadcasted_iota(jnp.int32, (bq, bq), 1)
    ).astype(F32).astype(BF16)
    carry = jnp.zeros((1, 128), F32)
    for i in range(total // bq):
        here = slice(i * bq, (i + 1) * bq)
        values = part[here, :].astype(F32)
        values = values * lax.rsqrt(jnp.mean(values * values, axis=1, keepdims=True) + EPS) * gain
        h_ref[here, :] = values.astype(BF16)
        tile = dot(h_ref[here, :], w_ref[...])
        logit = tile[:, 0:128] + bias_ref[...]
        z_ref[here, :] = logit
        cumul = dot(lower, log_sigmoid(logit).astype(BF16)) + carry
        cumul_ref[here, :] = cumul
        carry = cumul[bq - 1:bq, :]
        qkv_ref[here, :] = tile[:, 128:128 + 3 * columns].astype(BF16)
        g_ref[here, :] = tile[:, 128 + 3 * columns:]
        for h in range(heads):
            lo = 128 + columns + h * depth
            ka[h, here, :] = tile[:, lo:lo + depth].astype(BF16)
            lo += columns
            va[h, here, 0:depth] = tile[:, lo:lo + depth].astype(BF16)
            va[h, here, depth:] = jnp.ones((bq, 128 - depth), BF16)
    rows[...] = jnp.transpose(cumul_ref[...])
    lane = lax.broadcasted_iota(jnp.int32, (bq, 128), 1)
    for i in range(total // bq):
        first, span = window_of(i, bq, window)
        here = slice(i * bq, (i + 1) * bq)
        place = i * bq + lax.broadcasted_iota(jnp.int32, (bq, span), 0)
        other = first + lax.broadcasted_iota(jnp.int32, (bq, span), 1)
        mask = jnp.where((other <= place) & (other >= begin_ref[here, :]), 0.0, LOW)
        totals = jnp.zeros((bq, 128), F32)
        for h in range(heads):
            query = qkv_ref[here, h * depth:(h + 1) * depth] * scale
            score = dot(query, ka[h, first:first + span, :], ((1,), (1,)))
            score = score - rows[h:h + 1, first:first + span] + mask
            peak = jnp.max(score, axis=1, keepdims=True)
            weight = jnp.exp(score - peak)
            both = dot(weight.astype(BF16), va[h, first:first + span, :])
            a_ref[here, h * depth:(h + 1) * depth] = both[:, 0:depth] / both[:, depth:2 * depth]
            totals = jnp.where(lane == h, peak + jnp.log(both[:, depth:depth + 1]), totals)
        total_ref[here, :] = totals
        part[here, 0:columns] = (a_ref[here, :] * jax.nn.sigmoid(g_ref[here, :])).astype(BF16)
    for number, j, at in pieces(members, b_ref.shape[1], chunk):
        b_ref[j, at:at + chunk, :] = part[natural_rows(table, number, chunk), 0:columns]


def attend_back_kernel(heads, depth, chunk, members, streams, table, *refs):
    x_refs, refs = refs[:members], refs[members:]
    extra = members * max(0, streams - 1)
    other_refs, gated_refs, refs = refs[:extra], refs[extra:extra + streams], refs[extra + streams:]
    w_ref, o_ref, qkv_ref, g_ref, z_ref, a_ref, total_ref, cumul_ref, begin_ref = refs[:9]
    right_ref, far_ref, near_ref, dbias_ref = refs[9:13]
    part, below_grad, qa, ka, va, da, dkn, dvn, rows, deltas, dcumul = refs[-11:]
    if streams:
        out_grad = jnp.zeros(refs[13].shape, F32)
        for number, ref in enumerate(x_refs + other_refs):
            out_grad = out_grad + dot(gated_refs[number // members][number % members], ref[...], ((0,), (0,)))
        refs[13][...] = out_grad.astype(BF16)
    total = total_ref.shape[0]
    columns = heads * depth
    bq = min(BQ, total)
    window = total // 2
    scale = jnp.asarray(depth ** -0.5, BF16)
    lane = lax.broadcasted_iota(jnp.int32, (bq, 128), 1)
    per = x_refs[0].shape[0] // chunk
    for j in range(members):
        grad = dot(x_refs[j][...], o_ref[...], ((1,), (1,)))
        for k in range(per):
            below_grad[natural_rows(table, j * per + k, chunk), :] = grad[k * chunk:(k + 1) * chunk, :]
    dkn[...] = jnp.zeros_like(dkn)
    dvn[...] = jnp.zeros_like(dvn)
    for i in range(total // bq):
        here = slice(i * bq, (i + 1) * bq)
        grad = below_grad[here, :]
        opened = jax.nn.sigmoid(g_ref[here, :])
        attended = a_ref[here, :]
        below = (grad * opened).astype(BF16)
        right_ref[here, 128 + 3 * columns:] = (grad * attended * opened * (1.0 - opened)).astype(BF16)
        product = below.astype(F32) * attended
        delta = jnp.zeros((bq, 128), F32)
        for h in range(heads):
            da[h, here, :] = below[:, h * depth:(h + 1) * depth]
            delta = jnp.where(
                lane == h, jnp.sum(product[:, h * depth:(h + 1) * depth], axis=1, keepdims=True), delta
            )
            qa[h, here, 0:depth] = qkv_ref[here, h * depth:(h + 1) * depth] * scale
            qa[h, here, depth:] = jnp.ones((bq, 128 - depth), BF16)
            lo = columns + h * depth
            ka[h, here, 0:depth] = qkv_ref[here, lo:lo + depth]
            ka[h, here, depth:] = jnp.ones((bq, 128 - depth), BF16)
            lo += columns
            va[h, here, :] = qkv_ref[here, lo:lo + depth]
        dcumul[here, :] = delta
    deltas[...] = jnp.transpose(dcumul[...])
    rows[...] = jnp.transpose(total_ref[...])
    dcumul[...] = jnp.zeros_like(dcumul)
    for i in range(total // bq):
        first, span = window_of(i, bq, window)
        here, there = slice(i * bq, (i + 1) * bq), slice(first, first + span)
        place = i * bq + lax.broadcasted_iota(jnp.int32, (span, bq), 1)
        other = first + lax.broadcasted_iota(jnp.int32, (span, bq), 0)
        mask = jnp.where((other <= place) & (other >= begin_ref[:, here]), 0.0, LOW)
        for h in range(heads):
            query, below = qa[h, here, :], da[h, here, :]
            score = dot(ka[h, there, 0:depth], query[:, 0:depth], ((1,), (1,)))
            score = score - rows[h:h + 1, here] - cumul_ref[there, h:h + 1] + mask
            weight = jnp.exp(score)
            weight_grad = dot(va[h, there, :], below, ((1,), (1,))) - deltas[h:h + 1, here]
            score_grad = (weight * weight_grad).astype(BF16)
            dvn[h, there, :] += dot(weight.astype(BF16), below)
            dkn[h, there, :] += dot(score_grad, query)
            dq = dot(score_grad, ka[h, there, :], ((0,), (0,)))
            right_ref[here, 128 + h * depth:128 + (h + 1) * depth] = (dq[:, 0:depth] * depth ** -0.5).astype(BF16)
            mine = (lane == h) | (lane == h + heads)
            dcumul[here, :] += jnp.where(mine, dq[:, depth:depth + 1], 0.0)
    upper = (
        lax.broadcasted_iota(jnp.int32, (bq, bq), 0) <= lax.broadcasted_iota(jnp.int32, (bq, bq), 1)
    ).astype(F32)
    carry = jnp.zeros((1, 128), F32)
    sums = jnp.zeros((1, 128), F32)
    for i in reversed(range(total // bq)):
        here = slice(i * bq, (i + 1) * bq)
        change = dcumul[here, :]
        for h in range(heads):
            lo = 128 + columns + h * depth
            right_ref[here, lo:lo + depth] = dkn[h, here, 0:depth].astype(BF16)
            lo += columns
            right_ref[here, lo:lo + depth] = dvn[h, here, :].astype(BF16)
            mine = (lane == h) | (lane == h + heads)
            change = change - jnp.where(mine, dkn[h, here, depth:depth + 1], 0.0)
        summed = carry + jnp.dot(upper, change, precision=lax.Precision.HIGHEST, preferred_element_type=F32)
        carry = summed[0:1, :]
        grad = summed * jax.nn.sigmoid(-z_ref[here, :])
        sums = sums + jnp.sum(grad, axis=0, keepdims=True)
        high = grad.astype(BF16).astype(F32)
        pair = jnp.where(lane < heads, high, jnp.where(lane < 2 * heads, grad - high, 0.0))
        right_ref[here, 0:128] = pair.astype(BF16)
        part[here, :] = dot(right_ref[here, :], w_ref[...], ((1,), (1,))).astype(BF16)
    dbias_ref[...] = jnp.broadcast_to(sums, dbias_ref.shape)
    spread_rows(table, part, far_ref, near_ref, chunk)


def one_stream(blocks, m, streams):
    arrays, specs = [], []
    for block in blocks:
        array, place = (block[m], 0) if isinstance(block, list) else (block, m)
        rows, width = (array.shape[0] if isinstance(block, list) else array.shape[0] // streams), array.shape[1]
        arrays.append(array)
        specs.append(pl.BlockSpec((rows, width), lambda i, t, place=place: (place, 0), pipeline_mode=pl.Buffered(1)))
    return arrays, specs


def fixed(array):
    return pl.BlockSpec(array.shape, lambda i, t: (0,) * array.ndim, pipeline_mode=pl.Buffered(1))


def attend(table, blocks, m, streams, weights, bias, begin, heads, depth, chunk):
    arrays, specs = one_stream(blocks, m, streams)
    members, (rows, width) = len(arrays), specs[0].block_shape
    total = begin.shape[0]
    columns = heads * depth
    begin = begin[:, None]
    outs = [
        ((total, width), BF16), ((total, 3 * columns), BF16), ((total, columns), F32), ((total, 128), F32),
        ((total, columns), F32), ((total, 128), F32), ((total, 128), F32), ((members, rows, columns), BF16),
        ((8, width), F32),
    ]
    out_shape = [jax.ShapeDtypeStruct(shape, kind) for shape, kind in outs]
    return pl.pallas_call(
        functools.partial(attend_kernel, heads, depth, chunk, members),
        grid_spec=pltpu.PrefetchScalarGridSpec(
            num_scalar_prefetch=1,
            grid=(1,),
            in_specs=specs + [fixed(weights), fixed(bias), fixed(begin)],
            out_specs=[fixed(item) for item in out_shape],
            scratch_shapes=[
                pltpu.VMEM((heads, total, depth), BF16),
                pltpu.VMEM((heads, total, 128), BF16),
                pltpu.VMEM((128, total), F32),
                pltpu.VMEM((total, width), BF16),
            ],
        ),
        out_shape=out_shape,
        compiler_params=pltpu.CompilerParams(vmem_limit_bytes=VMEM_LIMIT),
        cost_estimate=pl.CostEstimate(flops=14 * 10 ** 9, bytes_accessed=10 ** 7, transcendentals=0),
        name="attend",
    )(table, *arrays, weights, bias, begin)


def attend_back(table, blocks, m, streams, weights, out_w, kept, begin, gated, heads, depth, chunk):
    arrays, specs = one_stream(blocks, m, streams)
    members, (rows, width) = len(arrays), specs[0].block_shape
    total = begin.shape[0]
    columns = heads * depth
    begin = begin[None, :]
    gated = [] if gated is None else gated
    for other in range(1, len(gated)):
        other_arrays, other_specs = one_stream(blocks, other, streams)
        arrays, specs = arrays + other_arrays, specs + other_specs
    outs = [
        ((total, 128 + 4 * columns), BF16), ((members // 2, rows, width), BF16), ((members // 2, rows, width), BF16),
        ((8, 128), F32),
    ] + [((columns, width), BF16)] * (len(gated) > 0)
    out_shape = [jax.ShapeDtypeStruct(shape, kind) for shape, kind in outs]
    return pl.pallas_call(
        functools.partial(attend_back_kernel, heads, depth, chunk, members, len(gated)),
        grid_spec=pltpu.PrefetchScalarGridSpec(
            num_scalar_prefetch=1,
            grid=(1,),
            in_specs=specs + [fixed(item) for item in (*gated, weights, out_w, *kept, begin)],
            out_specs=[fixed(item) for item in out_shape],
            scratch_shapes=[
                pltpu.VMEM((total, width), BF16),
                pltpu.VMEM((total, columns), F32),
                pltpu.VMEM((heads, total, 128), BF16),
                pltpu.VMEM((heads, total, 128), BF16),
                pltpu.VMEM((heads, total, depth), BF16),
                pltpu.VMEM((heads, total, depth), BF16),
                pltpu.VMEM((heads, total, 128), F32),
                pltpu.VMEM((heads, total, depth), F32),
                pltpu.VMEM((128, total), F32),
                pltpu.VMEM((128, total), F32),
                pltpu.VMEM((total, 128), F32),
            ],
        ),
        out_shape=out_shape,
        compiler_params=pltpu.CompilerParams(vmem_limit_bytes=VMEM_LIMIT),
        cost_estimate=pl.CostEstimate(flops=20 * 10 ** 9, bytes_accessed=10 ** 7, transcendentals=0),
        name="attend_back",
    )(table, *arrays, *gated, weights, out_w, *kept, begin)


def out_kernel(b_ref, o_ref, far_ref, near_ref):
    half = near_ref.shape[0]
    for j in range(2 * half):
        target = near_ref if j < half else far_ref
        target[j % half] = dot(b_ref[j], o_ref[...]).astype(BF16)


def out_product(gated, weights):
    members, rows, _ = gated.shape
    shape = jax.ShapeDtypeStruct((members // 2, rows, weights.shape[1]), BF16)
    return pl.pallas_call(
        out_kernel,
        out_shape=[shape, shape],
        compiler_params=pltpu.CompilerParams(vmem_limit_bytes=VMEM_LIMIT),
        name="out_product",
    )(gated, weights)


def ffn_kernel(h_ref, e_ref, w_ref, d_ref, *refs):
    m_ref, g_ref, part_ref = refs[-3:]
    down = d_ref[...].reshape(-1, d_ref.shape[-1])
    share = down.shape[0]
    pre = dot(h_ref[...], w_ref[...])
    gate, up = pre[:, :share], pre[:, share:]
    grad = dot(e_ref[...], down, ((1,), (1,)))
    opened = jax.nn.sigmoid(gate)
    silu = gate * opened
    m_ref[...] = (silu * up).astype(BF16)
    g_ref[:, :share] = (grad * up * (opened * (1.0 + gate * (1.0 - opened)))).astype(BF16)
    g_ref[:, share:] = (grad * silu).astype(BF16)
    part_ref[...] = dot(g_ref[...], w_ref[...], ((1,), (1,))).astype(BF16)


def ffn(normed, upstream, weights, down, unit, first, count, into):
    rows, width = normed.shape
    share = down.shape[0] * unit

    def blocks(lanes, shift):
        return pl.BlockSpec((BQ, lanes), lambda i: (i + shift, 0))

    def fixed(shape):
        return pl.BlockSpec(shape, lambda i: (0,) * len(shape), pipeline_mode=pl.Buffered(1))

    kept = [] if into is None else list(into)
    return pl.pallas_call(
        ffn_kernel,
        grid=(count,),
        in_specs=[blocks(width, first), blocks(width, first), fixed(weights.shape), fixed((down.shape[0], unit, width))]
        + [pl.BlockSpec(memory_space=pl.ANY)] * len(kept),
        out_specs=[blocks(share, first), blocks(2 * share, first), blocks(width, 0)],
        out_shape=[
            jax.ShapeDtypeStruct((rows, share), BF16),
            jax.ShapeDtypeStruct((rows, 2 * share), BF16),
            jax.ShapeDtypeStruct((count * BQ, width), BF16),
        ],
        input_output_aliases={4 + i: i for i in range(len(kept))},
        compiler_params=pltpu.CompilerParams(vmem_limit_bytes=VMEM_LIMIT),
        cost_estimate=pl.CostEstimate(
            flops=10 * count * BQ * width * share, bytes_accessed=count * BQ * width * 8, transcendentals=0
        ),
        name="ffn",
    )(normed, upstream, weights, down, *kept)


def layout(body, shapes, kind, *arrays):
    kinds = kind if isinstance(kind, list) else [kind] * len(shapes)
    out_shape = [jax.ShapeDtypeStruct(shape, own) for shape, own in zip(shapes, kinds)]
    return pl.pallas_call(body, out_shape=out_shape, name="layout")(*arrays)


def block_columns(block, columns, limit):
    return min(block * columns, limit), max(0, min((block + 1) * columns, limit) - min(block * columns, limit))


def pack_heads(forget, weights, nf, columns):
    slab, width = weights[0].shape
    plane = 2 * nf

    def body(f_ref, *refs):
        out = refs[-1]
        for t in range(plane):
            out[t, :, 0:128] = f_ref[:, t * 128:(t + 1) * 128]
            first, count = block_columns(t % nf * 2 + t // nf, columns, width)
            for number, ref in enumerate(refs[:-1]):
                lo = 128 + number * columns
                if count < columns:
                    out[t, :, lo:lo + columns] = jnp.zeros((slab, columns), BF16)
                if count:
                    out[t, :, lo:lo + count] = ref[:, first:first + count]

    return layout(body, [(plane, slab, 128 + 4 * columns)], BF16, forget, *weights)[0]


def unpack_heads(grads, weights, nf, columns):
    plane, slab, _ = grads.shape
    width = weights[0].shape[1]

    def body(x_ref, *refs):
        sums = jnp.zeros((slab, 1), F32)
        for number in range(4):
            weight, out = refs[number], refs[4 + number]
            for t in range(plane):
                first, count = block_columns(t % nf * 2 + t // nf, columns, width)
                lo = 128 + number * columns
                if count:
                    out[:, first:first + count] = x_ref[t, :, lo:lo + count].astype(F32)
            sums = sums + jnp.sum(weight[...].astype(F32) * out[...], axis=1, keepdims=True)
        refs[8][...] = sums

    return layout(body, [(slab, width)] * 4 + [(slab, 1)], F32, grads, *weights)


def pack_hidden(gate, up, nz, plane):
    slab, hidden = gate.shape
    unit = hidden // (nz * plane)

    def body(gate_ref, up_ref, out):
        for number, ref in enumerate((gate_ref, up_ref)):
            for t in range(plane):
                for z in range(nz):
                    lo = (number * nz + z) * unit
                    at = (z * plane + t) * unit
                    out[t, :, lo:lo + unit] = ref[:, at:at + unit]

    return layout(body, [(plane, slab, 2 * nz * unit)], BF16, gate, up)[0]


def unpack_hidden(grads, weights, nz):
    plane, slab, both = grads.shape
    unit = both // (2 * nz)

    def body(x_ref, *refs):
        sums = jnp.zeros((slab, 1), F32)
        for number in range(2):
            weight, out = refs[number], refs[2 + number]
            for t in range(plane):
                for z in range(nz):
                    lo = (number * nz + z) * unit
                    at = (z * plane + t) * unit
                    out[:, at:at + unit] = x_ref[t, :, lo:lo + unit].astype(F32)
            sums = sums + jnp.sum(weight[...].astype(F32) * out[...], axis=1, keepdims=True)
        refs[4][...] = sums

    return layout(body, [(slab, plane * nz * unit)] * 2 + [(slab, 1)], F32, grads, *weights)


def doc_begins(lengths_row, total):
    ends = jnp.cumsum(lengths_row)
    begins = ends - lengths_row
    place = jnp.arange(total, dtype=jnp.int32)
    inside = (place[:, None] >= begins[None, :]) & (place[:, None] < ends[None, :])
    return jnp.sum(jnp.where(inside, begins[None, :], 0), axis=1)


def all_to_all(x, axes):
    return lax.all_to_all(x, axes, split_axis=0, concat_axis=0, tiled=True)


def scatter_layers(grad):
    return lax.psum_scatter(grad, "z", scatter_dimension=0, tiled=True)


def join_grads(grad, down, nz):
    lanes, width = grad.shape[1], down.shape[1]
    grad, down = grad.reshape(nz, -1, lanes), down.reshape(nz, -1, width)
    parts = [grad] + [down[:, :, i * lanes:(i + 1) * lanes] for i in range(width // lanes)]
    rest = width % lanes
    if rest:
        count = lanes // rest
        rows = down.shape[1] // count
        over = down[:, :, width - rest:].reshape(nz, count, rows, rest)
        parts.append(jnp.concatenate([over[:, i] for i in range(count)], axis=2))
    return jnp.concatenate(parts, axis=1).reshape(-1, lanes)


def part_grads(joined, slabs, rows, width):
    lanes = joined.shape[1]
    grad, joined = joined[:slabs], joined[slabs:]
    whole = width // lanes
    parts = [joined[i * rows:(i + 1) * rows] for i in range(whole)]
    rest = width % lanes
    if rest:
        over = joined[whole * rows:]
        parts.append(jnp.concatenate([over[:, i * rest:(i + 1) * rest] for i in range(lanes // rest)], axis=0))
    return grad, jnp.concatenate(parts, axis=1)


def tie(*values):
    return lax.optimization_barrier(values)


def per_device(
    inputs, cotangent, lengths, deal, norm1_gain, w_query, w_key, w_value, w_outgate, w_out,
    forget_weight, forget_bias, norm2_gain, w_gate, w_up, w_down,
):
    nz, np_, nq = lax.axis_size("z"), lax.axis_size("p"), lax.axis_size("q")
    z, core, f = lax.axis_index("z"), lax.axis_index("core"), lax.axis_index(("p", "q"))
    nf = np_ * nq
    n_ctx = 2 * nz
    plane = 2 * nf
    devices = nz * plane
    everywhere, members = ("z", "core", "p", "q"), ("core", "p", "q")
    micro, _, tokens, width = inputs.shape
    heads = forget_bias.shape[0]
    depth = width // heads
    own_heads = -(-heads // plane)
    columns = own_heads * depth
    spare_heads = own_heads * plane - heads
    total = tokens * n_ctx
    chunk = tokens // nf
    block = tokens // 2
    hidden = w_gate.shape[1]
    slab = w_query.shape[0]
    unit = hidden // devices
    share = nz * unit
    own_block = f * 2 + core
    aligned = spare_heads == 0 and columns == nf * slab

    member_block = [t % nf * 2 + t // nf for t in range(plane)]
    head_of = jnp.arange(heads, dtype=jnp.int32)[:, None]
    lane_of = jnp.arange(plane * 128, dtype=jnp.int32)[None, :]
    lane_head = jnp.asarray(member_block, jnp.int32)[lane_of // 128] * own_heads + lane_of % 128 % own_heads
    select = ((lane_head == head_of) & (lane_of % 128 < 2 * own_heads)).astype(BF16)
    first_lanes = dot(forget_weight, select, out=BF16)
    for number, gain in enumerate((norm1_gain, norm2_gain)):
        first_lanes = jnp.where(lane_of % 128 == 2 * own_heads + number, gain[:, None], first_lanes)
    packed = pack_heads(first_lanes, (w_query, w_key, w_value, w_outgate), nf, columns)
    own = rows_to_layer(rows_to_plane(inputs[:, 0]))
    packed, own[1] = tie(packed, own[1])
    packed = all_to_all(packed, members)
    if aligned:
        out_w = jnp.stack([w_out] + [xor_permute(w_out, "z", k) for k in range(1, nz)])
        out_w = jnp.stack([pick(out_w, z ^ c) for c in range(nz)])
    else:
        out_w = jnp.pad(lax.all_gather(w_out, everywhere, axis=0, tiled=True), ((0, spare_heads * depth), (0, 0)))
        out_w = lax.dynamic_slice_in_dim(out_w, own_block * columns, columns, 0)
    own = jnp.concatenate(own, axis=1).reshape(-1, width)
    packed, own, out_w = tie(packed, own, out_w)
    packed = lax.all_gather(packed, "z", axis=0).reshape(width, -1)
    gathered = gather_first(own)
    ffn_send, gathered = tie(pack_hidden(w_gate, w_up, nz, plane), gathered)
    gathered = gather_rest(gathered)
    if aligned:
        out_w = all_to_all(out_w, ("p", "q")).reshape(columns, width)
    ffn_w = all_to_all(ffn_send, members)
    out_w, ffn_w, gathered, cotangent = tie(out_w, ffn_w, gathered, cotangent)
    upstream_own = rows_to_plane(cotangent[:, 0])
    packed, upstream_own = tie(packed, upstream_own)
    upstream_own = jnp.concatenate(rows_to_layer(upstream_own), axis=1).reshape(-1, width)

    lengths_own = lax.ppermute(
        lengths[:, 0], everywhere,
        [
            (((f_to * 2 + c) * nf) + z_to, ((z_to * 2 + c) * nf) + f_to)
            for z_to in range(nz) for c in range(2) for f_to in range(nf)
        ],
    )
    begins = [doc_begins(lengths_own[m], total) for m in range(micro)]
    number = jnp.arange(total // chunk, dtype=jnp.int32)
    from_core = core ^ (number // (nf * nz))
    from_f = f ^ (number // nz % nf)
    from_z = z ^ (number % nz)
    inside = from_f * chunk

    def natural_table(deal_row):
        dealt = jnp.take(deal_row, from_z * 2 + from_core)
        start = jnp.where(inside < block, dealt, 2 * n_ctx - 1 - dealt) * block + inside % block
        return (start // chunk).astype(jnp.int32)

    tables = [natural_table(deal[m]) for m in range(micro)]
    all_bias = jnp.pad(forget_bias, (0, spare_heads))
    own_bias = lax.dynamic_slice_in_dim(all_bias, own_block * own_heads, own_heads, 0)[None]
    bias_row = jnp.concatenate([own_bias, own_bias, jnp.zeros((1, 128 - 2 * own_heads), F32)], axis=1)

    def attend_stream(m, table):
        return attend(table, gathered, m, micro, packed, bias_row, begins[m], own_heads, depth, chunk)

    stream = own.astype(F32)
    attended = [attend_stream(0, tables[0])]
    gains = attended[0][8]
    gated = [attended[0][7]]
    parts = [out_product(gated[0], out_w)]
    table, upstream_own, gains, ffn_w, w_down = tie(tables[1], upstream_own, gains, ffn_w, w_down)
    ffn_w = lax.all_gather(ffn_w, "z", axis=0).reshape(width, 2 * share)
    down_w = lax.all_gather(w_down, "z", axis=0)
    attended.append(attend_stream(1, table))
    upstream = gather_first(upstream_own)
    last_gated, upstream = tie(attended[1][7], upstream)
    gated.append(last_gated)
    parts.append(out_product(gated[1], out_w))
    upstream = in_rows(gather_rest(upstream))
    gain_one, gain_two = gains[0:1], gains[1:2]
    middle = stream + scatter_rest(scatter_first([item[0] for item in parts], [item[1] for item in parts]))
    norm_two = lax.rsqrt(jnp.mean(middle * middle, axis=-1, keepdims=True) + EPS)
    normed_two = in_rows(gather_plane((middle * norm_two * gain_two).astype(BF16)))

    half_blocks = normed_two.shape[0] // BQ // 2
    weights = (normed_two, upstream, ffn_w, down_w, unit)
    activ, ffn_grad, far = ffn(*weights, half_blocks, half_blocks, None)
    activ, ffn_grad, near = ffn(*weights, 0, half_blocks, (activ, ffn_grad))
    def grad_of_ffn(hold):
        kept, _ = tie(normed_two, hold)
        return dot(kept, ffn_grad, ((0,), (0,)), BF16)

    state = scatter_first([far[None]], [near[None]], grad_of_ffn)
    grad_ffn_w = state[2]
    sends, held = tie(sent(state), activ)
    grad_down = dot(held, upstream, ((0,), (0,)), BF16)
    arrived, grad_ffn = tie(received(state, sends), join_grads(grad_ffn_w, grad_down, nz))
    grad_ffn = scatter_layers(grad_ffn)
    normed_two_grad = add_up(*state[0], *arrived)

    unit_two = middle * norm_two
    scaled_two = normed_two_grad * gain_two
    middle_grad = upstream_own.astype(F32) + norm_two * (
        scaled_two - unit_two * jnp.mean(scaled_two * unit_two, axis=-1, keepdims=True)
    )
    branch_own, held = tie(middle_grad.astype(BF16), activ)
    half = activ.shape[0] // 2
    down_rows = down_w.reshape(share, width)
    part_out = [dot(item, down_rows, out=BF16)[None] for item in (held[half:], held[:half])]
    branch_grad, part_out = tie(gather_first(branch_own), part_out)
    result = scatter_core(part_out[:1], part_out[1:])
    branch_grad = gather_rest(branch_grad)

    def back_stream(m, table, gated):
        return attend_back(
            table, branch_grad, m, micro, packed, out_w, attended[m][1:7], begins[m], gated, own_heads, depth, chunk
        )

    def first_back(hold):
        table, _ = tie(tables[0], hold)
        return back_stream(0, table, gated)

    result = scatter_diagonal(*result, first_back)
    backs = [result[2]]
    grad_packed = dot(attended[0][0], backs[0][0], ((0,), (0,)))
    grad_out = backs[0][4]
    if aligned:
        grad_out = all_to_all(grad_out.reshape(nf, slab, width), ("p", "q"))
    if aligned:
        grad_out = scatter_layers(grad_out.reshape(nf * slab, width))
    table, grad_packed, sends, grad_ffn = tie(tables[1], grad_packed, sent(result), grad_ffn)
    grad_ffn_w, grad_down = part_grads(grad_ffn, plane * slab, unit, width)
    arrived, last_back = tie(received(result, sends), back_stream(1, table, None))
    backs.append(last_back)
    result_base, far = tie(result[0], backs[1][1])
    result = (middle + add_up(*result_base, *arrived)).astype(BF16)
    output = rows_from_layer(result.reshape(micro, -1, width))
    bias_sum = sum(item[3][0] for item in backs)
    bias_all = lax.dynamic_update_slice_in_dim(
        jnp.zeros((own_heads * plane,), F32), bias_sum[:own_heads], own_block * own_heads, 0
    )[:heads]

    def grad_of_packed(hold):
        right, _ = tie(backs[1][0], hold)
        grad = (grad_packed + dot(attended[1][0], right, ((0,), (0,)))).astype(BF16)
        return grad, output, total_over("p", total_over("core", bias_all)), grad_down, grad_out

    state = scatter_first([backs[0][1], far], [item[2] for item in backs], grad_of_packed)
    grad_packed, output, bias_all, grad_down, grad_out = state[2]
    grad_packed = scatter_layers(grad_packed)
    sends, grad_ffn_w = tie(sent(state), grad_ffn_w)
    grad_ffn_w = all_to_all(grad_ffn_w.reshape(plane, slab, 2 * share), members)
    arrived, bias_all = tie(received(state, sends), total_over("q", bias_all))
    normed_grad = add_up(*state[0], *arrived)
    norm_one = lax.rsqrt(jnp.mean(stream * stream, axis=-1, keepdims=True) + EPS)
    unit_one = stream * norm_one
    scaled_one = normed_grad * gain_one
    stream_grad = middle_grad + norm_one * (
        scaled_one - unit_one * jnp.mean(scaled_one * unit_one, axis=-1, keepdims=True)
    )
    stream_grad, bias_all = tie(stream_grad.astype(BF16), bias_all)
    input_grad = rows_from_layer(stream_grad.reshape(micro, -1, width))
    input_grad, grad_packed, grad_ffn_w = tie(input_grad, grad_packed, grad_ffn_w)
    grad_packed = all_to_all(grad_packed.reshape(plane, slab, -1), members)
    grad_bias = total_over("z", bias_all)
    returned = rows_from_plane([jnp.concatenate(pair, axis=0) for pair in zip(output, input_grad)])
    output, input_grad = returned[:micro], returned[micro:].astype(F32)

    if not aligned:
        spread = jnp.zeros((own_heads * depth * plane, width), BF16)
        spread = lax.dynamic_update_slice_in_dim(spread, grad_out, own_block * columns, 0)
        grad_out = lax.psum_scatter(spread[:width], everywhere, scatter_dimension=0, tiled=True)
    grad_out = grad_out.astype(F32)
    grad_down = grad_down.astype(F32)
    grad_gate, grad_up, sums_two = unpack_hidden(grad_ffn_w, (w_gate, w_up), nz)
    grad_query, grad_key, grad_value, grad_outgate, sums_one = unpack_heads(
        grad_packed, (w_query, w_key, w_value, w_outgate), nf, columns
    )
    grad_forget = lax.dot_general(
        grad_packed[:, :, :128], select.reshape(heads, plane, 128), (((0, 2), (1, 2)), ((), ())),
        preferred_element_type=F32,
    )
    sums_one = sums_one[:, 0] + jnp.sum(forget_weight.astype(F32) * grad_forget, axis=1)
    grad_gain_one = sums_one / norm1_gain.astype(F32)
    grad_gain_two = sums_two[:, 0] / norm2_gain.astype(F32)
    return (
        output[:, None], input_grad[:, None], grad_gain_one, grad_query, grad_key, grad_value, grad_outgate,
        grad_out, grad_forget, grad_bias, grad_gain_two, grad_gate, grad_up, grad_down,
    )


def solution(mesh):
    n_ctx, n_fsdp = mesh.shape["ctx"], mesh.shape["fsdp"]
    fine = Mesh(mesh.devices.reshape(n_ctx // 2, 2, n_fsdp // 2, 2), ("z", "core", "p", "q"))
    ctx, fsdp, every = ("z", "core"), ("p", "q"), ("z", "core", "p", "q")
    rows = P(None, fsdp, ctx, None)
    vector, matrix = P(every), P(every, None)
    return jax.shard_map(
        per_device,
        mesh=fine,
        in_specs=(
            rows, rows, P(None, fsdp, None), P(), vector, matrix, matrix, matrix, matrix, matrix, matrix, P(),
            vector, matrix, matrix, matrix,
        ),
        out_specs=(
            rows, rows, vector, matrix, matrix, matrix, matrix, matrix, matrix, P(), vector, matrix, matrix, matrix,
        ),
        check_vma=False,
    )
```

time: 719 us -> 592 us (0.82)
  blocking collectives: 147 us -> 0 us
  Pallas kernels: 30.2 us -> 119 us
  matrix products: 91 us -> 37 us
  local copies, waits for them, and re-layouts: 86.8 us -> 41.5 us
  starting transfers between devices: 70.9 us -> 105 us
  waiting for transfers between devices: 233 us -> 213 us
  other arithmetic: 39.1 us -> 55.6 us
    pallas_call x2 -> x12, Pallas kernels: 30.2 us -> 119 us  [the longest x2 46.1 us: attend_back(): pl.pallas_call(functools.partial(attend_back_kernel, heads, depth, chunk,...]
    all_gather x1 -> x0, blocking collectives: 73.3 us -> none  [per_device(): lax.all_gather(jnp.stack([norm1_gain, norm2_gain]), everywhere, axis=0)]
    dot_general x13 -> x7, matrix products: 91 us -> 35.3 us  [dot(): lax.dot_general(left, right, (contract, ((), ())), preferred_element_type...]
    psum x1 -> x0, blocking collectives: 39.9 us -> none  [per_device(): lax.psum(jnp.stack([gain_one_sum, gain_two_sum, bias_sum]), everywhere)]
    all_to_all x3 -> x0, blocking collectives: 34.1 us -> none  [the longest x1 13.3 us: per_device(): lax.all_to_all(packed, ('core', 'p'), split_axis=0, concat_axis=0, tiled=...]
    ppermute x53 -> x78, waiting for transfers between devices: 197 us -> 173 us  [xor_permute(): return lax.ppermute(x, axis, [(i, i ^ step) for i in range(n)])]
    unnamed x146 -> x141, local copies, waits for them, and re-layouts: 38.1 us -> 16 us
    reshape x23 -> x0, local copies, waits for them, and re-layouts: 19.3 us -> none  [the longest x5 4.58 us: per_device(): item.reshape(plane, slab, nz, unit).transpose(1, 2, 0, 3)]
  transfers between devices with their start and end apart: 66 -> 100, of which waited for: 29 -> 40; matrix products, arithmetic and copies ran while one was open for 25% -> 19% of each run, Pallas kernels for 4% -> 18%
where the time goes in v2:
time: 592 us; the launch traced here: 587 us
  waiting for transfers between devices  213 us (36%)
  Pallas kernels  119 us (20%)
  starting transfers between devices  105 us (18%)
  other arithmetic  55.6 us (9%)
  local copies, waits for them, and re-layouts  41.5 us (7%)
  matrix products  37 us (6%)
  between operations  16.1 us (3%)
    ppermute x78, waiting for transfers between devices, xor_permute(): return lax.ppermute(x, axis, [(i, i ^ step) for i in range(n)])  173 us
    ppermute x78, starting transfers between devices, xor_permute(): return lax.ppermute(x, axis, [(i, i ^ step) for i in range(n)])  69.5 us
    pallas_call x2, Pallas kernels, attend_back(): pl.pallas_call(functools.partial(attend_back_kernel, heads, depth, chunk,...  46.1 us
    dot_general x7, matrix products, dot(): lax.dot_general(left, right, (contract, ((), ())), preferred_element_type...  35.3 us
    pallas_call x2, Pallas kernels, attend(): pl.pallas_call(functools.partial(attend_kernel, heads, depth, chunk, memb...  30.6 us
    pallas_call x2, Pallas kernels, ffn(): pl.pallas_call(ffn_kernel, grid=(count,), in_specs=[blocks(width, first),...  26.3 us
    all_to_all x6, starting transfers between devices, all_to_all(): return lax.all_to_all(x, axes, split_axis=0, concat_axis=0, tiled=True)  22.7 us
    unnamed x141, local copies, waits for them, and re-layouts  16 us
  transfers between devices with their start and end apart: 100, of which 40 were waited for; matrix products, arithmetic and copies ran while one was open for 19% of the time, Pallas kernels for 18%

profile of v2, /device:TPU:0, one launch (start us, length us, event | category | flops | bytes accessed | tf_op | source)
XLA Modules:
  0.0 587.3 jit_solution(6716724660686490027)
XLA Ops:
  26.3 4.9 collective-permute-done.8
  33.5 4.3 all-to-all-start
  40.8 12.8 %collective-permute-done.4 = bf16[2,32,1536]{2,1,0:T(8,128)(2,1)S(1)} collective-permute-done((bf16[2,32,1536]{2,1,0:T(8,128)(2,1)S(1)}, bf16[2,32,1536]{2,1,0:T(8,128)(2,1)S(1)}, u32[]{:S(2)}, u32[]{:S(2)}) %collective-permute-start.4) | collective-permute-done | bytes 196640 | tf_op jit(solution)/shard_map/ppermute | solution.py:24
  64.1 12.0 %collective-permute-done.10.refs_2_ = bf16[256,1536]{1,0:T(8,128)(2,1)} collective-permute-done((bf16[256,1536]{1,0:T(8,128)(2,1)S(1)}, bf16[256,1536]{1,0:T(8,128)(2,1)}, u32[]{:S(2)}, u32[]{:S(2)}) %collective-permute-start.10) | collective-permute-done | bytes 786464 | tf_op jit(solution)/shard_map/ppermute | solution.py:24
  88.3 4.3 collective-permute-done.11.refs_3_
  94.4 5.5 all-to-all-done.2
  107.6 5.1 collective-permute-done.19
  120.1 15.4 %attend.2 = (bf16[1024,1536]{1,0:T(8,128)(2,1)}, bf16[1024,576]{1,0:T(8,128)(2,1)}, f32[1024,192]{1,0:T(8,128)}, f32[1024,128]{1,0:T(8,128)}, f32[1024,192]{1,0:...) custom-call(s32[32]{0:T(128)} %get-tuple-element.240.table, ...), custom_call_target="tpu_custom_call" | custom-call | flops 14000000000 | bytes 10000000 | tf_op jit(solution)/shard_map/attend/pallas_call | solution.py:367
  142.6 15.2 %attend.3 = (bf16[1024,1536]{1,0:T(8,128)(2,1)}, bf16[1024,576]{1,0:T(8,128)(2,1)}, f32[1024,192]{1,0:T(8,128)}, f32[1024,128]{1,0:T(8,128)}, f32[1024,192]{1,0:...) custom-call(s32[32]{0:T(128)} %get-tuple-element.265.table, ...), custom_call_target="tpu_custom_call" | custom-call | flops 14000000000 | bytes 10000000 | tf_op jit(solution)/shard_map/attend/pallas_call | solution.py:367
  173.1 7.2 %collective-permute-done.43 = bf16[128,1536]{1,0:T(8,128)(2,1)S(1)} collective-permute-done((bf16[128,1536]{1,0:T(8,128)(2,1)S(1)}, bf16[128,1536]{1,0:T(8,128)(2,1)S(1)}, u32[]{:S(2)}, u32[]{:S(2)}) %collective-permute-start.43) | collective-permute-done | bytes 393248 | tf_op jit(solution)/shard_map/ppermute | solution.py:24
  187.0 7.0 %collective-permute-done.29 = bf16[128,1536]{1,0:T(8,128)(2,1)S(1)} collective-permute-done((bf16[128,1536]{1,0:T(8,128)(2,1)S(1)}, bf16[128,1536]{1,0:T(8,128)(2,1)S(1)}, u32[]{:S(2)}, u32[]{:S(2)}) %collective-permute-start.29) | collective-permute-done | bytes 393248 | tf_op jit(solution)/shard_map/ppermute | solution.py:24
  197.8 16.5 %collective-permute-done.30 = bf16[256,1536]{1,0:T(8,128)(2,1)S(1)} collective-permute-done((bf16[256,1536]{1,0:T(8,128)(2,1)S(1)}, bf16[256,1536]{1,0:T(8,128)(2,1)S(1)}, u32[]{:S(2)}, u32[]{:S(2)}) %collective-permute-start.30) | collective-permute-done | bytes 786464 | tf_op jit(solution)/shard_map/ppermute | solution.py:24
  220.3 16.0 %collective-permute-done.33 = bf16[256,1536]{1,0:T(8,128)(2,1)S(1)} collective-permute-done((bf16[256,1536]{1,0:T(8,128)(2,1)S(1)}, bf16[256,1536]{1,0:T(8,128)(2,1)S(1)}, u32[]{:S(2)}, u32[]{:S(2)}) %collective-permute-start.33) | collective-permute-done | bytes 786464 | tf_op jit(solution)/shard_map/ppermute | solution.py:24
  241.0 5.5 collective-permute-done.35
  253.3 13.2 %ffn.2 = (bf16[2048,512]{1,0:T(8,128)(2,1)}, bf16[2048,1024]{1,0:T(8,128)(2,1)}, bf16[1024,1536]{1,0:T(8,128)(2,1)}) custom-call(bf16[2048,1536]{1,0:T(8,128)(2,1)} %constant_dynamic-update-slice_fusion.h_ref, bf16[2048,1536]{1,0:T(8,128)(2,1)} %copy-done.32, bf16[1536,1024]{1,0:T(8,128)(2,1)} %bitcast.321, bf16[4,128,1536]{2,1,0:T(8,128)(2,1)} %bitcast.328), custom_call_target="tpu_custom_call" | custom-call | flops 8053063680 | bytes 12582912 | tf_op jit(solution)/shard_map/ffn/pallas_call | solution.py:475
  267.0 13.1 %ffn.3 = (bf16[2048,512]{1,0:T(8,128)(2,1)}, bf16[2048,1024]{1,0:T(8,128)(2,1)}, bf16[1024,1536]{1,0:T(8,128)(2,1)}) custom-call(bf16[2048,1536]{1,0:T(8,128)(2,1)} %constant_dynamic-update-slice_fusion.h_ref, bf16[2048,1536]{1,0:T(8,128)(2,1)} %copy-done.32, bf16[1536,1024]{1,0:T(8,128)(2,1)} %bitcast.322, ...), custom_call_target="tpu_custom_call", output_to_operand_aliasing={{0}: (4, {}), {1}: (5, {})} | custom-call | flops 8053063680 | bytes 12582912 | tf_op jit(solution)/shard_map/ffn/pallas_call | solution.py:475
  285.5 9.1 %fusion.91 = bf16[1536,1024]{1,0:T(8,128)(2,1)S(1)} fusion(bf16[2048,1536]{1,0:T(8,128)(2,1)} %constant_dynamic-update-slice_fusion.h_ref, bf16[2048,1024]{1,0:T(8,128)(2,1)S(1)} %copy-done.57), kind=kOutput, calls=%fused_computation.294 | convolution fusion | flops 6442450944 | bytes 13631488 | tf_op jit(solution)/shard_map/dot_general | solution.py:19
  303.1 11.8 %collective-permute-done.52 = bf16[256,1536]{1,0:T(8,128)(2,1)} collective-permute-done((bf16[256,1536]{1,0:T(8,128)(2,1)S(1)}, bf16[256,1536]{1,0:T(8,128)(2,1)}, u32[]{:S(2)}, u32[]{:S(2)}) %collective-permute-start.52) | collective-permute-done | bytes 786464 | tf_op jit(solution)/shard_map/ppermute | solution.py:24
  317.5 4.1 fusion.83
  330.8 9.7 %collective-permute-done.54.refs_1_.refs_9_ = bf16[256,1536]{1,0:T(8,128)(2,1)} collective-permute-done((bf16[256,1536]{1,0:T(8,128)(2,1)S(1)}, bf16[256,1536]{1,0:T(8,128)(2,1)}, u32[]{:S(2)}, u32[]{:S(2)}) %collective-permute-start.54) | collective-permute-done | bytes 786464 | tf_op jit(solution)/shard_map/ppermute | solution.py:24
  345.4 9.0 %collective-permute-done.59.refs_3_ = bf16[128,1536]{1,0:T(8,128)(2,1)S(1)} collective-permute-done((bf16[128,1536]{1,0:T(8,128)(2,1)S(1)}, bf16[128,1536]{1,0:T(8,128)(2,1)S(1)}, u32[]{:S(2)}, u32[]{:S(2)}) %collective-permute-start.59) | collective-permute-done | bytes 393248 | tf_op jit(solution)/shard_map/ppermute | solution.py:24
  366.4 24.9 %attend_back.2 = (bf16[1024,896]{1,0:T(8,128)(2,1)}, bf16[4,128,1536]{2,1,0:T(8,128)(2,1)}, bf16[4,128,1536]{2,1,0:T(8,128)(2,1)}, f32[8,128]{1,0:T(8,128)}, bf16[192,1536]{1,0:T(8,128)(2,1)}) custom-call(s32[32]{0:T(128)} %get-tuple-element.240.table, bf16[256,1536]{1,0:T(8,128)(2,1)} %copy-done.25, ...), custom_call_target="tpu_custom_call" | custom-call | flops 20000000000 | bytes 10000000 | tf_op jit(solution)/shard_map/attend_back/pallas_call | solution.py:403
  392.1 4.2 all-to-all-start.3
  399.2 8.3 %fusion.93 = f32[1536,896]{1,0:T(8,128)} fusion(bf16[1024,1536]{1,0:T(8,128)(2,1)} %get-tuple-element.256, bf16[1024,896]{1,0:T(8,128)(2,1)} %get-tuple-element.257), kind=kOutput, calls=%fused_computation.296 | convolution fusion | flops 2818572288 | bytes 10485760 | tf_op jit(solution)/shard_map/dot_general | solution.py:19
  411.8 14.4 %reduce-scatter.4.cloned.1.call-done = bf16[576,1024]{1,0:T(8,128)(2,1)} async-done(((bf16[2304,1024]{1,0:T(8,128)(2,1)}), bf16[576,1024]{1,0:T(8,128)(2,1)}) %reduce-scatter.4.cloned.1.call-update) | async-done | bytes 1179664 | tf_op jit(solution)/shard_map/reduce_scatter | solution.py:590
  429.1 21.2 %attend_back.3 = (bf16[1024,896]{1,0:T(8,128)(2,1)}, bf16[4,128,1536]{2,1,0:T(8,128)(2,1)}, bf16[4,128,1536]{2,1,0:T(8,128)(2,1)}, f32[8,128]{1,0:T(8,128)}) custom-call(s32[32]{0:T(128)} %get-tuple-element.265.table, bf16[256,1536]{1,0:T(8,128)(2,1)} %copy-done.25, bf16[256,1536]{1,0:T(8,128)(2,1)} %collective-permute-done.54.refs_1_.refs_9_, ...), custom_call_target="tpu_custom_call" | custom-call | flops 20000000000 | bytes 10000000 | tf_op jit(solution)/shard_map/attend_back/pallas_call | solution.py:403
  465.0 6.6 %add_convert_fusion = bf16[1536,896]{1,0:T(8,128)(2,1)} fusion(f32[1536,896]{1,0:T(8,128)} %fusion.93, bf16[1024,1536]{1,0:T(8,128)(2,1)S(1)} %copy-done.58, bf16[1024,896]{1,0:T(8,128)(2,1)S(1)} %copy-done.59), kind=kOutput, calls=%fused_computation.2 | convolution fusion | flops 2821324800 | bytes 13238272 | tf_op jit(solution)/shard_map/dot_general | solution.py:19
  489.6 12.6 %collective-permute-done.79 = f32[24]{0:T(128)} collective-permute-done((f32[24]{0:T(128)S(1)}, f32[24]{0:T(128)}, u32[]{:S(2)}, u32[]{:S(2)}) %collective-permute-start.79) | collective-permute-done | bytes 128 | tf_op jit(solution)/shard_map/ppermute | solution.py:24
  514.2 14.0 %collective-permute-done.80 = bf16[2,32,1536]{2,1,0:T(8,128)(2,1)S(1)} collective-permute-done((bf16[2,32,1536]{2,1,0:T(8,128)(2,1)S(1)}, bf16[2,32,1536]{2,1,0:T(8,128)(2,1)S(1)}, u32[]{:S(2)}, u32[]{:S(2)}) %collective-permute-start.80) | collective-permute-done | bytes 196640 | tf_op jit(solution)/shard_map/ppermute | solution.py:24
  528.2 11.7 %collective-permute-done.81 = bf16[2,32,1536]{2,1,0:T(8,128)(2,1)S(1)} collective-permute-done((bf16[2,32,1536]{2,1,0:T(8,128)(2,1)S(1)}, bf16[2,32,1536]{2,1,0:T(8,128)(2,1)S(1)}, u32[]{:S(2)}, u32[]{:S(2)}) %collective-permute-start.81) | collective-permute-done | bytes 196640 | tf_op jit(solution)/shard_map/ppermute | solution.py:24
  548.5 4.1 collective-permute-start.86
  568.7 5.0 all-to-all-done.5.x_ref
  (474 shorter events, 242.6 us)
Async XLA Ops:
  33.5 20.1 %all-to-all-start = ((bf16[8,48,896]{2,1,0:T(8,128)(2,1)}), bf16[8,48,896]{2,1,0:T(8,128)(2,1)S(1)}, u32[]{:S(2)}, u32[]{:S(2)}) async-start(bf16[8,48,896]{2,1,0:T(8,128)(2,1)} %layout.4), calls=%async_computation | async-start | bytes 1376256 | tf_op jit(solution)/shard_map/all_to_all | solution.py:586
  37.8 76.5 %all-gather.7.cloned.1.call-start = ((), (), s32[]{:S(2)}) async-start(), calls=%async_computation.12 | async-start | bytes 3440640 | tf_op jit(solution)/shard_map/all_gather | solution.py:669
  54.6 21.6 %collective-permute-start.10 = (bf16[256,1536]{1,0:T(8,128)(2,1)S(1)}, bf16[256,1536]{1,0:T(8,128)(2,1)}, u32[]{:S(2)}, u32[]{:S(2)}) collective-permute-start(bf16[256,1536]{1,0:T(8,128)(2,1)S(1)} %bitcast.264), channel_id=1, source_target_pairs={{0,2},{2,0},{1,3},{3,1},{4,6},{6,4},{5,7},{7,5},{8,10},{10,8},{9,1... | collective-permute-start | bytes 2359304 | tf_op jit(solution)/shard_map/ppermute | solution.py:24
  56.3 20.6 %collective-permute-start.9 = (bf16[256,1536]{1,0:T(8,128)(2,1)S(1)}, bf16[256,1536]{1,0:T(8,128)(2,1)}, u32[]{:S(2)}, u32[]{:S(2)}) collective-permute-start(bf16[256,1536]{1,0:T(8,128)(2,1)S(1)} %bitcast.265), channel_id=1, source_target_pairs={{0,1},{1,0},{2,3},{3,2},{4,5},{5,4},{6,7},{7,6},{8,9},{9,8},{10,11... | collective-permute-start | bytes 2359304 | tf_op jit(solution)/shard_map/ppermute | solution.py:24
  57.8 24.5 %all-to-all-start.1 = ((bf16[4,48,1536]{2,1,0:T(8,128)(2,1)}), bf16[4,48,1536]{2,1,0:T(8,128)(2,1)S(1)}, u32[]{:S(2)}, u32[]{:S(2)}) async-start(bf16[4,48,1536]{2,1,0:T(8,128)(2,1)} %pad_maximum_fusion.18), calls=%async_computation.1 | async-start | bytes 1179648 | tf_op jit(solution)/shard_map/all_to_all | solution.py:586
  61.3 21.0 %collective-permute-start.24 = (s32[2,4]{1,0:T(2,128)S(1)}, s32[2,4]{1,0:T(2,128)S(1)}, u32[]{:S(2)}, u32[]{:S(2)}) collective-permute-start(s32[2,4]{1,0:T(2,128)S(1)} %bitcast.330), channel_id=1, source_target_pairs={{0,0},{8,1},{16,2},{24,3},{4,4},{12,5},{20,6},{28,7},{1,8},{9,9},{... | collective-permute-start | bytes 104 | tf_op jit(solution)/shard_map/ppermute | solution.py:681
  78.7 21.3 %collective-permute-start.14 = (bf16[256,1536]{1,0:T(8,128)(2,1)}, bf16[256,1536]{1,0:T(8,128)(2,1)}, u32[]{:S(2)}, u32[]{:S(2)}) collective-permute-start(bf16[256,1536]{1,0:T(8,128)(2,1)} %collective-permute-done.9.refs_1_), channel_id=1, source_target_pairs={{0,4},{4,0},{1,5},{5,1},{2,6},{6,2},{3,7},{7,3},{8,12},{12,8},{9,1... | collective-permute-start | bytes 2359304 | tf_op jit(solution)/shard_map/ppermute | solution.py:24
  79.8 20.2 %collective-permute-start.15 = (bf16[256,1536]{1,0:T(8,128)(2,1)}, bf16[256,1536]{1,0:T(8,128)(2,1)}, u32[]{:S(2)}, u32[]{:S(2)}) collective-permute-start(bf16[256,1536]{1,0:T(8,128)(2,1)} %collective-permute-done.10.refs_2_), channel_id=1, source_target_pairs={{0,4},{4,0},{1,5},{5,1},{2,6},{6,2},{3,7},{7,3},{8,12},{12,8},{9,1... | collective-permute-start | bytes 2359304 | tf_op jit(solution)/shard_map/ppermute | solution.py:24
  85.9 167.4 %all-gather.11.cloned.1.call-start = ((), (), s32[]{:S(2)}) async-start(), calls=%async_computation.14 | async-start | bytes 1966080 | tf_op jit(solution)/shard_map/all_gather | solution.py:715
  114.4 21.1 %collective-permute-start.21 = (bf16[2,32,1536]{2,1,0:T(8,128)(2,1)S(1)}, bf16[2,32,1536]{2,1,0:T(8,128)(2,1)S(1)}, u32[]{:S(2)}, u32[]{:S(2)}) collective-permute-start(bf16[2,32,1536]{2,1,0:T(8,128)(2,1)S(1)} %get-tuple-element.373), channel_id=1, source_target_pairs={{0,8},{8,0},{16,24},{24,16},{1,9},{9,1},{17,25},{25,17},{2,10},{10... | collective-permute-start | bytes 589832 | tf_op jit(solution)/shard_map/ppermute | solution.py:24
  135.6 117.7 %all-gather.9.cloned.1.call-start = ((), (), s32[]{:S(2)}) async-start(), calls=%async_computation.13 | async-start | bytes 3932160 | tf_op jit(solution)/shard_map/all_gather | solution.py:714
  140.2 40.1 %collective-permute-start.27 = (bf16[4,128,1536]{2,1,0:T(8,128)(2,1)}, bf16[4,128,1536]{2,1,0:T(8,128)(2,1)}, u32[]{:S(2)}, u32[]{:S(2)}) collective-permute-start(bf16[4,128,1536]{2,1,0:T(8,128)(2,1)} %get-tuple-element.204), channel_id=1, source_target_pairs={{0,4},{4,0},{1,5},{5,1},{2,6},{6,2},{3,7},{7,3},{8,12},{12,8},{9,1... | collective-permute-start | bytes 4718600 | tf_op jit(solution)/shard_map/ppermute | solution.py:24
  140.2 20.1 %collective-permute-start.25 = (bf16[256,1536]{1,0:T(8,128)(2,1)S(1)}, bf16[256,1536]{1,0:T(8,128)(2,1)}, u32[]{:S(2)}, u32[]{:S(2)}) collective-permute-start(bf16[256,1536]{1,0:T(8,128)(2,1)S(1)} %bitcast.272), channel_id=1, source_target_pairs={{0,1},{1,0},{2,3},{3,2},{4,5},{5,4},{6,7},{7,6},{8,9},{9,8},{10,11... | collective-permute-start | bytes 2359304 | tf_op jit(solution)/shard_map/ppermute | solution.py:24
  142.1 284.0 %reduce-scatter.4.cloned.1.call-start = ((), (), s32[]{:S(2)}) async-start(), calls=%async_computation.9 | async-start | bytes 5898240 | tf_op jit(solution)/shard_map/reduce_scatter | solution.py:590
  173.0 45.3 %collective-permute-start.45 = (bf16[256,1536]{1,0:T(8,128)(2,1)}, bf16[256,1536]{1,0:T(8,128)(2,1)S(1)}, u32[]{:S(2)}, u32[]{:S(2)}) collective-permute-start(bf16[256,1536]{1,0:T(8,128)(2,1)} %collective-permute-done.25), channel_id=1, source_target_pairs={{0,4},{4,0},{1,5},{5,1},{2,6},{6,2},{3,7},{7,3},{8,12},{12,8},{9,1... | collective-permute-start | bytes 2359304 | tf_op jit(solution)/shard_map/ppermute | solution.py:24
  180.3 39.7 %collective-permute-start.46 = (bf16[256,1536]{1,0:T(8,128)(2,1)}, bf16[256,1536]{1,0:T(8,128)(2,1)S(1)}, u32[]{:S(2)}, u32[]{:S(2)}) collective-permute-start(bf16[256,1536]{1,0:T(8,128)(2,1)} %collective-permute-done.26), channel_id=1, source_target_pairs={{0,4},{4,0},{1,5},{5,1},{2,6},{6,2},{3,7},{7,3},{8,12},{12,8},{9,1... | collective-permute-start | bytes 2359304 | tf_op jit(solution)/shard_map/ppermute | solution.py:24
  180.4 39.8 %collective-permute-start.47 = (bf16[128,1536]{1,0:T(8,128)(2,1)S(1)}, bf16[128,1536]{1,0:T(8,128)(2,1)S(1)}, u32[]{:S(2)}, u32[]{:S(2)}) collective-permute-start(bf16[128,1536]{1,0:T(8,128)(2,1)S(1)} %collective-permute-done.42), channel_id=1, source_target_pairs={{0,4},{4,0},{1,5},{5,1},{2,6},{6,2},{3,7},{7,3},{8,12},{12,8},{9,1... | collective-permute-start | bytes 1179656 | tf_op jit(solution)/shard_map/ppermute | solution.py:24
  220.2 28.6 %collective-permute-start.37 = (bf16[256,1536]{1,0:T(8,128)(2,1)S(1)}, bf16[256,1536]{1,0:T(8,128)(2,1)S(1)}, u32[]{:S(2)}, u32[]{:S(2)}) collective-permute-start(bf16[256,1536]{1,0:T(8,128)(2,1)S(1)} %get-tuple-element.334), channel_id=1, source_target_pairs={{0,4},{4,0},{1,5},{5,1},{2,6},{6,2},{3,7},{7,3},{8,12},{12,8},{9,1... | collective-permute-start | bytes 2359304 | tf_op jit(solution)/shard_map/ppermute | solution.py:24
  344.9 21.5 %collective-permute-start.61 = (bf16[256,1536]{1,0:T(8,128)(2,1)}, bf16[256,1536]{1,0:T(8,128)(2,1)}, u32[]{:S(2)}, u32[]{:S(2)}) collective-permute-start(bf16[256,1536]{1,0:T(8,128)(2,1)} %collective-permute-done.54.refs_1_.refs_9_), channel_id=1, source_target_pairs={{0,4},{4,0},{1,5},{5,1},{2,6},{6,2},{3,7},{7,3},{8,12},{12,8},{9,1... | collective-permute-start | bytes 2359304 | tf_op jit(solution)/shard_map/ppermute | solution.py:24
  344.9 21.5 %collective-permute-start.62 = (bf16[256,1536]{1,0:T(8,128)(2,1)}, bf16[256,1536]{1,0:T(8,128)(2,1)}, u32[]{:S(2)}, u32[]{:S(2)}) collective-permute-start(bf16[256,1536]{1,0:T(8,128)(2,1)} %collective-permute-done.55.refs_2_.refs_10_), channel_id=1, source_target_pairs={{0,4},{4,0},{1,5},{5,1},{2,6},{6,2},{3,7},{7,3},{8,12},{12,8},{9,1... | collective-permute-start | bytes 2359304 | tf_op jit(solution)/shard_map/ppermute | solution.py:24
  363.1 28.9 %collective-permute-start.57 = (bf16[128,1536]{1,0:T(8,128)(2,1)}, bf16[128,1536]{1,0:T(8,128)(2,1)}, u32[]{:S(2)}, u32[]{:S(2)}) collective-permute-start(bf16[128,1536]{1,0:T(8,128)(2,1)} %get-tuple-element.364), channel_id=1, source_target_pairs={{0,2},{2,0},{1,3},{3,1},{4,6},{6,4},{5,7},{7,5},{8,10},{10,8},{9,1... | collective-permute-start | bytes 1179656 | tf_op jit(solution)/shard_map/ppermute | solution.py:24
  365.0 27.1 %collective-permute-start.58 = (bf16[128,1536]{1,0:T(8,128)(2,1)}, bf16[128,1536]{1,0:T(8,128)(2,1)}, u32[]{:S(2)}, u32[]{:S(2)}) collective-permute-start(bf16[128,1536]{1,0:T(8,128)(2,1)} %get-tuple-element.363), channel_id=1, source_target_pairs={{0,1},{1,0},{2,3},{3,2},{4,5},{5,4},{6,7},{7,6},{8,9},{9,8},{10,11... | collective-permute-start | bytes 1179656 | tf_op jit(solution)/shard_map/ppermute | solution.py:24
  396.3 76.4 %reduce-scatter.6.cloned.1.call-start = ((), (), s32[]{:S(2)}) async-start(), calls=%async_computation.10 | async-start | bytes 737280 | tf_op jit(solution)/shard_map/reduce_scatter | solution.py:590
  409.5 131.3 %reduce-scatter.8.cloned.1.call-start = ((), (), s32[]{:S(2)}) async-start(), calls=%async_computation.11 | async-start | bytes 3440640 | tf_op jit(solution)/shard_map/reduce_scatter | solution.py:590
  426.1 25.2 %collective-permute-start.66 = (bf16[256,1536]{1,0:T(8,128)(2,1)}, bf16[256,1536]{1,0:T(8,128)(2,1)S(1)}, u32[]{:S(2)}, u32[]{:S(2)}) collective-permute-start(bf16[256,1536]{1,0:T(8,128)(2,1)} %pad_maximum_fusion.12), channel_id=1, source_target_pairs={{0,1},{1,0},{2,3},{3,2},{4,5},{5,4},{6,7},{7,6},{8,9},{9,8},{10,11... | collective-permute-start | bytes 2359304 | tf_op jit(solution)/shard_map/ppermute | solution.py:24
  427.6 23.8 %collective-permute-start.67 = (bf16[256,1536]{1,0:T(8,128)(2,1)}, bf16[256,1536]{1,0:T(8,128)(2,1)S(1)}, u32[]{:S(2)}, u32[]{:S(2)}) collective-permute-start(bf16[256,1536]{1,0:T(8,128)(2,1)} %pad_maximum_fusion.13), channel_id=1, source_target_pairs={{0,2},{2,0},{1,3},{3,1},{4,6},{6,4},{5,7},{7,5},{8,10},{10,8},{9,1... | collective-permute-start | bytes 2359304 | tf_op jit(solution)/shard_map/ppermute | solution.py:24
  481.4 21.5 %collective-permute-start.77 = (bf16[256,1536]{1,0:T(8,128)(2,1)}, bf16[256,1536]{1,0:T(8,128)(2,1)}, u32[]{:S(2)}, u32[]{:S(2)}) collective-permute-start(bf16[256,1536]{1,0:T(8,128)(2,1)} %pad_maximum_fusion.15), channel_id=1, source_target_pairs={{0,1},{1,0},{2,3},{3,2},{4,5},{5,4},{6,7},{7,6},{8,9},{9,8},{10,11... | collective-permute-start | bytes 2359304 | tf_op jit(solution)/shard_map/ppermute | solution.py:24
  481.9 21.5 %collective-permute-start.78 = (bf16[256,1536]{1,0:T(8,128)(2,1)}, bf16[256,1536]{1,0:T(8,128)(2,1)}, u32[]{:S(2)}, u32[]{:S(2)}) collective-permute-start(bf16[256,1536]{1,0:T(8,128)(2,1)} %pad_maximum_fusion.16), channel_id=1, source_target_pairs={{0,2},{2,0},{1,3},{3,1},{4,6},{6,4},{5,7},{7,5},{8,10},{10,8},{9,1... | collective-permute-start | bytes 2359304 | tf_op jit(solution)/shard_map/ppermute | solution.py:24
  486.0 28.1 %all-to-all-start.4 = ((bf16[8,48,1024]{2,1,0:T(8,128)(2,1)}), bf16[8,48,1024]{2,1,0:T(8,128)(2,1)S(1)}, u32[]{:S(2)}, u32[]{:S(2)}) async-start(bf16[8,48,1024]{2,1,0:T(8,128)(2,1)} %bitcast.103), calls=%async_computation.7 | async-start | bytes 1572864 | tf_op jit(solution)/shard_map/all_to_all | solution.py:586
  511.2 28.7 %collective-permute-start.81 = (bf16[2,32,1536]{2,1,0:T(8,128)(2,1)S(1)}, bf16[2,32,1536]{2,1,0:T(8,128)(2,1)S(1)}, u32[]{:S(2)}, u32[]{:S(2)}) collective-permute-start(bf16[2,32,1536]{2,1,0:T(8,128)(2,1)S(1)} %get-tuple-element.354), channel_id=1, source_target_pairs={{0,16},{8,24},{16,0},{24,8},{1,17},{9,25},{17,1},{25,9},{2,18},{10... | collective-permute-start | bytes 589832 | tf_op jit(solution)/shard_map/ppermute | solution.py:24
  512.8 27.1 %collective-permute-start.82 = (bf16[2,32,1536]{2,1,0:T(8,128)(2,1)S(1)}, bf16[2,32,1536]{2,1,0:T(8,128)(2,1)S(1)}, u32[]{:S(2)}, u32[]{:S(2)}) collective-permute-start(bf16[2,32,1536]{2,1,0:T(8,128)(2,1)S(1)} %get-tuple-element.353), channel_id=1, source_target_pairs={{0,24},{8,16},{16,8},{24,0},{1,25},{9,17},{17,9},{25,1},{2,26},{10... | collective-permute-start | bytes 589832 | tf_op jit(solution)/shard_map/ppermute | solution.py:24
  544.9 21.7 %collective-permute-start.83 = (bf16[4,32,1536]{2,1,0:T(8,128)(2,1)}, bf16[4,32,1536]{2,1,0:T(8,128)(2,1)S(1)}, u32[]{:S(2)}, u32[]{:S(2)}) collective-permute-start(bf16[4,32,1536]{2,1,0:T(8,128)(2,1)} %get-tuple-element.350), channel_id=1, source_target_pairs={{0,1},{1,0},{2,3},{3,2},{4,5},{5,4},{6,7},{7,6},{8,9},{9,8},{10,11... | collective-permute-start | bytes 1179656 | tf_op jit(solution)/shard_map/ppermute | solution.py:33
  (130 other events, 1563.6 us)
Sparse Core Ops, SparseCore 0:
  54.7 59.5 all-gather.6
  135.7 36.5 all-gather.10
  174.5 62.3 all-gather.8
  341.8 84.2 reduce-scatter.3
  428.3 22.3 reduce-scatter.5
  473.5 67.3 reduce-scatter.7

commit v3 on v2

--- a/solution.py
+++ b/solution.py
@@ -68,7 +68,7 @@
     return [x, xor_permute(x, "q", 1)] + [xor_permute(x, "p", k) for k in range(1, np_)]
 
 
-def gather_rest(first):
+def gather_own_core(first):
     np_ = lax.axis_size("p")
     x, over_q = first[:2]
     half = x.shape[0] // 2
@@ -79,7 +79,15 @@
         own = [x, over_q]
         for k in range(1, np_):
             own += [first[1 + k], xor_permute(over_q, "p", k)]
+    return own
+
+
+def gather_both_cores(own):
     return own + jax.tree.map(lambda block: xor_permute(block, "core", 1), own)
+
+
+def gather_rest(first):
+    return gather_both_cores(gather_own_core(first))
 
 
 def gather_plane(x):
@@ -94,12 +102,55 @@
     return sum(part.astype(F32) for part in parts)
 
 
+def term(items, number=None):
+    operands = []
+    for item in items:
+        if number is None:
+            operands.append((item, pl.BlockSpec(item.shape, lambda i: (0, 0))))
+        else:
+            operands.append((item, pl.BlockSpec((None,) + item.shape[1:], lambda i: (number, 0, 0))))
+    return operands
+
+
+def read_term(refs):
+    parts = [ref[...].astype(F32) for ref in refs]
+    return parts[0] if len(parts) == 1 else jnp.concatenate(parts, axis=0)
+
+
+def rows_kernel(body, terms, outs, name):
+    counts = [len(item) for item in terms]
+    operands = [pair for item in terms for pair in item]
+
+    def kernel(*refs):
+        values, at = [], 0
+        for count in counts:
+            values.append(read_term(refs[at:at + count]))
+            at += count
+        for ref, value in zip(refs[at:], body(*values)):
+            ref[...] = value.astype(ref.dtype)
+
+    return pl.pallas_call(
+        kernel,
+        grid=(1,),
+        in_specs=[spec for _, spec in operands],
+        out_specs=[pl.BlockSpec(shape, lambda i: (0, 0)) for shape, _ in outs],
+        out_shape=[jax.ShapeDtypeStruct(shape, kind) for shape, kind in outs],
+        compiler_params=pltpu.CompilerParams(vmem_limit_bytes=VMEM_LIMIT),
+        name=name,
+    )(*[array for array, _ in operands])
+
+
 def scatter_core(far, near):
     got = [xor_permute(item, "core", 1) for item in far]
-    shape = (2 * lax.axis_size("p"), -1, near[0].shape[-1])
-    near = [item.reshape(shape) for item in near]
-    got = [item.reshape(shape) for item in got]
-    return near, got, both_cores(near, got, shape[0] - 1).astype(BF16)
+    last = 2 * lax.axis_size("p") - 1
+    rows, width = sum(item.shape[1] for item in near), near[0].shape[2]
+    half = rows // 2
+
+    def body(one, other):
+        total = one + other
+        return total[:half], total[half:]
+
+    return near, got, rows_kernel(body, [term(near, last), term(got, last)], [((half, width), BF16)] * 2, "sum_last")
 
 
 def both_cores(near, got, number):
@@ -111,24 +162,31 @@
     near, got, last = lax.optimization_barrier((near, got, last))
     made = ()
     if np_ == 2:
-        half = last.shape[0] // 2
-        into_q = xor_permute(last[:half], "p", 1)
-        into_p = xor_permute(last[half:], "q", 1)
+        into_q = xor_permute(last[0], "p", 1)
+        into_p = xor_permute(last[1], "q", 1)
         if beside is not None:
             into_q, into_p, made = lax.optimization_barrier((into_q, into_p, beside(last)))
-        to_q, to_p = both_cores(near, got, 1), both_cores(near, got, 2)
-        to_q = jnp.concatenate([add_up(to_q[:half], into_q), to_q[half:]], axis=0).astype(BF16)
-        to_p = jnp.concatenate([to_p[:half], add_up(to_p[half:], into_p)], axis=0).astype(BF16)
-        own = [side[0][0] if len(side) == 1 else jnp.concatenate([item[0] for item in side]) for side in (near, got)]
-        return own, [(to_q, "q"), (to_p, "p")], made
+        half, width = last[0].shape
+
+        def body(near_q, got_q, near_p, got_p, into_q, into_p):
+            to_q, to_p = near_q + got_q, near_p + got_p
+            to_q = jnp.concatenate([to_q[:half] + into_q, to_q[half:]], axis=0)
+            return to_q, jnp.concatenate([to_p[:half], to_p[half:] + into_p], axis=0)
+
+        to_q, to_p = rows_kernel(
+            body, [term(near, 1), term(got, 1), term(near, 2), term(got, 2), term([into_q]), term([into_p])],
+            [((2 * half, width), BF16)] * 2, "sum_next",
+        )
+        return [(near, 0), (got, 0)], [(to_q, "q"), (to_p, "p")], made
     if beside is not None:
         made = beside(last)
+    last = jnp.concatenate(last, axis=0)
     pair = [both_cores(near, got, 0), both_cores(near, got, 1)]
     for k in range(1, np_):
         for side in range(2):
             item = last if 2 * k + side == 2 * np_ - 1 else both_cores(near, got, 2 * k + side).astype(BF16)
             pair[side] = pair[side] + xor_permute(item, "p", k).astype(F32)
-    return [pair[0]], [(pair[1].astype(BF16), "q")], made
+    return [([pair[0]], None)], [(pair[1].astype(BF16), "q")], made
 
 
 def scatter_first(far, near, beside=None):
@@ -143,12 +201,45 @@
     return [xor_permute(item, axis, 1) for item, (_, axis) in zip(sends, state[1])]
 
 
-def scatter_rest(state):
-    return add_up(*state[0], *received(state, sent(state)))
-
-
-def total_over(axis, x):
-    step = 1
+def sum_terms(parts, arrived):
+    return [term(*part) for part in parts] + [term([item]) for item in arrived]
+
+
+def normed_rows(x):
+    return x * lax.rsqrt(jnp.mean(x * x, axis=-1, keepdims=True) + EPS)
+
+
+def add_and_norm(parts, arrived, own, gain):
+    terms = sum_terms(parts, arrived)
+
+    def body(own, gain, *values):
+        total = own + sum(values)
+        return total, normed_rows(total) * gain
+
+    return rows_kernel(body, [term([own]), term([gain])] + terms, [(own.shape, F32), (own.shape, BF16)], "add_norm")
+
+
+def norm_back(parts, arrived, above, x, gain, kinds):
+    terms = sum_terms(parts, arrived)
+
+    def body(above, x, gain, *values):
+        r = lax.rsqrt(jnp.mean(x * x, axis=-1, keepdims=True) + EPS)
+        unit, scaled = x * r, sum(values) * gain
+        total = above + r * (scaled - unit * jnp.mean(scaled * unit, axis=-1, keepdims=True))
+        return [total] * len(kinds)
+
+    return rows_kernel(
+        body, [term([above]), term([x]), term([gain])] + terms, [(x.shape, kind) for kind in kinds], "norm_back"
+    )
+
+
+def add_rows(parts, arrived, own):
+    return rows_kernel(
+        lambda *values: [sum(values)], [term([own])] + sum_terms(parts, arrived), [(own.shape, BF16)], "add_rows"
+    )[0]
+
+
+def total_over(axis, x, step=1):
     while step < lax.axis_size(axis):
         x = x + xor_permute(x, axis, step)
         step *= 2
@@ -183,8 +274,8 @@
 def attend_kernel(heads, depth, chunk, members, table, *refs):
     x_refs, refs = refs[:members], refs[members:]
     w_ref, bias_ref, begin_ref = refs[:3]
-    h_ref, qkv_ref, g_ref, z_ref, a_ref, total_ref, cumul_ref, b_ref, gain_ref = refs[3:12]
-    ka, va, rows, part = refs[12:]
+    h_ref, qkv_ref, g_ref, z_ref, a_ref, total_ref, cumul_ref, b_ref, gain_ref = refs[-13:-4]
+    ka, va, rows, part = refs[-4:]
     total = total_ref.shape[0]
     columns = heads * depth
     bq = min(BQ, total)
@@ -242,11 +333,12 @@
         b_ref[j, at:at + chunk, :] = part[natural_rows(table, number, chunk), 0:columns]
 
 
-def attend_back_kernel(heads, depth, chunk, members, streams, table, *refs):
+def attend_back_kernel(heads, depth, chunk, members, streams, held, table, *refs):
     x_refs, refs = refs[:members], refs[members:]
     extra = members * max(0, streams - 1)
     other_refs, gated_refs, refs = refs[:extra], refs[extra:extra + streams], refs[extra + streams:]
     w_ref, o_ref, qkv_ref, g_ref, z_ref, a_ref, total_ref, cumul_ref, begin_ref = refs[:9]
+    refs = refs[held:]
     right_ref, far_ref, near_ref, dbias_ref = refs[9:13]
     part, below_grad, qa, ka, va, da, dkn, dvn, rows, deltas, dcumul = refs[-11:]
     if streams:
@@ -352,14 +444,19 @@
     return pl.BlockSpec(array.shape, lambda i, t: (0,) * array.ndim, pipeline_mode=pl.Buffered(1))
 
 
-def attend(table, blocks, m, streams, weights, bias, begin, heads, depth, chunk):
+def own_part(shape, m):
+    return pl.BlockSpec(shape, lambda i, t: (m, 0), pipeline_mode=pl.Buffered(1))
+
+
+def attend(table, blocks, m, streams, weights, bias, begin, into, heads, depth, chunk):
     arrays, specs = one_stream(blocks, m, streams)
     members, (rows, width) = len(arrays), specs[0].block_shape
     total = begin.shape[0]
     columns = heads * depth
     begin = begin[:, None]
+    into = [] if into is None else [into]
     outs = [
-        ((total, width), BF16), ((total, 3 * columns), BF16), ((total, columns), F32), ((total, 128), F32),
+        ((streams * total, width), BF16), ((total, 3 * columns), BF16), ((total, columns), F32), ((total, 128), F32),
         ((total, columns), F32), ((total, 128), F32), ((total, 128), F32), ((members, rows, columns), BF16),
         ((8, width), F32),
     ]
@@ -369,8 +466,8 @@
         grid_spec=pltpu.PrefetchScalarGridSpec(
             num_scalar_prefetch=1,
             grid=(1,),
-            in_specs=specs + [fixed(weights), fixed(bias), fixed(begin)],
-            out_specs=[fixed(item) for item in out_shape],
+            in_specs=specs + [fixed(weights), fixed(bias), fixed(begin)] + [pl.BlockSpec(memory_space=pl.ANY)] * len(into),
+            out_specs=[own_part((total, width), m)] + [fixed(item) for item in out_shape[1:]],
             scratch_shapes=[
                 pltpu.VMEM((heads, total, depth), BF16),
                 pltpu.VMEM((heads, total, 128), BF16),
@@ -380,33 +477,36 @@
         ),
         out_shape=out_shape,
         compiler_params=pltpu.CompilerParams(vmem_limit_bytes=VMEM_LIMIT),
+        input_output_aliases={1 + members + 3: 0} if into else {},
         cost_estimate=pl.CostEstimate(flops=14 * 10 ** 9, bytes_accessed=10 ** 7, transcendentals=0),
         name="attend",
-    )(table, *arrays, weights, bias, begin)
-
-
-def attend_back(table, blocks, m, streams, weights, out_w, kept, begin, gated, heads, depth, chunk):
+    )(table, *arrays, weights, bias, begin, *into)
+
+
+def attend_back(table, blocks, m, streams, weights, out_w, kept, begin, gated, into, heads, depth, chunk):
     arrays, specs = one_stream(blocks, m, streams)
     members, (rows, width) = len(arrays), specs[0].block_shape
     total = begin.shape[0]
     columns = heads * depth
     begin = begin[None, :]
     gated = [] if gated is None else gated
+    into = [] if into is None else [into]
     for other in range(1, len(gated)):
         other_arrays, other_specs = one_stream(blocks, other, streams)
         arrays, specs = arrays + other_arrays, specs + other_specs
     outs = [
-        ((total, 128 + 4 * columns), BF16), ((members // 2, rows, width), BF16), ((members // 2, rows, width), BF16),
+        ((streams * total, 128 + 4 * columns), BF16), ((members // 2, rows, width), BF16), ((members // 2, rows, width), BF16),
         ((8, 128), F32),
     ] + [((columns, width), BF16)] * (len(gated) > 0)
     out_shape = [jax.ShapeDtypeStruct(shape, kind) for shape, kind in outs]
     return pl.pallas_call(
-        functools.partial(attend_back_kernel, heads, depth, chunk, members, len(gated)),
+        functools.partial(attend_back_kernel, heads, depth, chunk, members, len(gated), len(into)),
         grid_spec=pltpu.PrefetchScalarGridSpec(
             num_scalar_prefetch=1,
             grid=(1,),
-            in_specs=specs + [fixed(item) for item in (*gated, weights, out_w, *kept, begin)],
-            out_specs=[fixed(item) for item in out_shape],
+            in_specs=specs + [fixed(item) for item in (*gated, weights, out_w, *kept, begin)]
+            + [pl.BlockSpec(memory_space=pl.ANY)] * len(into),
+            out_specs=[own_part((total, 128 + 4 * columns), m)] + [fixed(item) for item in out_shape[1:]],
             scratch_shapes=[
                 pltpu.VMEM((total, width), BF16),
                 pltpu.VMEM((total, columns), F32),
@@ -423,9 +523,10 @@
         ),
         out_shape=out_shape,
         compiler_params=pltpu.CompilerParams(vmem_limit_bytes=VMEM_LIMIT),
+        input_output_aliases={1 + len(arrays) + len(gated) + 3 + len(kept): 0} if into else {},
         cost_estimate=pl.CostEstimate(flops=20 * 10 ** 9, bytes_accessed=10 ** 7, transcendentals=0),
         name="attend_back",
-    )(table, *arrays, *gated, weights, out_w, *kept, begin)
+    )(table, *arrays, *gated, weights, out_w, *kept, begin, *into)
 
 
 def out_kernel(b_ref, o_ref, far_ref, near_ref):
@@ -477,11 +578,13 @@
         grid=(count,),
         in_specs=[blocks(width, first), blocks(width, first), fixed(weights.shape), fixed((down.shape[0], unit, width))]
         + [pl.BlockSpec(memory_space=pl.ANY)] * len(kept),
-        out_specs=[blocks(share, first), blocks(2 * share, first), blocks(width, 0)],
+        out_specs=[
+            blocks(share, first), blocks(2 * share, first), pl.BlockSpec((None, BQ, width), lambda i: (i, 0, 0)),
+        ],
         out_shape=[
             jax.ShapeDtypeStruct((rows, share), BF16),
             jax.ShapeDtypeStruct((rows, 2 * share), BF16),
-            jax.ShapeDtypeStruct((count * BQ, width), BF16),
+            jax.ShapeDtypeStruct((count, BQ, width), BF16),
         ],
         input_output_aliases={4 + i: i for i in range(len(kept))},
         compiler_params=pltpu.CompilerParams(vmem_limit_bytes=VMEM_LIMIT),
@@ -702,27 +805,27 @@
     own_bias = lax.dynamic_slice_in_dim(all_bias, own_block * own_heads, own_heads, 0)[None]
     bias_row = jnp.concatenate([own_bias, own_bias, jnp.zeros((1, 128 - 2 * own_heads), F32)], axis=1)
 
-    def attend_stream(m, table):
-        return attend(table, gathered, m, micro, packed, bias_row, begins[m], own_heads, depth, chunk)
-
-    stream = own.astype(F32)
-    attended = [attend_stream(0, tables[0])]
+    def attend_stream(m, table, into):
+        return attend(table, gathered, m, micro, packed, bias_row, begins[m], into, own_heads, depth, chunk)
+
+    attended = [attend_stream(0, tables[0], None)]
     gains = attended[0][8]
     gated = [attended[0][7]]
     parts = [out_product(gated[0], out_w)]
     table, upstream_own, gains, ffn_w, w_down = tie(tables[1], upstream_own, gains, ffn_w, w_down)
     ffn_w = lax.all_gather(ffn_w, "z", axis=0).reshape(width, 2 * share)
     down_w = lax.all_gather(w_down, "z", axis=0)
-    attended.append(attend_stream(1, table))
+    attended.append(attend_stream(1, table, attended[0][0]))
     upstream = gather_first(upstream_own)
     last_gated, upstream = tie(attended[1][7], upstream)
     gated.append(last_gated)
-    parts.append(out_product(gated[1], out_w))
-    upstream = in_rows(gather_rest(upstream))
+    upstream, last_part = tie(gather_own_core(upstream), out_product(gated[1], out_w))
+    parts.append(last_part)
+    upstream = in_rows(gather_both_cores(upstream))
     gain_one, gain_two = gains[0:1], gains[1:2]
-    middle = stream + scatter_rest(scatter_first([item[0] for item in parts], [item[1] for item in parts]))
-    norm_two = lax.rsqrt(jnp.mean(middle * middle, axis=-1, keepdims=True) + EPS)
-    normed_two = in_rows(gather_plane((middle * norm_two * gain_two).astype(BF16)))
+    state = scatter_first([item[0] for item in parts], [item[1] for item in parts])
+    middle, normed_two = add_and_norm(state[0], received(state, sent(state)), own, gain_two)
+    normed_two = in_rows(gather_plane(normed_two))
 
     half_blocks = normed_two.shape[0] // BQ // 2
     weights = (normed_two, upstream, ffn_w, down_w, unit)
@@ -732,89 +835,82 @@
         kept, _ = tie(normed_two, hold)
         return dot(kept, ffn_grad, ((0,), (0,)), BF16)
 
-    state = scatter_first([far[None]], [near[None]], grad_of_ffn)
+    state = scatter_first([far], [near], grad_of_ffn)
     grad_ffn_w = state[2]
     sends, held = tie(sent(state), activ)
     grad_down = dot(held, upstream, ((0,), (0,)), BF16)
     arrived, grad_ffn = tie(received(state, sends), join_grads(grad_ffn_w, grad_down, nz))
     grad_ffn = scatter_layers(grad_ffn)
-    normed_two_grad = add_up(*state[0], *arrived)
-
-    unit_two = middle * norm_two
-    scaled_two = normed_two_grad * gain_two
-    middle_grad = upstream_own.astype(F32) + norm_two * (
-        scaled_two - unit_two * jnp.mean(scaled_two * unit_two, axis=-1, keepdims=True)
-    )
-    branch_own, held = tie(middle_grad.astype(BF16), activ)
+    middle_grad, branch_own = norm_back(state[0], arrived, upstream_own, middle, gain_two, (F32, BF16))
+    branch_own, held = tie(branch_own, activ)
     half = activ.shape[0] // 2
     down_rows = down_w.reshape(share, width)
-    part_out = [dot(item, down_rows, out=BF16)[None] for item in (held[half:], held[:half])]
+    part_out = [
+        dot(item, down_rows, out=BF16).reshape(plane // 2, -1, width) for item in (held[half:], held[:half])
+    ]
     branch_grad, part_out = tie(gather_first(branch_own), part_out)
     result = scatter_core(part_out[:1], part_out[1:])
     branch_grad = gather_rest(branch_grad)
 
-    def back_stream(m, table, gated):
+    def back_stream(m, table, gated, into):
         return attend_back(
-            table, branch_grad, m, micro, packed, out_w, attended[m][1:7], begins[m], gated, own_heads, depth, chunk
+            table, branch_grad, m, micro, packed, out_w, attended[m][1:7], begins[m], gated, into, own_heads, depth, chunk
         )
 
     def first_back(hold):
         table, _ = tie(tables[0], hold)
-        return back_stream(0, table, gated)
+        return back_stream(0, table, gated, None)
 
     result = scatter_diagonal(*result, first_back)
     backs = [result[2]]
-    grad_packed = dot(attended[0][0], backs[0][0], ((0,), (0,)))
+    sends, table = tie(sent(result), tables[1])
     grad_out = backs[0][4]
     if aligned:
         grad_out = all_to_all(grad_out.reshape(nf, slab, width), ("p", "q"))
-    if aligned:
-        grad_out = scatter_layers(grad_out.reshape(nf * slab, width))
-    table, grad_packed, sends, grad_ffn = tie(tables[1], grad_packed, sent(result), grad_ffn)
-    grad_ffn_w, grad_down = part_grads(grad_ffn, plane * slab, unit, width)
-    arrived, last_back = tie(received(result, sends), back_stream(1, table, None))
+    arrived, grad_out, last_back = tie(received(result, sends), grad_out, back_stream(1, table, None, backs[0][0]))
     backs.append(last_back)
-    result_base, far = tie(result[0], backs[1][1])
-    result = (middle + add_up(*result_base, *arrived)).astype(BF16)
-    output = rows_from_layer(result.reshape(micro, -1, width))
+    grad_packed = dot(attended[1][0], backs[1][0], ((0,), (0,)), BF16)
     bias_sum = sum(item[3][0] for item in backs)
     bias_all = lax.dynamic_update_slice_in_dim(
         jnp.zeros((own_heads * plane,), F32), bias_sum[:own_heads], own_block * own_heads, 0
     )[:heads]
 
-    def grad_of_packed(hold):
-        right, _ = tie(backs[1][0], hold)
-        grad = (grad_packed + dot(attended[1][0], right, ((0,), (0,)))).astype(BF16)
-        return grad, output, total_over("p", total_over("core", bias_all)), grad_down, grad_out
-
-    state = scatter_first([backs[0][1], far], [item[2] for item in backs], grad_of_packed)
-    grad_packed, output, bias_all, grad_down, grad_out = state[2]
+    def rows_of_output(hold):
+        own_arrived, own_bias, _ = tie(arrived, bias_all, hold)
+        rows = add_rows(result[0], own_arrived, middle)
+        return rows, total_over("p", total_over("core", own_bias))
+
+    near, got, last = scatter_core([item[1] for item in backs], [item[2] for item in backs])
+    grad_packed, last, grad_ffn = tie(grad_packed, last, grad_ffn)
     grad_packed = scatter_layers(grad_packed)
-    sends, grad_ffn_w = tie(sent(state), grad_ffn_w)
+    state = scatter_diagonal(near, got, last, rows_of_output)
+    output, bias_all = state[2]
+    output = rows_from_layer(output.reshape(micro, -1, width))
+    sends, grad_ffn = tie(sent(state), grad_ffn)
+    grad_ffn_w, grad_down = part_grads(grad_ffn, plane * slab, unit, width)
     grad_ffn_w = all_to_all(grad_ffn_w.reshape(plane, slab, 2 * share), members)
     arrived, bias_all = tie(received(state, sends), total_over("q", bias_all))
-    normed_grad = add_up(*state[0], *arrived)
-    norm_one = lax.rsqrt(jnp.mean(stream * stream, axis=-1, keepdims=True) + EPS)
-    unit_one = stream * norm_one
-    scaled_one = normed_grad * gain_one
-    stream_grad = middle_grad + norm_one * (
-        scaled_one - unit_one * jnp.mean(scaled_one * unit_one, axis=-1, keepdims=True)
-    )
-    stream_grad, bias_all = tie(stream_grad.astype(BF16), bias_all)
+    (stream_grad,) = norm_back(state[0], arrived, middle_grad, own, gain_one, (BF16,))
+    stream_grad, bias_all = tie(stream_grad, bias_all)
     input_grad = rows_from_layer(stream_grad.reshape(micro, -1, width))
-    input_grad, grad_packed, grad_ffn_w = tie(input_grad, grad_packed, grad_ffn_w)
+    bias_all = bias_all + xor_permute(bias_all, "z", 1)
+    input_grad, grad_packed, bias_all = tie(input_grad, grad_packed, bias_all)
+    if aligned:
+        grad_out, grad_packed = tie(grad_out, grad_packed)
+        grad_out = scatter_layers(grad_out.reshape(nf * slab, width))
     grad_packed = all_to_all(grad_packed.reshape(plane, slab, -1), members)
-    grad_bias = total_over("z", bias_all)
+    input_grad, grad_packed, bias_all = tie(input_grad, grad_packed, bias_all)
+    grad_bias = total_over("z", bias_all, 2)
     returned = rows_from_plane([jnp.concatenate(pair, axis=0) for pair in zip(output, input_grad)])
     output, input_grad = returned[:micro], returned[micro:].astype(F32)
 
+    grad_gate, grad_up, sums_two = unpack_hidden(grad_ffn_w, (w_gate, w_up), nz)
     if not aligned:
         spread = jnp.zeros((own_heads * depth * plane, width), BF16)
         spread = lax.dynamic_update_slice_in_dim(spread, grad_out, own_block * columns, 0)
         grad_out = lax.psum_scatter(spread[:width], everywhere, scatter_dimension=0, tiled=True)
     grad_out = grad_out.astype(F32)
     grad_down = grad_down.astype(F32)
-    grad_gate, grad_up, sums_two = unpack_hidden(grad_ffn_w, (w_gate, w_up), nz)
     grad_query, grad_key, grad_value, grad_outgate, sums_one = unpack_heads(
         grad_packed, (w_query, w_key, w_value, w_outgate), nf, columns
     )

time: 592 us -> 577 us (0.975)
  Pallas kernels: 119 us -> 161 us
  other arithmetic: 55.6 us -> 17.7 us
  waiting for transfers between devices: 213 us -> 190 us
  local copies, waits for them, and re-layouts: 41.5 us -> 52.8 us
  starting transfers between devices: 105 us -> 99 us
    pallas_call x0 -> x12, Pallas kernels: none -> 41.5 us  [rows_kernel(): pl.pallas_call(kernel, grid=(1,), in_specs=[spec for _, spec in operands]...]
    unnamed x141 -> x152, local copies, waits for them, and re-layouts: 16 us -> 34.1 us
    reduce_scatter x3, waiting for transfers between devices: 15.4 us -> 2.66 us  [scatter_layers(): return lax.psum_scatter(grad, 'z', scatter_dimension=0, tiled=True)]
    convert_element_type x5 -> x0, other arithmetic: 10.6 us -> none  [the longest x1 4.05 us: per_device(): branch_own, held = tie(middle_grad.astype(BF16), activ)]
    add x10 -> x1, other arithmetic: 10.5 us -> 0.01 us  [per_device(): bias_all = bias_all + xor_permute(bias_all, 'z', 1)]
    ppermute x78, waiting for transfers between devices: 173 us -> 163 us  [xor_permute(): return lax.ppermute(x, axis, [(i, i ^ step) for i in range(n)])]
    another operation x10 -> x2, other arithmetic: 6.95 us -> 0.36 us
    squeeze x10 -> x0, local copies, waits for them, and re-layouts: 6.45 us -> none  [the longest x8 4.35 us: scatter_diagonal(): item[0]]
  transfers between devices with their start and end apart: 100 -> 100, of which waited for: 40 -> 45; matrix products, arithmetic and copies ran while one was open for 19% -> 15% of each run, Pallas kernels for 18% -> 24%
where the time goes in v3:
time: 577 us; the launch traced here: 572 us
  waiting for transfers between devices  190 us (33%)
  Pallas kernels  161 us (28%)
  starting transfers between devices  99 us (17%)
  local copies, waits for them, and re-layouts  52.8 us (9%)
  matrix products  36.3 us (6%)
  other arithmetic  17.7 us (3%)
  between operations  15.4 us (3%)
    ppermute x78, waiting for transfers between devices, xor_permute(): return lax.ppermute(x, axis, [(i, i ^ step) for i in range(n)])  163 us
    ppermute x78, starting transfers between devices, xor_permute(): return lax.ppermute(x, axis, [(i, i ^ step) for i in range(n)])  63.4 us
    pallas_call x2, Pallas kernels, attend_back(): pl.pallas_call(functools.partial(attend_back_kernel, heads, depth, chunk,...  46.2 us
    pallas_call x12, Pallas kernels, rows_kernel(): pl.pallas_call(kernel, grid=(1,), in_specs=[spec for _, spec in operands]...  41.5 us
    dot_general x6, matrix products, dot(): lax.dot_general(left, right, (contract, ((), ())), preferred_element_type...  34.6 us
    unnamed x152, local copies, waits for them, and re-layouts  34.1 us
    pallas_call x2, Pallas kernels, attend(): pl.pallas_call(functools.partial(attend_kernel, heads, depth, chunk, memb...  30.6 us
    pallas_call x2, Pallas kernels, ffn(): pl.pallas_call(ffn_kernel, grid=(count,), in_specs=[blocks(width, first),...  26.3 us
  transfers between devices with their start and end apart: 100, of which 45 were waited for; matrix products, arithmetic and copies ran while one was open for 15% of the time, Pallas kernels for 24%

profile of v3, /device:TPU:0, one launch (start us, length us, event | category | flops | bytes accessed | tf_op | source)
XLA Modules:
  0.0 572.5 jit_solution(13294090961327741879)
XLA Ops:
  7.2 5.1 collective-permute-start.8
  28.0 4.2 collective-permute-done.3
  39.6 6.1 %collective-permute-done.5 = bf16[2,32,1536]{2,1,0:T(8,128)(2,1)S(1)} collective-permute-done((bf16[2,32,1536]{2,1,0:T(8,128)(2,1)S(1)}, bf16[2,32,1536]{2,1,0:T(8,128)(2,1)S(1)}, u32[]{:S(2)}, u32[]{:S(2)}) %collective-permute-start.5) | collective-permute-done | bytes 196640 | tf_op jit(solution)/shard_map/ppermute | solution.py:24
  45.7 11.1 %collective-permute-done.4 = bf16[2,32,1536]{2,1,0:T(8,128)(2,1)S(1)} collective-permute-done((bf16[2,32,1536]{2,1,0:T(8,128)(2,1)S(1)}, bf16[2,32,1536]{2,1,0:T(8,128)(2,1)S(1)}, u32[]{:S(2)}, u32[]{:S(2)}) %collective-permute-start.4) | collective-permute-done | bytes 196640 | tf_op jit(solution)/shard_map/ppermute | solution.py:24
  67.5 10.9 %collective-permute-done.9.refs_1_ = bf16[256,1536]{1,0:T(8,128)(2,1)} collective-permute-done((bf16[256,1536]{1,0:T(8,128)(2,1)S(1)}, bf16[256,1536]{1,0:T(8,128)(2,1)}, u32[]{:S(2)}, u32[]{:S(2)}) %collective-permute-start.9) | collective-permute-done | bytes 786464 | tf_op jit(solution)/shard_map/ppermute | solution.py:24
  78.4 4.8 collective-permute-done.10.refs_2_
  94.0 4.9 collective-permute-done.11.refs_3_
  101.1 5.2 all-to-all-done.2
  123.5 15.4 %attend.2 = (bf16[2048,1536]{1,0:T(8,128)(2,1)}, bf16[1024,576]{1,0:T(8,128)(2,1)}, f32[1024,192]{1,0:T(8,128)}, f32[1024,128]{1,0:T(8,128)}, f32[1024,192]{1,0:...) custom-call(s32[32]{0:T(128)} %get-tuple-element.299.table, ...), custom_call_target="tpu_custom_call" | custom-call | flops 14000000000 | bytes 10000000 | tf_op jit(solution)/shard_map/attend/pallas_call | solution.py:464
  141.2 15.2 %attend.3 = (bf16[2048,1536]{1,0:T(8,128)(2,1)}, bf16[1024,576]{1,0:T(8,128)(2,1)}, f32[1024,192]{1,0:T(8,128)}, f32[1024,128]{1,0:T(8,128)}, f32[1024,192]{1,0:...) custom-call(s32[32]{0:T(128)} %get-tuple-element.324.table, ...), custom_call_target="tpu_custom_call", output_to_operand_aliasing={{0}: (12, {})} | custom-call | flops 14000000000 | bytes 10000000 | tf_op jit(solution)/shard_map/attend/pallas_call | solution.py:464
  180.7 7.7 %collective-permute-done.31.refs_8_ = bf16[128,1536]{1,0:T(8,128)(2,1)S(1)} collective-permute-done((bf16[128,1536]{1,0:T(8,128)(2,1)}, bf16[128,1536]{1,0:T(8,128)(2,1)S(1)}, u32[]{:S(2)}, u32[]{:S(2)}) %collective-permute-start.31) | collective-permute-done | bytes 393248 | tf_op jit(solution)/shard_map/ppermute | solution.py:24
  199.5 12.6 %collective-permute-done.33.refs_6_ = bf16[256,1536]{1,0:T(8,128)(2,1)S(1)} collective-permute-done((bf16[256,1536]{1,0:T(8,128)(2,1)}, bf16[256,1536]{1,0:T(8,128)(2,1)S(1)}, u32[]{:S(2)}, u32[]{:S(2)}) %collective-permute-start.33) | collective-permute-done | bytes 786464 | tf_op jit(solution)/shard_map/ppermute | solution.py:24
  214.4 4.1 add_norm.1
  223.5 13.3 %collective-permute-done.35 = bf16[256,1536]{1,0:T(8,128)(2,1)S(1)} collective-permute-done((bf16[256,1536]{1,0:T(8,128)(2,1)}, bf16[256,1536]{1,0:T(8,128)(2,1)S(1)}, u32[]{:S(2)}, u32[]{:S(2)}) %collective-permute-start.35) | collective-permute-done | bytes 786464 | tf_op jit(solution)/shard_map/ppermute | solution.py:24
  241.2 4.6 collective-permute-done.37
  252.3 13.2 %ffn.2 = (bf16[2048,512]{1,0:T(8,128)(2,1)}, bf16[2048,1024]{1,0:T(8,128)(2,1)}, bf16[4,256,1536]{2,1,0:T(8,128)(2,1)}) custom-call(bf16[2048,1536]{1,0:T(8,128)(2,1)} %constant_dynamic-update-slice_fusion.h_ref, bf16[2048,1536]{1,0:T(8,128)(2,1)} %constant_dynamic-update-slice_fusion.10.e_ref, bf16[1536,1024]{1,0:T(8,128)(2,1)} %bitcast.204, ...), custom_call_target="tpu_custom_call" | custom-call | flops 8053063680 | bytes 12582912 | tf_op jit(solution)/shard_map/ffn/pallas_call | solution.py:576
  265.5 13.1 %ffn.3 = (bf16[2048,512]{1,0:T(8,128)(2,1)}, bf16[2048,1024]{1,0:T(8,128)(2,1)}, bf16[4,256,1536]{2,1,0:T(8,128)(2,1)}) custom-call(bf16[2048,1536]{1,0:T(8,128)(2,1)} %constant_dynamic-update-slice_fusion.h_ref, bf16[2048,1536]{1,0:T(8,128)(2,1)} %constant_dynamic-update-slice_fusion.10.e_ref, ...), custom_call_target="tpu_custom_call", output_to_operand_aliasing={{0}: (4, {}), {1}: (5, {})} | custom-call | flops 8053063680 | bytes 12582912 | tf_op jit(solution)/shard_map/ffn/pallas_call | solution.py:576
  284.9 8.9 %fusion.53 = bf16[1536,1024]{1,0:T(8,128)(2,1)S(1)} fusion(bf16[2048,1536]{1,0:T(8,128)(2,1)} %constant_dynamic-update-slice_fusion.h_ref, bf16[2048,1024]{1,0:T(8,128)(2,1)S(1)} %copy-done.66), kind=kOutput, calls=%fused_computation.189 | convolution fusion | flops 6442450944 | bytes 13631488 | tf_op jit(solution)/shard_map/dot_general | solution.py:19
  301.6 6.3 %fusion.54 = bf16[512,1536]{1,0:T(8,128)(2,1)S(1)} fusion(bf16[2048,512]{1,0:T(8,128)(2,1)S(1)} %copy-done.17, bf16[2048,1536]{1,0:T(8,128)(2,1)} %constant_dynamic-update-slice_fusion.10.e_ref), kind=kOutput, calls=%fused_computation.190 | convolution fusion | flops 3221225472 | bytes 9961472 | tf_op jit(solution)/shard_map/dot_general | solution.py:19
  310.8 8.0 %collective-permute-done.52.refs_5_ = bf16[256,1536]{1,0:T(8,128)(2,1)S(1)} collective-permute-done((bf16[256,1536]{1,0:T(8,128)(2,1)}, bf16[256,1536]{1,0:T(8,128)(2,1)S(1)}, u32[]{:S(2)}, u32[]{:S(2)}) %collective-permute-start.52) | collective-permute-done | bytes 786464 | tf_op jit(solution)/shard_map/ppermute | solution.py:24
  319.8 5.2 norm_back.2
  336.1 7.5 %collective-permute-done.54.refs_1_.refs_9_ = bf16[256,1536]{1,0:T(8,128)(2,1)} collective-permute-done((bf16[256,1536]{1,0:T(8,128)(2,1)}, bf16[256,1536]{1,0:T(8,128)(2,1)}, u32[]{:S(2)}, u32[]{:S(2)}) %collective-permute-start.54) | collective-permute-done | bytes 786464 | tf_op jit(solution)/shard_map/ppermute | solution.py:24
  348.8 8.2 %collective-permute-done.59.refs_3_ = bf16[128,1536]{1,0:T(8,128)(2,1)S(1)} collective-permute-done((bf16[128,1536]{1,0:T(8,128)(2,1)S(1)}, bf16[128,1536]{1,0:T(8,128)(2,1)S(1)}, u32[]{:S(2)}, u32[]{:S(2)}) %collective-permute-start.59) | collective-permute-done | bytes 393248 | tf_op jit(solution)/shard_map/ppermute | solution.py:24
  366.6 25.1 %attend_back.2 = (bf16[2048,896]{1,0:T(8,128)(2,1)}, bf16[4,128,1536]{2,1,0:T(8,128)(2,1)}, bf16[4,128,1536]{2,1,0:T(8,128)(2,1)}, f32[8,128]{1,0:T(8,128)}, bf16[192,1536]{1,0:T(8,128)(2,1)}) custom-call(s32[32]{0:T(128)} %get-tuple-element.299.table, bf16[256,1536]{1,0:T(8,128)(2,1)} %get-tuple-element.300.refs_0_.refs_8_, ...), custom_call_target="tpu_custom_call" | custom-call | flops 20000000000 | bytes 10000000 | tf_op jit(solution)/shard_map/attend_back/pallas_call | solution.py:502
  401.8 21.1 %attend_back.3 = (bf16[2048,896]{1,0:T(8,128)(2,1)}, bf16[4,128,1536]{2,1,0:T(8,128)(2,1)}, bf16[4,128,1536]{2,1,0:T(8,128)(2,1)}, f32[8,128]{1,0:T(8,128)}) custom-call(s32[32]{0:T(128)} %get-tuple-element.324.table, bf16[256,1536]{1,0:T(8,128)(2,1)} %get-tuple-element.300.refs_0_.refs_8_, ...), custom_call_target="tpu_custom_call", output_to_operand_aliasing={{0}: (18, {})} | custom-call | flops 20000000000 | bytes 10000000 | tf_op jit(solution)/shard_map/attend_back/pallas_call | solution.py:502
  424.6 11.1 %fusion.55 = bf16[1536,896]{1,0:T(8,128)(2,1)} fusion(bf16[2048,1536]{1,0:T(8,128)(2,1)} %get-tuple-element.339, bf16[2048,896]{1,0:T(8,128)(2,1)} %get-tuple-element.340), kind=kOutput, calls=%fused_computation.191 | convolution fusion | flops 5637144576 | bytes 12713984 | tf_op jit(solution)/shard_map/dot_general | solution.py:19
  465.2 13.1 %collective-permute-done.76 = f32[24]{0:T(128)S(1)} collective-permute-done((f32[24]{0:T(128)S(1)}, f32[24]{0:T(128)S(1)}, u32[]{:S(2)}, u32[]{:S(2)}) %collective-permute-start.76) | collective-permute-done | bytes 128 | tf_op jit(solution)/shard_map/ppermute | solution.py:24
  479.6 4.7 norm_back.3
  490.9 13.1 %collective-permute-done.80 = f32[24]{0:T(128)S(1)} collective-permute-done((f32[24]{0:T(128)S(1)}, f32[24]{0:T(128)S(1)}, u32[]{:S(2)}, u32[]{:S(2)}) %collective-permute-start.80) | collective-permute-done | bytes 128 | tf_op jit(solution)/shard_map/ppermute | solution.py:24
  508.1 4.7 all-to-all-start.4
  525.1 10.7 %collective-permute-done.82 = bf16[2,32,1536]{2,1,0:T(8,128)(2,1)} collective-permute-done((bf16[2,32,1536]{2,1,0:T(8,128)(2,1)}, bf16[2,32,1536]{2,1,0:T(8,128)(2,1)}, u32[]{:S(2)}, u32[]{:S(2)}) %collective-permute-start.82) | collective-permute-done | bytes 196640 | tf_op jit(solution)/shard_map/ppermute | solution.py:24
  551.3 7.5 %collective-permute-done.85 = bf16[4,32,1536]{2,1,0:T(8,128)(2,1)S(1)} collective-permute-done((bf16[4,32,1536]{2,1,0:T(8,128)(2,1)S(1)}, bf16[4,32,1536]{2,1,0:T(8,128)(2,1)S(1)}, u32[]{:S(2)}, u32[]{:S(2)}) %collective-permute-start.85) | collective-permute-done | bytes 393248 | tf_op jit(solution)/shard_map/ppermute | solution.py:33
  (436 shorter events, 250.6 us)
Async XLA Ops:
  32.2 24.6 %all-to-all-start = ((bf16[8,48,896]{2,1,0:T(8,128)(2,1)}), bf16[8,48,896]{2,1,0:T(8,128)(2,1)S(1)}, u32[]{:S(2)}, u32[]{:S(2)}) async-start(bf16[8,48,896]{2,1,0:T(8,128)(2,1)} %layout.4), calls=%async_computation | async-start | bytes 1376256 | tf_op jit(solution)/shard_map/all_to_all | solution.py:689
  35.9 83.0 %all-gather.7.cloned.1.call-start = ((), (), s32[]{:S(2)}) async-start(), calls=%async_computation.12 | async-start | bytes 3440640 | tf_op jit(solution)/shard_map/all_gather | solution.py:772
  57.8 20.6 %collective-permute-start.9 = (bf16[256,1536]{1,0:T(8,128)(2,1)S(1)}, bf16[256,1536]{1,0:T(8,128)(2,1)}, u32[]{:S(2)}, u32[]{:S(2)}) collective-permute-start(bf16[256,1536]{1,0:T(8,128)(2,1)S(1)} %bitcast.155), channel_id=1, source_target_pairs={{0,1},{1,0},{2,3},{3,2},{4,5},{5,4},{6,7},{7,6},{8,9},{9,8},{10,11... | collective-permute-start | bytes 2359304 | tf_op jit(solution)/shard_map/ppermute | solution.py:24
  59.5 23.6 %collective-permute-start.10 = (bf16[256,1536]{1,0:T(8,128)(2,1)S(1)}, bf16[256,1536]{1,0:T(8,128)(2,1)}, u32[]{:S(2)}, u32[]{:S(2)}) collective-permute-start(bf16[256,1536]{1,0:T(8,128)(2,1)S(1)} %bitcast.156), channel_id=1, source_target_pairs={{0,2},{2,0},{1,3},{3,1},{4,6},{6,4},{5,7},{7,5},{8,10},{10,8},{9,1... | collective-permute-start | bytes 2359304 | tf_op jit(solution)/shard_map/ppermute | solution.py:24
  61.0 27.1 %all-to-all-start.1 = ((bf16[4,48,1536]{2,1,0:T(8,128)(2,1)}), bf16[4,48,1536]{2,1,0:T(8,128)(2,1)S(1)}, u32[]{:S(2)}, u32[]{:S(2)}) async-start(bf16[4,48,1536]{2,1,0:T(8,128)(2,1)} %pad_maximum_fusion.8), calls=%async_computation.1 | async-start | bytes 1179648 | tf_op jit(solution)/shard_map/all_to_all | solution.py:689
  64.5 23.5 %collective-permute-start.24 = (s32[2,4]{1,0:T(2,128)S(1)}, s32[2,4]{1,0:T(2,128)S(1)}, u32[]{:S(2)}, u32[]{:S(2)}) collective-permute-start(s32[2,4]{1,0:T(2,128)S(1)} %bitcast.212), channel_id=1, source_target_pairs={{0,0},{8,1},{16,2},{24,3},{4,4},{12,5},{20,6},{28,7},{1,8},{9,9},{... | collective-permute-start | bytes 104 | tf_op jit(solution)/shard_map/ppermute | solution.py:784
  84.9 21.3 %collective-permute-start.14 = (bf16[256,1536]{1,0:T(8,128)(2,1)}, bf16[256,1536]{1,0:T(8,128)(2,1)}, u32[]{:S(2)}, u32[]{:S(2)}) collective-permute-start(bf16[256,1536]{1,0:T(8,128)(2,1)} %collective-permute-done.9.refs_1_), channel_id=1, source_target_pairs={{0,4},{4,0},{1,5},{5,1},{2,6},{6,2},{3,7},{7,3},{8,12},{12,8},{9,1... | collective-permute-start | bytes 2359304 | tf_op jit(solution)/shard_map/ppermute | solution.py:24
  86.0 20.2 %collective-permute-start.15 = (bf16[256,1536]{1,0:T(8,128)(2,1)}, bf16[256,1536]{1,0:T(8,128)(2,1)}, u32[]{:S(2)}, u32[]{:S(2)}) collective-permute-start(bf16[256,1536]{1,0:T(8,128)(2,1)} %collective-permute-done.10.refs_2_), channel_id=1, source_target_pairs={{0,4},{4,0},{1,5},{5,1},{2,6},{6,2},{3,7},{7,3},{8,12},{12,8},{9,1... | collective-permute-start | bytes 2359304 | tf_op jit(solution)/shard_map/ppermute | solution.py:24
  91.7 160.7 %all-gather.11.cloned.1.call-start = ((), (), s32[]{:S(2)}) async-start(), calls=%async_computation.14 | async-start | bytes 1966080 | tf_op jit(solution)/shard_map/all_gather | solution.py:817
  119.0 19.8 %collective-permute-start.23 = (bf16[2,32,1536]{2,1,0:T(8,128)(2,1)S(1)}, bf16[2,32,1536]{2,1,0:T(8,128)(2,1)S(1)}, u32[]{:S(2)}, u32[]{:S(2)}) collective-permute-start(bf16[2,32,1536]{2,1,0:T(8,128)(2,1)S(1)} %get-tuple-element.422), channel_id=1, source_target_pairs={{0,24},{8,16},{16,8},{24,0},{1,25},{9,17},{17,9},{25,1},{2,26},{10... | collective-permute-start | bytes 589832 | tf_op jit(solution)/shard_map/ppermute | solution.py:24
  140.7 111.6 %all-gather.9.cloned.1.call-start = ((), (), s32[]{:S(2)}) async-start(), calls=%async_computation.13 | async-start | bytes 3932160 | tf_op jit(solution)/shard_map/all_gather | solution.py:816
  168.7 271.5 %reduce-scatter.4.cloned.1.call-start = ((), (), s32[]{:S(2)}) async-start(), calls=%async_computation.9 | async-start | bytes 5898240 | tf_op jit(solution)/shard_map/reduce_scatter | solution.py:693
  172.5 24.6 %collective-permute-start.44 = (bf16[256,1536]{1,0:T(8,128)(2,1)}, bf16[256,1536]{1,0:T(8,128)(2,1)S(1)}, u32[]{:S(2)}, u32[]{:S(2)}) collective-permute-start(bf16[256,1536]{1,0:T(8,128)(2,1)} %bitcast.165), channel_id=1, source_target_pairs={{0,4},{4,0},{1,5},{5,1},{2,6},{6,2},{3,7},{7,3},{8,12},{12,8},{9,1... | collective-permute-start | bytes 2359304 | tf_op jit(solution)/shard_map/ppermute | solution.py:24
  172.5 25.6 %collective-permute-start.45 = (bf16[256,1536]{1,0:T(8,128)(2,1)}, bf16[256,1536]{1,0:T(8,128)(2,1)S(1)}, u32[]{:S(2)}, u32[]{:S(2)}) collective-permute-start(bf16[256,1536]{1,0:T(8,128)(2,1)} %copy-done.20), channel_id=1, source_target_pairs={{0,4},{4,0},{1,5},{5,1},{2,6},{6,2},{3,7},{7,3},{8,12},{12,8},{9,1... | collective-permute-start | bytes 2359304 | tf_op jit(solution)/shard_map/ppermute | solution.py:24
  179.8 40.3 %collective-permute-start.46 = (bf16[256,1536]{1,0:T(8,128)(2,1)S(1)}, bf16[256,1536]{1,0:T(8,128)(2,1)S(1)}, u32[]{:S(2)}, u32[]{:S(2)}) collective-permute-start(bf16[256,1536]{1,0:T(8,128)(2,1)S(1)} %copy-done.19), channel_id=1, source_target_pairs={{0,4},{4,0},{1,5},{5,1},{2,6},{6,2},{3,7},{7,3},{8,12},{12,8},{9,1... | collective-permute-start | bytes 2359304 | tf_op jit(solution)/shard_map/ppermute | solution.py:24
  197.1 23.9 %collective-permute-start.47 = (bf16[128,1536]{1,0:T(8,128)(2,1)S(1)}, bf16[128,1536]{1,0:T(8,128)(2,1)S(1)}, u32[]{:S(2)}, u32[]{:S(2)}) collective-permute-start(bf16[128,1536]{1,0:T(8,128)(2,1)S(1)} %copy-done.42), channel_id=1, source_target_pairs={{0,4},{4,0},{1,5},{5,1},{2,6},{6,2},{3,7},{7,3},{8,12},{12,8},{9,1... | collective-permute-start | bytes 1179656 | tf_op jit(solution)/shard_map/ppermute | solution.py:24
  198.1 23.7 %collective-permute-start.48 = (bf16[128,1536]{1,0:T(8,128)(2,1)S(1)}, bf16[128,1536]{1,0:T(8,128)(2,1)S(1)}, u32[]{:S(2)}, u32[]{:S(2)}) collective-permute-start(bf16[128,1536]{1,0:T(8,128)(2,1)S(1)} %collective-permute-done.28), channel_id=1, source_target_pairs={{0,4},{4,0},{1,5},{5,1},{2,6},{6,2},{3,7},{7,3},{8,12},{12,8},{9,1... | collective-permute-start | bytes 1179656 | tf_op jit(solution)/shard_map/ppermute | solution.py:24
  222.6 25.3 %collective-permute-start.39 = (bf16[256,1536]{1,0:T(8,128)(2,1)S(1)}, bf16[256,1536]{1,0:T(8,128)(2,1)S(1)}, u32[]{:S(2)}, u32[]{:S(2)}) collective-permute-start(bf16[256,1536]{1,0:T(8,128)(2,1)S(1)} %copy-done.29), channel_id=1, source_target_pairs={{0,4},{4,0},{1,5},{5,1},{2,6},{6,2},{3,7},{7,3},{8,12},{12,8},{9,1... | collective-permute-start | bytes 2359304 | tf_op jit(solution)/shard_map/ppermute | solution.py:24
  299.4 19.4 %collective-permute-start.52 = (bf16[256,1536]{1,0:T(8,128)(2,1)}, bf16[256,1536]{1,0:T(8,128)(2,1)S(1)}, u32[]{:S(2)}, u32[]{:S(2)}) collective-permute-start(bf16[256,1536]{1,0:T(8,128)(2,1)} %get-tuple-element.284), channel_id=1, source_target_pairs={{0,1},{1,0},{2,3},{3,2},{4,5},{5,4},{6,7},{7,6},{8,9},{9,8},{10,11... | collective-permute-start | bytes 2359304 | tf_op jit(solution)/shard_map/ppermute | solution.py:24
  363.3 28.4 %collective-permute-start.57 = (bf16[128,1536]{1,0:T(8,128)(2,1)}, bf16[128,1536]{1,0:T(8,128)(2,1)S(1)}, u32[]{:S(2)}, u32[]{:S(2)}) collective-permute-start(bf16[128,1536]{1,0:T(8,128)(2,1)} %get-tuple-element.297), channel_id=1, source_target_pairs={{0,2},{2,0},{1,3},{3,1},{4,6},{6,4},{5,7},{7,5},{8,10},{10,8},{9,1... | collective-permute-start | bytes 1179656 | tf_op jit(solution)/shard_map/ppermute | solution.py:24
  364.5 27.2 %collective-permute-start.58 = (bf16[128,1536]{1,0:T(8,128)(2,1)}, bf16[128,1536]{1,0:T(8,128)(2,1)S(1)}, u32[]{:S(2)}, u32[]{:S(2)}) collective-permute-start(bf16[128,1536]{1,0:T(8,128)(2,1)} %get-tuple-element.298), channel_id=1, source_target_pairs={{0,1},{1,0},{2,3},{3,2},{4,5},{5,4},{6,7},{7,6},{8,9},{9,8},{10,11... | collective-permute-start | bytes 1179656 | tf_op jit(solution)/shard_map/ppermute | solution.py:24
  396.1 26.8 %collective-permute-start.66 = (bf16[256,1536]{1,0:T(8,128)(2,1)}, bf16[256,1536]{1,0:T(8,128)(2,1)S(1)}, u32[]{:S(2)}, u32[]{:S(2)}) collective-permute-start(bf16[256,1536]{1,0:T(8,128)(2,1)} %get-tuple-element.321), channel_id=1, source_target_pairs={{0,1},{1,0},{2,3},{3,2},{4,5},{5,4},{6,7},{7,6},{8,9},{9,8},{10,11... | collective-permute-start | bytes 2359304 | tf_op jit(solution)/shard_map/ppermute | solution.py:24
  397.3 25.7 %collective-permute-start.67 = (bf16[256,1536]{1,0:T(8,128)(2,1)}, bf16[256,1536]{1,0:T(8,128)(2,1)}, u32[]{:S(2)}, u32[]{:S(2)}) collective-permute-start(bf16[256,1536]{1,0:T(8,128)(2,1)} %get-tuple-element.322), channel_id=1, source_target_pairs={{0,2},{2,0},{1,3},{3,1},{4,6},{6,4},{5,7},{7,5},{8,10},{10,8},{9,1... | collective-permute-start | bytes 2359304 | tf_op jit(solution)/shard_map/ppermute | solution.py:24
  398.1 24.9 %all-to-all-start.3 = ((bf16[4,48,1536]{2,1,0:T(8,128)(2,1)}), bf16[4,48,1536]{2,1,0:T(8,128)(2,1)S(1)}, u32[]{:S(2)}, u32[]{:S(2)}) async-start(bf16[4,48,1536]{2,1,0:T(8,128)(2,1)} %bitcast.60), calls=%async_computation.3 | async-start | bytes 1179648 | tf_op jit(solution)/shard_map/all_to_all | solution.py:689
  401.5 106.6 %reduce-scatter.6.cloned.1.call-start = ((), (), s32[]{:S(2)}) async-start(), calls=%async_computation.10 | async-start | bytes 3440640 | tf_op jit(solution)/shard_map/reduce_scatter | solution.py:693
  401.8 33.9 %collective-permute-start.68 = (bf16[4,128,1536]{2,1,0:T(8,128)(2,1)}, bf16[4,128,1536]{2,1,0:T(8,128)(2,1)S(1)}, u32[]{:S(2)}, u32[]{:S(2)}) collective-permute-start(bf16[4,128,1536]{2,1,0:T(8,128)(2,1)} %get-tuple-element.337), channel_id=1, source_target_pairs={{0,4},{4,0},{1,5},{5,1},{2,6},{6,2},{3,7},{7,3},{8,12},{12,8},{9,1... | collective-permute-start | bytes 4718600 | tf_op jit(solution)/shard_map/ppermute | solution.py:24
  457.5 20.8 %collective-permute-start.74 = (bf16[256,1536]{1,0:T(8,128)(2,1)}, bf16[256,1536]{1,0:T(8,128)(2,1)S(1)}, u32[]{:S(2)}, u32[]{:S(2)}) collective-permute-start(bf16[256,1536]{1,0:T(8,128)(2,1)} %get-tuple-element.366), channel_id=1, source_target_pairs={{0,1},{1,0},{2,3},{3,2},{4,5},{5,4},{6,7},{7,6},{8,9},{9,8},{10,11... | collective-permute-start | bytes 2359304 | tf_op jit(solution)/shard_map/ppermute | solution.py:24
  459.0 20.6 %collective-permute-start.75 = (bf16[256,1536]{1,0:T(8,128)(2,1)}, bf16[256,1536]{1,0:T(8,128)(2,1)}, u32[]{:S(2)}, u32[]{:S(2)}) collective-permute-start(bf16[256,1536]{1,0:T(8,128)(2,1)} %get-tuple-element.367), channel_id=1, source_target_pairs={{0,2},{2,0},{1,3},{3,1},{4,6},{6,4},{5,7},{7,5},{8,10},{10,8},{9,1... | collective-permute-start | bytes 2359304 | tf_op jit(solution)/shard_map/ppermute | solution.py:24
  461.6 46.5 %all-to-all-start.5 = ((bf16[8,48,1024]{2,1,0:T(8,128)(2,1)}), bf16[8,48,1024]{2,1,0:T(8,128)(2,1)S(1)}, u32[]{:S(2)}, u32[]{:S(2)}) async-start(bf16[8,48,1024]{2,1,0:T(8,128)(2,1)} %bitcast.85), calls=%async_computation.8 | async-start | bytes 1572864 | tf_op jit(solution)/shard_map/all_to_all | solution.py:689
  512.8 51.0 %reduce-scatter.8.cloned.1.call-start = ((), (), s32[]{:S(2)}) async-start(), calls=%async_computation.11 | async-start | bytes 737280 | tf_op jit(solution)/shard_map/reduce_scatter | solution.py:693
  515.6 20.2 %collective-permute-start.82 = (bf16[2,32,1536]{2,1,0:T(8,128)(2,1)}, bf16[2,32,1536]{2,1,0:T(8,128)(2,1)}, u32[]{:S(2)}, u32[]{:S(2)}) collective-permute-start(bf16[2,32,1536]{2,1,0:T(8,128)(2,1)} %get-tuple-element.415), channel_id=1, source_target_pairs={{0,16},{8,24},{16,0},{24,8},{1,17},{9,25},{17,1},{25,9},{2,18},{10... | collective-permute-start | bytes 589832 | tf_op jit(solution)/shard_map/ppermute | solution.py:24
  517.7 19.2 %collective-permute-start.81 = (bf16[2,32,1536]{2,1,0:T(8,128)(2,1)}, bf16[2,32,1536]{2,1,0:T(8,128)(2,1)}, u32[]{:S(2)}, u32[]{:S(2)}) collective-permute-start(bf16[2,32,1536]{2,1,0:T(8,128)(2,1)} %get-tuple-element.416), channel_id=1, source_target_pairs={{0,8},{8,0},{16,24},{24,16},{1,9},{9,1},{17,25},{25,17},{2,10},{10... | collective-permute-start | bytes 589832 | tf_op jit(solution)/shard_map/ppermute | solution.py:24
  (135 other events, 1485.8 us)
Sparse Core Ops, SparseCore 0:
  57.9 57.4 all-gather.6
  140.8 36.4 all-gather.10
  178.9 62.3 all-gather.8
  328.3 84.2 reduce-scatter.3
  440.4 60.8 reduce-scatter.5
  542.6 21.1 reduce-scatter.7

commit v4 on v3

--- a/solution.py
+++ b/solution.py
@@ -878,30 +878,28 @@
     def rows_of_output(hold):
         own_arrived, own_bias, _ = tie(arrived, bias_all, hold)
         rows = add_rows(result[0], own_arrived, middle)
-        return rows, total_over("p", total_over("core", own_bias))
+        own_bias = total_over("core", own_bias)
+        return rows, own_bias + xor_permute(own_bias, "z", 1)
 
     near, got, last = scatter_core([item[1] for item in backs], [item[2] for item in backs])
     grad_packed, last, grad_ffn = tie(grad_packed, last, grad_ffn)
     grad_packed = scatter_layers(grad_packed)
     state = scatter_diagonal(near, got, last, rows_of_output)
     output, bias_all = state[2]
-    output = rows_from_layer(output.reshape(micro, -1, width))
-    sends, grad_ffn = tie(sent(state), grad_ffn)
+    sends, grad_ffn, grad_out = tie(sent(state), grad_ffn, grad_out)
     grad_ffn_w, grad_down = part_grads(grad_ffn, plane * slab, unit, width)
     grad_ffn_w = all_to_all(grad_ffn_w.reshape(plane, slab, 2 * share), members)
-    arrived, bias_all = tie(received(state, sends), total_over("q", bias_all))
+    arrived, bias_all = tie(received(state, sends), total_over("z", bias_all, 2))
     (stream_grad,) = norm_back(state[0], arrived, middle_grad, own, gain_one, (BF16,))
     stream_grad, bias_all = tie(stream_grad, bias_all)
-    input_grad = rows_from_layer(stream_grad.reshape(micro, -1, width))
-    bias_all = bias_all + xor_permute(bias_all, "z", 1)
-    input_grad, grad_packed, bias_all = tie(input_grad, grad_packed, bias_all)
+    returned = jnp.concatenate([output, stream_grad], axis=0).reshape(2 * micro, -1, width)
+    returned = rows_from_layer(returned)
+    grad_bias = total_over("q", total_over("p", bias_all))
+    returned, grad_packed, grad_bias, grad_out = tie(returned, grad_packed, grad_bias, grad_out)
     if aligned:
-        grad_out, grad_packed = tie(grad_out, grad_packed)
         grad_out = scatter_layers(grad_out.reshape(nf * slab, width))
     grad_packed = all_to_all(grad_packed.reshape(plane, slab, -1), members)
-    input_grad, grad_packed, bias_all = tie(input_grad, grad_packed, bias_all)
-    grad_bias = total_over("z", bias_all, 2)
-    returned = rows_from_plane([jnp.concatenate(pair, axis=0) for pair in zip(output, input_grad)])
+    returned, grad_packed = tie(rows_from_plane(returned), grad_packed)
     output, input_grad = returned[:micro], returned[micro:].astype(F32)
 
     grad_gate, grad_up, sums_two = unpack_hidden(grad_ffn_w, (w_gate, w_up), nz)

time: 577 us -> 579 us (level)
  waiting for transfers between devices: 190 us -> 197 us
    reduce_scatter x3, waiting for transfers between devices: 2.66 us -> 9.4 us  [scatter_layers(): return lax.psum_scatter(grad, 'z', scatter_dimension=0, tiled=True)]
    ppermute x78 -> x75, waiting for transfers between devices: 163 us -> 160 us  [xor_permute(): return lax.ppermute(x, axis, [(i, i ^ step) for i in range(n)])]
    ppermute x78 -> x75, starting transfers between devices: 63.4 us -> 61.1 us  [xor_permute(): return lax.ppermute(x, axis, [(i, i ^ step) for i in range(n)])]
    unnamed x152 -> x150, local copies, waits for them, and re-layouts: 34.1 us -> 35.3 us
  transfers between devices with their start and end apart: 100 -> 97, of which waited for: 45 -> 44; matrix products, arithmetic and copies ran while one was open for 15% -> 15% of each run, Pallas kernels for 24% -> 24%
where the time goes in v4:
time: 579 us; the launch traced here: 575 us
  waiting for transfers between devices  197 us (34%)
  Pallas kernels  161 us (28%)
  starting transfers between devices  95.7 us (17%)
  local copies, waits for them, and re-layouts  52.7 us (9%)
  matrix products  36.3 us (6%)
  other arithmetic  16.7 us (3%)
  between operations  15.3 us (3%)
    ppermute x75, waiting for transfers between devices, xor_permute(): return lax.ppermute(x, axis, [(i, i ^ step) for i in range(n)])  160 us
    ppermute x75, starting transfers between devices, xor_permute(): return lax.ppermute(x, axis, [(i, i ^ step) for i in range(n)])  61.1 us
    pallas_call x2, Pallas kernels, attend_back(): pl.pallas_call(functools.partial(attend_back_kernel, heads, depth, chunk,...  46.3 us
    pallas_call x12, Pallas kernels, rows_kernel(): pl.pallas_call(kernel, grid=(1,), in_specs=[spec for _, spec in operands]...  41.7 us
    unnamed x150, local copies, waits for them, and re-layouts  35.3 us
    dot_general x6, matrix products, dot(): lax.dot_general(left, right, (contract, ((), ())), preferred_element_type...  34.7 us
    pallas_call x2, Pallas kernels, attend(): pl.pallas_call(functools.partial(attend_kernel, heads, depth, chunk, memb...  30.6 us
    pallas_call x2, Pallas kernels, ffn(): pl.pallas_call(ffn_kernel, grid=(count,), in_specs=[blocks(width, first),...  26.3 us
  transfers between devices with their start and end apart: 97, of which 44 were waited for; matrix products, arithmetic and copies ran while one was open for 15% of the time, Pallas kernels for 24%

profile of v4, /device:TPU:0, one launch (start us, length us, event | category | flops | bytes accessed | tf_op | source)
XLA Modules:
  0.0 574.5 jit_solution(16296206451722126135)
XLA Ops:
  7.2 5.1 collective-permute-start.8
  28.0 4.2 collective-permute-done.3
  39.6 6.1 %collective-permute-done.5 = bf16[2,32,1536]{2,1,0:T(8,128)(2,1)S(1)} collective-permute-done((bf16[2,32,1536]{2,1,0:T(8,128)(2,1)S(1)}, bf16[2,32,1536]{2,1,0:T(8,128)(2,1)S(1)}, u32[]{:S(2)}, u32[]{:S(2)}) %collective-permute-start.5) | collective-permute-done | bytes 196640 | tf_op jit(solution)/shard_map/ppermute | solution.py:24
  45.7 11.1 %collective-permute-done.4 = bf16[2,32,1536]{2,1,0:T(8,128)(2,1)S(1)} collective-permute-done((bf16[2,32,1536]{2,1,0:T(8,128)(2,1)S(1)}, bf16[2,32,1536]{2,1,0:T(8,128)(2,1)S(1)}, u32[]{:S(2)}, u32[]{:S(2)}) %collective-permute-start.4) | collective-permute-done | bytes 196640 | tf_op jit(solution)/shard_map/ppermute | solution.py:24
  67.5 10.9 %collective-permute-done.9.refs_1_ = bf16[256,1536]{1,0:T(8,128)(2,1)} collective-permute-done((bf16[256,1536]{1,0:T(8,128)(2,1)S(1)}, bf16[256,1536]{1,0:T(8,128)(2,1)}, u32[]{:S(2)}, u32[]{:S(2)}) %collective-permute-start.9) | collective-permute-done | bytes 786464 | tf_op jit(solution)/shard_map/ppermute | solution.py:24
  78.4 4.8 collective-permute-done.10.refs_2_
  94.0 4.9 collective-permute-done.11.refs_3_
  101.1 5.2 all-to-all-done.2
  123.5 15.4 %attend.2 = (bf16[2048,1536]{1,0:T(8,128)(2,1)}, bf16[1024,576]{1,0:T(8,128)(2,1)}, f32[1024,192]{1,0:T(8,128)}, f32[1024,128]{1,0:T(8,128)}, f32[1024,192]{1,0:...) custom-call(s32[32]{0:T(128)} %get-tuple-element.295.table, ...), custom_call_target="tpu_custom_call" | custom-call | flops 14000000000 | bytes 10000000 | tf_op jit(solution)/shard_map/attend/pallas_call | solution.py:464
  141.2 15.2 %attend.3 = (bf16[2048,1536]{1,0:T(8,128)(2,1)}, bf16[1024,576]{1,0:T(8,128)(2,1)}, f32[1024,192]{1,0:T(8,128)}, f32[1024,128]{1,0:T(8,128)}, f32[1024,192]{1,0:...) custom-call(s32[32]{0:T(128)} %get-tuple-element.320.table, ...), custom_call_target="tpu_custom_call", output_to_operand_aliasing={{0}: (12, {})} | custom-call | flops 14000000000 | bytes 10000000 | tf_op jit(solution)/shard_map/attend/pallas_call | solution.py:464
  180.7 7.6 %collective-permute-done.31.refs_8_ = bf16[128,1536]{1,0:T(8,128)(2,1)S(1)} collective-permute-done((bf16[128,1536]{1,0:T(8,128)(2,1)}, bf16[128,1536]{1,0:T(8,128)(2,1)S(1)}, u32[]{:S(2)}, u32[]{:S(2)}) %collective-permute-start.31) | collective-permute-done | bytes 393248 | tf_op jit(solution)/shard_map/ppermute | solution.py:24
  199.6 12.6 %collective-permute-done.33.refs_6_ = bf16[256,1536]{1,0:T(8,128)(2,1)S(1)} collective-permute-done((bf16[256,1536]{1,0:T(8,128)(2,1)}, bf16[256,1536]{1,0:T(8,128)(2,1)S(1)}, u32[]{:S(2)}, u32[]{:S(2)}) %collective-permute-start.33) | collective-permute-done | bytes 786464 | tf_op jit(solution)/shard_map/ppermute | solution.py:24
  223.6 13.2 %collective-permute-done.35 = bf16[256,1536]{1,0:T(8,128)(2,1)S(1)} collective-permute-done((bf16[256,1536]{1,0:T(8,128)(2,1)}, bf16[256,1536]{1,0:T(8,128)(2,1)S(1)}, u32[]{:S(2)}, u32[]{:S(2)}) %collective-permute-start.35) | collective-permute-done | bytes 786464 | tf_op jit(solution)/shard_map/ppermute | solution.py:24
  241.3 4.6 collective-permute-done.37
  252.4 13.2 %ffn.2 = (bf16[2048,512]{1,0:T(8,128)(2,1)}, bf16[2048,1024]{1,0:T(8,128)(2,1)}, bf16[4,256,1536]{2,1,0:T(8,128)(2,1)}) custom-call(bf16[2048,1536]{1,0:T(8,128)(2,1)} %constant_dynamic-update-slice_fusion.h_ref, bf16[2048,1536]{1,0:T(8,128)(2,1)} %constant_dynamic-update-slice_fusion.10.e_ref, bf16[1536,1024]{1,0:T(8,128)(2,1)} %bitcast.198, ...), custom_call_target="tpu_custom_call" | custom-call | flops 8053063680 | bytes 12582912 | tf_op jit(solution)/shard_map/ffn/pallas_call | solution.py:576
  265.5 13.1 %ffn.3 = (bf16[2048,512]{1,0:T(8,128)(2,1)}, bf16[2048,1024]{1,0:T(8,128)(2,1)}, bf16[4,256,1536]{2,1,0:T(8,128)(2,1)}) custom-call(bf16[2048,1536]{1,0:T(8,128)(2,1)} %constant_dynamic-update-slice_fusion.h_ref, bf16[2048,1536]{1,0:T(8,128)(2,1)} %constant_dynamic-update-slice_fusion.10.e_ref, ...), custom_call_target="tpu_custom_call", output_to_operand_aliasing={{0}: (4, {}), {1}: (5, {})} | custom-call | flops 8053063680 | bytes 12582912 | tf_op jit(solution)/shard_map/ffn/pallas_call | solution.py:576
  284.9 8.9 %fusion.51 = bf16[1536,1024]{1,0:T(8,128)(2,1)S(1)} fusion(bf16[2048,1536]{1,0:T(8,128)(2,1)} %constant_dynamic-update-slice_fusion.h_ref, bf16[2048,1024]{1,0:T(8,128)(2,1)S(1)} %copy-done.65), kind=kOutput, calls=%fused_computation.184 | convolution fusion | flops 6442450944 | bytes 13631488 | tf_op jit(solution)/shard_map/dot_general | solution.py:19
  301.6 6.3 %fusion.52 = bf16[512,1536]{1,0:T(8,128)(2,1)S(1)} fusion(bf16[2048,512]{1,0:T(8,128)(2,1)S(1)} %copy-done.17, bf16[2048,1536]{1,0:T(8,128)(2,1)} %constant_dynamic-update-slice_fusion.10.e_ref), kind=kOutput, calls=%fused_computation.185 | convolution fusion | flops 3221225472 | bytes 9961472 | tf_op jit(solution)/shard_map/dot_general | solution.py:19
  310.9 7.9 %collective-permute-done.52.refs_5_ = bf16[256,1536]{1,0:T(8,128)(2,1)S(1)} collective-permute-done((bf16[256,1536]{1,0:T(8,128)(2,1)}, bf16[256,1536]{1,0:T(8,128)(2,1)S(1)}, u32[]{:S(2)}, u32[]{:S(2)}) %collective-permute-start.52) | collective-permute-done | bytes 786464 | tf_op jit(solution)/shard_map/ppermute | solution.py:24
  319.8 5.2 norm_back.2
  336.2 7.4 %collective-permute-done.54.refs_1_.refs_9_ = bf16[256,1536]{1,0:T(8,128)(2,1)} collective-permute-done((bf16[256,1536]{1,0:T(8,128)(2,1)}, bf16[256,1536]{1,0:T(8,128)(2,1)}, u32[]{:S(2)}, u32[]{:S(2)}) %collective-permute-start.54) | collective-permute-done | bytes 786464 | tf_op jit(solution)/shard_map/ppermute | solution.py:24
  349.0 8.2 %collective-permute-done.59.refs_3_ = bf16[128,1536]{1,0:T(8,128)(2,1)S(1)} collective-permute-done((bf16[128,1536]{1,0:T(8,128)(2,1)S(1)}, bf16[128,1536]{1,0:T(8,128)(2,1)S(1)}, u32[]{:S(2)}, u32[]{:S(2)}) %collective-permute-start.59) | collective-permute-done | bytes 393248 | tf_op jit(solution)/shard_map/ppermute | solution.py:24
  366.6 25.2 %attend_back.2 = (bf16[2048,896]{1,0:T(8,128)(2,1)}, bf16[4,128,1536]{2,1,0:T(8,128)(2,1)}, bf16[4,128,1536]{2,1,0:T(8,128)(2,1)}, f32[8,128]{1,0:T(8,128)}, bf16[192,1536]{1,0:T(8,128)(2,1)}) custom-call(s32[32]{0:T(128)} %get-tuple-element.295.table, bf16[256,1536]{1,0:T(8,128)(2,1)} %get-tuple-element.296.refs_0_.refs_8_, ...), custom_call_target="tpu_custom_call" | custom-call | flops 20000000000 | bytes 10000000 | tf_op jit(solution)/shard_map/attend_back/pallas_call | solution.py:502
  402.0 21.1 %attend_back.3 = (bf16[2048,896]{1,0:T(8,128)(2,1)}, bf16[4,128,1536]{2,1,0:T(8,128)(2,1)}, bf16[4,128,1536]{2,1,0:T(8,128)(2,1)}, f32[8,128]{1,0:T(8,128)}) custom-call(s32[32]{0:T(128)} %get-tuple-element.320.table, bf16[256,1536]{1,0:T(8,128)(2,1)} %get-tuple-element.296.refs_0_.refs_8_, ...), custom_call_target="tpu_custom_call", output_to_operand_aliasing={{0}: (18, {})} | custom-call | flops 20000000000 | bytes 10000000 | tf_op jit(solution)/shard_map/attend_back/pallas_call | solution.py:502
  424.7 11.1 %fusion.53 = bf16[1536,896]{1,0:T(8,128)(2,1)} fusion(bf16[2048,1536]{1,0:T(8,128)(2,1)} %get-tuple-element.335, bf16[2048,896]{1,0:T(8,128)(2,1)} %get-tuple-element.336), kind=kOutput, calls=%fused_computation.186 | convolution fusion | flops 5637144576 | bytes 12713984 | tf_op jit(solution)/shard_map/dot_general | solution.py:19
  445.9 4.2 add_rows.1
  464.6 11.7 %collective-permute-done.74.refs_7_ = bf16[256,1536]{1,0:T(8,128)(2,1)S(1)} collective-permute-done((bf16[256,1536]{1,0:T(8,128)(2,1)}, bf16[256,1536]{1,0:T(8,128)(2,1)S(1)}, u32[]{:S(2)}, u32[]{:S(2)}) %collective-permute-start.74) | collective-permute-done | bytes 786464 | tf_op jit(solution)/shard_map/ppermute | solution.py:24
  478.4 4.8 norm_back.3
  499.8 10.3 %collective-permute-done.77 = bf16[4,32,1536]{2,1,0:T(8,128)(2,1)S(1)} collective-permute-done((bf16[4,32,1536]{2,1,0:T(8,128)(2,1)}, bf16[4,32,1536]{2,1,0:T(8,128)(2,1)S(1)}, u32[]{:S(2)}, u32[]{:S(2)}) %collective-permute-start.77) | collective-permute-done | bytes 393248 | tf_op jit(solution)/shard_map/ppermute | solution.py:24
  510.1 10.9 %collective-permute-done.79 = bf16[4,32,1536]{2,1,0:T(8,128)(2,1)} collective-permute-done((bf16[4,32,1536]{2,1,0:T(8,128)(2,1)S(1)}, bf16[4,32,1536]{2,1,0:T(8,128)(2,1)}, u32[]{:S(2)}, u32[]{:S(2)}) %collective-permute-start.79) | collective-permute-done | bytes 393248 | tf_op jit(solution)/shard_map/ppermute | solution.py:24
  536.0 5.8 %collective-permute-done.83 = bf16[4,32,1536]{2,1,0:T(8,128)(2,1)S(1)} collective-permute-done((bf16[4,32,1536]{2,1,0:T(8,128)(2,1)S(1)}, bf16[4,32,1536]{2,1,0:T(8,128)(2,1)S(1)}, u32[]{:S(2)}, u32[]{:S(2)}) %collective-permute-start.83) | collective-permute-done | bytes 393248 | tf_op jit(solution)/shard_map/ppermute | solution.py:33
  556.4 9.4 %reduce-scatter.8.cloned.1.call-done = bf16[48,1536]{1,0:T(8,128)(2,1)} async-done(((bf16[192,1536]{1,0:T(8,128)(2,1)}), bf16[48,1536]{1,0:T(8,128)(2,1)}) %reduce-scatter.8.cloned.1.call-update) | async-done | bytes 147472 | tf_op jit(solution)/shard_map/reduce_scatter | solution.py:693
  (425 shorter events, 253.7 us)
Async XLA Ops:
  32.2 24.6 %all-to-all-start = ((bf16[8,48,896]{2,1,0:T(8,128)(2,1)}), bf16[8,48,896]{2,1,0:T(8,128)(2,1)S(1)}, u32[]{:S(2)}, u32[]{:S(2)}) async-start(bf16[8,48,896]{2,1,0:T(8,128)(2,1)} %layout.4), calls=%async_computation | async-start | bytes 1376256 | tf_op jit(solution)/shard_map/all_to_all | solution.py:689
  35.9 83.0 %all-gather.7.cloned.1.call-start = ((), (), s32[]{:S(2)}) async-start(), calls=%async_computation.12 | async-start | bytes 3440640 | tf_op jit(solution)/shard_map/all_gather | solution.py:772
  57.8 20.6 %collective-permute-start.9 = (bf16[256,1536]{1,0:T(8,128)(2,1)S(1)}, bf16[256,1536]{1,0:T(8,128)(2,1)}, u32[]{:S(2)}, u32[]{:S(2)}) collective-permute-start(bf16[256,1536]{1,0:T(8,128)(2,1)S(1)} %bitcast.148), channel_id=1, source_target_pairs={{0,1},{1,0},{2,3},{3,2},{4,5},{5,4},{6,7},{7,6},{8,9},{9,8},{10,11... | collective-permute-start | bytes 2359304 | tf_op jit(solution)/shard_map/ppermute | solution.py:24
  59.5 23.6 %collective-permute-start.10 = (bf16[256,1536]{1,0:T(8,128)(2,1)S(1)}, bf16[256,1536]{1,0:T(8,128)(2,1)}, u32[]{:S(2)}, u32[]{:S(2)}) collective-permute-start(bf16[256,1536]{1,0:T(8,128)(2,1)S(1)} %bitcast.149), channel_id=1, source_target_pairs={{0,2},{2,0},{1,3},{3,1},{4,6},{6,4},{5,7},{7,5},{8,10},{10,8},{9,1... | collective-permute-start | bytes 2359304 | tf_op jit(solution)/shard_map/ppermute | solution.py:24
  61.0 27.1 %all-to-all-start.1 = ((bf16[4,48,1536]{2,1,0:T(8,128)(2,1)}), bf16[4,48,1536]{2,1,0:T(8,128)(2,1)S(1)}, u32[]{:S(2)}, u32[]{:S(2)}) async-start(bf16[4,48,1536]{2,1,0:T(8,128)(2,1)} %pad_maximum_fusion.9), calls=%async_computation.1 | async-start | bytes 1179648 | tf_op jit(solution)/shard_map/all_to_all | solution.py:689
  64.5 23.5 %collective-permute-start.24 = (s32[2,4]{1,0:T(2,128)S(1)}, s32[2,4]{1,0:T(2,128)S(1)}, u32[]{:S(2)}, u32[]{:S(2)}) collective-permute-start(s32[2,4]{1,0:T(2,128)S(1)} %bitcast.206), channel_id=1, source_target_pairs={{0,0},{8,1},{16,2},{24,3},{4,4},{12,5},{20,6},{28,7},{1,8},{9,9},{... | collective-permute-start | bytes 104 | tf_op jit(solution)/shard_map/ppermute | solution.py:784
  84.9 21.3 %collective-permute-start.14 = (bf16[256,1536]{1,0:T(8,128)(2,1)}, bf16[256,1536]{1,0:T(8,128)(2,1)}, u32[]{:S(2)}, u32[]{:S(2)}) collective-permute-start(bf16[256,1536]{1,0:T(8,128)(2,1)} %collective-permute-done.9.refs_1_), channel_id=1, source_target_pairs={{0,4},{4,0},{1,5},{5,1},{2,6},{6,2},{3,7},{7,3},{8,12},{12,8},{9,1... | collective-permute-start | bytes 2359304 | tf_op jit(solution)/shard_map/ppermute | solution.py:24
  86.0 20.2 %collective-permute-start.15 = (bf16[256,1536]{1,0:T(8,128)(2,1)}, bf16[256,1536]{1,0:T(8,128)(2,1)}, u32[]{:S(2)}, u32[]{:S(2)}) collective-permute-start(bf16[256,1536]{1,0:T(8,128)(2,1)} %collective-permute-done.10.refs_2_), channel_id=1, source_target_pairs={{0,4},{4,0},{1,5},{5,1},{2,6},{6,2},{3,7},{7,3},{8,12},{12,8},{9,1... | collective-permute-start | bytes 2359304 | tf_op jit(solution)/shard_map/ppermute | solution.py:24
  91.7 160.7 %all-gather.11.cloned.1.call-start = ((), (), s32[]{:S(2)}) async-start(), calls=%async_computation.14 | async-start | bytes 1966080 | tf_op jit(solution)/shard_map/all_gather | solution.py:817
  119.0 19.8 %collective-permute-start.23 = (bf16[2,32,1536]{2,1,0:T(8,128)(2,1)S(1)}, bf16[2,32,1536]{2,1,0:T(8,128)(2,1)S(1)}, u32[]{:S(2)}, u32[]{:S(2)}) collective-permute-start(bf16[2,32,1536]{2,1,0:T(8,128)(2,1)S(1)} %get-tuple-element.410), channel_id=1, source_target_pairs={{0,24},{8,16},{16,8},{24,0},{1,25},{9,17},{17,9},{25,1},{2,26},{10... | collective-permute-start | bytes 589832 | tf_op jit(solution)/shard_map/ppermute | solution.py:24
  140.7 111.7 %all-gather.9.cloned.1.call-start = ((), (), s32[]{:S(2)}) async-start(), calls=%async_computation.13 | async-start | bytes 3932160 | tf_op jit(solution)/shard_map/all_gather | solution.py:816
  168.8 271.7 %reduce-scatter.4.cloned.1.call-start = ((), (), s32[]{:S(2)}) async-start(), calls=%async_computation.9 | async-start | bytes 5898240 | tf_op jit(solution)/shard_map/reduce_scatter | solution.py:693
  172.5 24.6 %collective-permute-start.44 = (bf16[256,1536]{1,0:T(8,128)(2,1)}, bf16[256,1536]{1,0:T(8,128)(2,1)S(1)}, u32[]{:S(2)}, u32[]{:S(2)}) collective-permute-start(bf16[256,1536]{1,0:T(8,128)(2,1)} %bitcast.158), channel_id=1, source_target_pairs={{0,4},{4,0},{1,5},{5,1},{2,6},{6,2},{3,7},{7,3},{8,12},{12,8},{9,1... | collective-permute-start | bytes 2359304 | tf_op jit(solution)/shard_map/ppermute | solution.py:24
  172.5 25.6 %collective-permute-start.45 = (bf16[256,1536]{1,0:T(8,128)(2,1)}, bf16[256,1536]{1,0:T(8,128)(2,1)S(1)}, u32[]{:S(2)}, u32[]{:S(2)}) collective-permute-start(bf16[256,1536]{1,0:T(8,128)(2,1)} %copy-done.20), channel_id=1, source_target_pairs={{0,4},{4,0},{1,5},{5,1},{2,6},{6,2},{3,7},{7,3},{8,12},{12,8},{9,1... | collective-permute-start | bytes 2359304 | tf_op jit(solution)/shard_map/ppermute | solution.py:24
  179.8 40.4 %collective-permute-start.46 = (bf16[256,1536]{1,0:T(8,128)(2,1)S(1)}, bf16[256,1536]{1,0:T(8,128)(2,1)S(1)}, u32[]{:S(2)}, u32[]{:S(2)}) collective-permute-start(bf16[256,1536]{1,0:T(8,128)(2,1)S(1)} %copy-done.19), channel_id=1, source_target_pairs={{0,4},{4,0},{1,5},{5,1},{2,6},{6,2},{3,7},{7,3},{8,12},{12,8},{9,1... | collective-permute-start | bytes 2359304 | tf_op jit(solution)/shard_map/ppermute | solution.py:24
  197.1 23.9 %collective-permute-start.47 = (bf16[128,1536]{1,0:T(8,128)(2,1)S(1)}, bf16[128,1536]{1,0:T(8,128)(2,1)S(1)}, u32[]{:S(2)}, u32[]{:S(2)}) collective-permute-start(bf16[128,1536]{1,0:T(8,128)(2,1)S(1)} %copy-done.41), channel_id=1, source_target_pairs={{0,4},{4,0},{1,5},{5,1},{2,6},{6,2},{3,7},{7,3},{8,12},{12,8},{9,1... | collective-permute-start | bytes 1179656 | tf_op jit(solution)/shard_map/ppermute | solution.py:24
  198.1 23.8 %collective-permute-start.48 = (bf16[128,1536]{1,0:T(8,128)(2,1)S(1)}, bf16[128,1536]{1,0:T(8,128)(2,1)S(1)}, u32[]{:S(2)}, u32[]{:S(2)}) collective-permute-start(bf16[128,1536]{1,0:T(8,128)(2,1)S(1)} %collective-permute-done.28), channel_id=1, source_target_pairs={{0,4},{4,0},{1,5},{5,1},{2,6},{6,2},{3,7},{7,3},{8,12},{12,8},{9,1... | collective-permute-start | bytes 1179656 | tf_op jit(solution)/shard_map/ppermute | solution.py:24
  222.7 25.3 %collective-permute-start.39 = (bf16[256,1536]{1,0:T(8,128)(2,1)S(1)}, bf16[256,1536]{1,0:T(8,128)(2,1)S(1)}, u32[]{:S(2)}, u32[]{:S(2)}) collective-permute-start(bf16[256,1536]{1,0:T(8,128)(2,1)S(1)} %copy-done.30), channel_id=1, source_target_pairs={{0,4},{4,0},{1,5},{5,1},{2,6},{6,2},{3,7},{7,3},{8,12},{12,8},{9,1... | collective-permute-start | bytes 2359304 | tf_op jit(solution)/shard_map/ppermute | solution.py:24
  299.5 19.4 %collective-permute-start.52 = (bf16[256,1536]{1,0:T(8,128)(2,1)}, bf16[256,1536]{1,0:T(8,128)(2,1)S(1)}, u32[]{:S(2)}, u32[]{:S(2)}) collective-permute-start(bf16[256,1536]{1,0:T(8,128)(2,1)} %get-tuple-element.280), channel_id=1, source_target_pairs={{0,1},{1,0},{2,3},{3,2},{4,5},{5,4},{6,7},{7,6},{8,9},{9,8},{10,11... | collective-permute-start | bytes 2359304 | tf_op jit(solution)/shard_map/ppermute | solution.py:24
  300.6 19.2 %collective-permute-start.53 = (bf16[256,1536]{1,0:T(8,128)(2,1)}, bf16[256,1536]{1,0:T(8,128)(2,1)}, u32[]{:S(2)}, u32[]{:S(2)}) collective-permute-start(bf16[256,1536]{1,0:T(8,128)(2,1)} %get-tuple-element.281), channel_id=1, source_target_pairs={{0,2},{2,0},{1,3},{3,1},{4,6},{6,4},{5,7},{7,5},{8,10},{10,8},{9,1... | collective-permute-start | bytes 2359304 | tf_op jit(solution)/shard_map/ppermute | solution.py:24
  363.4 28.3 %collective-permute-start.57 = (bf16[128,1536]{1,0:T(8,128)(2,1)}, bf16[128,1536]{1,0:T(8,128)(2,1)S(1)}, u32[]{:S(2)}, u32[]{:S(2)}) collective-permute-start(bf16[128,1536]{1,0:T(8,128)(2,1)} %get-tuple-element.293), channel_id=1, source_target_pairs={{0,2},{2,0},{1,3},{3,1},{4,6},{6,4},{5,7},{7,5},{8,10},{10,8},{9,1... | collective-permute-start | bytes 1179656 | tf_op jit(solution)/shard_map/ppermute | solution.py:24
  364.6 27.2 %collective-permute-start.58 = (bf16[128,1536]{1,0:T(8,128)(2,1)}, bf16[128,1536]{1,0:T(8,128)(2,1)S(1)}, u32[]{:S(2)}, u32[]{:S(2)}) collective-permute-start(bf16[128,1536]{1,0:T(8,128)(2,1)} %get-tuple-element.294), channel_id=1, source_target_pairs={{0,1},{1,0},{2,3},{3,2},{4,5},{5,4},{6,7},{7,6},{8,9},{9,8},{10,11... | collective-permute-start | bytes 1179656 | tf_op jit(solution)/shard_map/ppermute | solution.py:24
  396.2 27.0 %collective-permute-start.66 = (bf16[256,1536]{1,0:T(8,128)(2,1)}, bf16[256,1536]{1,0:T(8,128)(2,1)S(1)}, u32[]{:S(2)}, u32[]{:S(2)}) collective-permute-start(bf16[256,1536]{1,0:T(8,128)(2,1)} %get-tuple-element.317), channel_id=1, source_target_pairs={{0,1},{1,0},{2,3},{3,2},{4,5},{5,4},{6,7},{7,6},{8,9},{9,8},{10,11... | collective-permute-start | bytes 2359304 | tf_op jit(solution)/shard_map/ppermute | solution.py:24
  397.4 25.7 %collective-permute-start.67 = (bf16[256,1536]{1,0:T(8,128)(2,1)}, bf16[256,1536]{1,0:T(8,128)(2,1)}, u32[]{:S(2)}, u32[]{:S(2)}) collective-permute-start(bf16[256,1536]{1,0:T(8,128)(2,1)} %get-tuple-element.318), channel_id=1, source_target_pairs={{0,2},{2,0},{1,3},{3,1},{4,6},{6,4},{5,7},{7,5},{8,10},{10,8},{9,1... | collective-permute-start | bytes 2359304 | tf_op jit(solution)/shard_map/ppermute | solution.py:24
  398.2 24.9 %all-to-all-start.3 = ((bf16[4,48,1536]{2,1,0:T(8,128)(2,1)}), bf16[4,48,1536]{2,1,0:T(8,128)(2,1)S(1)}, u32[]{:S(2)}, u32[]{:S(2)}) async-start(bf16[4,48,1536]{2,1,0:T(8,128)(2,1)} %bitcast.60), calls=%async_computation.3 | async-start | bytes 1179648 | tf_op jit(solution)/shard_map/all_to_all | solution.py:689
  401.7 119.2 %reduce-scatter.6.cloned.1.call-start = ((), (), s32[]{:S(2)}) async-start(), calls=%async_computation.10 | async-start | bytes 3440640 | tf_op jit(solution)/shard_map/reduce_scatter | solution.py:693
  401.9 33.9 %collective-permute-start.68 = (bf16[4,128,1536]{2,1,0:T(8,128)(2,1)}, bf16[4,128,1536]{2,1,0:T(8,128)(2,1)S(1)}, u32[]{:S(2)}, u32[]{:S(2)}) collective-permute-start(bf16[4,128,1536]{2,1,0:T(8,128)(2,1)} %get-tuple-element.333), channel_id=1, source_target_pairs={{0,4},{4,0},{1,5},{5,1},{2,6},{6,2},{3,7},{7,3},{8,12},{12,8},{9,1... | collective-permute-start | bytes 4718600 | tf_op jit(solution)/shard_map/ppermute | solution.py:24
  485.6 24.5 %collective-permute-start.77 = (bf16[4,32,1536]{2,1,0:T(8,128)(2,1)}, bf16[4,32,1536]{2,1,0:T(8,128)(2,1)S(1)}, u32[]{:S(2)}, u32[]{:S(2)}) collective-permute-start(bf16[4,32,1536]{2,1,0:T(8,128)(2,1)} %get-tuple-element.405), channel_id=1, source_target_pairs={{0,8},{8,0},{16,24},{24,16},{1,9},{9,1},{17,25},{25,17},{2,10},{10... | collective-permute-start | bytes 1179656 | tf_op jit(solution)/shard_map/ppermute | solution.py:24
  485.6 24.5 %collective-permute-start.78 = (bf16[4,32,1536]{2,1,0:T(8,128)(2,1)}, bf16[4,32,1536]{2,1,0:T(8,128)(2,1)S(1)}, u32[]{:S(2)}, u32[]{:S(2)}) collective-permute-start(bf16[4,32,1536]{2,1,0:T(8,128)(2,1)} %get-tuple-element.404), channel_id=1, source_target_pairs={{0,16},{8,24},{16,0},{24,8},{1,17},{9,25},{17,1},{25,9},{2,18},{10... | collective-permute-start | bytes 1179656 | tf_op jit(solution)/shard_map/ppermute | solution.py:24
  488.4 32.5 %collective-permute-start.79 = (bf16[4,32,1536]{2,1,0:T(8,128)(2,1)S(1)}, bf16[4,32,1536]{2,1,0:T(8,128)(2,1)}, u32[]{:S(2)}, u32[]{:S(2)}) collective-permute-start(bf16[4,32,1536]{2,1,0:T(8,128)(2,1)S(1)} %get-tuple-element.403), channel_id=1, source_target_pairs={{0,24},{8,16},{16,8},{24,0},{1,25},{9,17},{17,9},{25,1},{2,26},{10... | collective-permute-start | bytes 1179656 | tf_op jit(solution)/shard_map/ppermute | solution.py:24
  495.7 31.1 %all-to-all-start.5 = ((bf16[8,48,1024]{2,1,0:T(8,128)(2,1)}), bf16[8,48,1024]{2,1,0:T(8,128)(2,1)S(1)}, u32[]{:S(2)}, u32[]{:S(2)}) async-start(bf16[8,48,1024]{2,1,0:T(8,128)(2,1)} %bitcast.84), calls=%async_computation.8 | async-start | bytes 1572864 | tf_op jit(solution)/shard_map/all_to_all | solution.py:689
  535.4 30.4 %reduce-scatter.8.cloned.1.call-start = ((), (), s32[]{:S(2)}) async-start(), calls=%async_computation.11 | async-start | bytes 737280 | tf_op jit(solution)/shard_map/reduce_scatter | solution.py:693
  (132 other events, 1375.5 us)
Sparse Core Ops, SparseCore 0:
  57.9 57.4 all-gather.6
  140.8 36.4 all-gather.10
  178.9 62.3 all-gather.8
  328.3 84.2 reduce-scatter.3
  440.6 64.7 reduce-scatter.5
  538.2 27.5 reduce-scatter.7

commit v5 on v4

--- a/solution.py
+++ b/solution.py
@@ -895,11 +895,12 @@
     returned = jnp.concatenate([output, stream_grad], axis=0).reshape(2 * micro, -1, width)
     returned = rows_from_layer(returned)
     grad_bias = total_over("q", total_over("p", bias_all))
-    returned, grad_packed, grad_bias, grad_out = tie(returned, grad_packed, grad_bias, grad_out)
+    returned, grad_packed, grad_bias = tie(returned, grad_packed, grad_bias)
     if aligned:
         grad_out = scatter_layers(grad_out.reshape(nf * slab, width))
     grad_packed = all_to_all(grad_packed.reshape(plane, slab, -1), members)
-    returned, grad_packed = tie(rows_from_plane(returned), grad_packed)
+    returned, grad_packed = tie(returned, grad_packed)
+    returned, grad_out = tie(rows_from_plane(returned), grad_out)
     output, input_grad = returned[:micro], returned[micro:].astype(F32)
 
     grad_gate, grad_up, sums_two = unpack_hidden(grad_ffn_w, (w_gate, w_up), nz)

time: 579 us -> 576 us (level)
  waiting for transfers between devices: 197 us -> 189 us
    reduce_scatter x3, waiting for transfers between devices: 9.4 us -> 0.02 us  [scatter_layers(): return lax.psum_scatter(grad, 'z', scatter_dimension=0, tiled=True)]
    unnamed x150 -> x148, local copies, waits for them, and re-layouts: 35.3 us -> 32.6 us
  transfers between devices with their start and end apart: 97 -> 97, of which waited for: 44 -> 43; matrix products, arithmetic and copies ran while one was open for 15% -> 15% of each run, Pallas kernels for 24% -> 24%
where the time goes in v5:
time: 576 us; the launch traced here: 568 us
  waiting for transfers between devices  189 us (33%)
  Pallas kernels  161 us (28%)
  starting transfers between devices  101 us (18%)
  local copies, waits for them, and re-layouts  48.4 us (8%)
  matrix products  36.3 us (6%)
  other arithmetic  16.2 us (3%)
  between operations  15.4 us (3%)
    ppermute x75, waiting for transfers between devices, xor_permute(): return lax.ppermute(x, axis, [(i, i ^ step) for i in range(n)])  157 us
    ppermute x75, starting transfers between devices, xor_permute(): return lax.ppermute(x, axis, [(i, i ^ step) for i in range(n)])  65.9 us
    pallas_call x2, Pallas kernels, attend_back(): pl.pallas_call(functools.partial(attend_back_kernel, heads, depth, chunk,...  46.2 us
    pallas_call x12, Pallas kernels, rows_kernel(): pl.pallas_call(kernel, grid=(1,), in_specs=[spec for _, spec in operands]...  41.7 us
    dot_general x6, matrix products, dot(): lax.dot_general(left, right, (contract, ((), ())), preferred_element_type...  34.7 us
    unnamed x148, local copies, waits for them, and re-layouts  32.6 us
    pallas_call x2, Pallas kernels, attend(): pl.pallas_call(functools.partial(attend_kernel, heads, depth, chunk, memb...  30.5 us
    pallas_call x2, Pallas kernels, ffn(): pl.pallas_call(ffn_kernel, grid=(count,), in_specs=[blocks(width, first),...  26.3 us
  transfers between devices with their start and end apart: 97, of which 43 were waited for; matrix products, arithmetic and copies ran while one was open for 15% of the time, Pallas kernels for 24%

profile of v5, /device:TPU:0, one launch (start us, length us, event | category | flops | bytes accessed | tf_op | source)
XLA Modules:
  0.0 567.9 jit_solution(13868070694597952999)
XLA Ops:
  7.2 5.1 collective-permute-start.8
  39.6 6.1 %collective-permute-done.5 = bf16[2,32,1536]{2,1,0:T(8,128)(2,1)S(1)} collective-permute-done((bf16[2,32,1536]{2,1,0:T(8,128)(2,1)S(1)}, bf16[2,32,1536]{2,1,0:T(8,128)(2,1)S(1)}, u32[]{:S(2)}, u32[]{:S(2)}) %collective-permute-start.5) | collective-permute-done | bytes 196640 | tf_op jit(solution)/shard_map/ppermute | solution.py:24
  45.7 11.1 %collective-permute-done.4 = bf16[2,32,1536]{2,1,0:T(8,128)(2,1)S(1)} collective-permute-done((bf16[2,32,1536]{2,1,0:T(8,128)(2,1)S(1)}, bf16[2,32,1536]{2,1,0:T(8,128)(2,1)S(1)}, u32[]{:S(2)}, u32[]{:S(2)}) %collective-permute-start.4) | collective-permute-done | bytes 196640 | tf_op jit(solution)/shard_map/ppermute | solution.py:24
  67.5 10.9 %collective-permute-done.9.refs_1_ = bf16[256,1536]{1,0:T(8,128)(2,1)} collective-permute-done((bf16[256,1536]{1,0:T(8,128)(2,1)S(1)}, bf16[256,1536]{1,0:T(8,128)(2,1)}, u32[]{:S(2)}, u32[]{:S(2)}) %collective-permute-start.9) | collective-permute-done | bytes 786464 | tf_op jit(solution)/shard_map/ppermute | solution.py:24
  78.4 4.8 collective-permute-done.10.refs_2_
  94.0 4.9 collective-permute-done.11.refs_3_
  101.1 5.2 all-to-all-done.2
  123.5 15.4 %attend.2 = (bf16[2048,1536]{1,0:T(8,128)(2,1)}, bf16[1024,576]{1,0:T(8,128)(2,1)}, f32[1024,192]{1,0:T(8,128)}, f32[1024,128]{1,0:T(8,128)}, f32[1024,192]{1,0:...) custom-call(s32[32]{0:T(128)} %get-tuple-element.299.table, ...), custom_call_target="tpu_custom_call" | custom-call | flops 14000000000 | bytes 10000000 | tf_op jit(solution)/shard_map/attend/pallas_call | solution.py:464
  141.2 15.2 %attend.3 = (bf16[2048,1536]{1,0:T(8,128)(2,1)}, bf16[1024,576]{1,0:T(8,128)(2,1)}, f32[1024,192]{1,0:T(8,128)}, f32[1024,128]{1,0:T(8,128)}, f32[1024,192]{1,0:...) custom-call(s32[32]{0:T(128)} %get-tuple-element.324.table, ...), custom_call_target="tpu_custom_call", output_to_operand_aliasing={{0}: (12, {})} | custom-call | flops 14000000000 | bytes 10000000 | tf_op jit(solution)/shard_map/attend/pallas_call | solution.py:464
  180.7 7.7 %collective-permute-done.31.refs_8_ = bf16[128,1536]{1,0:T(8,128)(2,1)S(1)} collective-permute-done((bf16[128,1536]{1,0:T(8,128)(2,1)}, bf16[128,1536]{1,0:T(8,128)(2,1)S(1)}, u32[]{:S(2)}, u32[]{:S(2)}) %collective-permute-start.31) | collective-permute-done | bytes 393248 | tf_op jit(solution)/shard_map/ppermute | solution.py:24
  199.5 12.6 %collective-permute-done.33.refs_6_ = bf16[256,1536]{1,0:T(8,128)(2,1)S(1)} collective-permute-done((bf16[256,1536]{1,0:T(8,128)(2,1)}, bf16[256,1536]{1,0:T(8,128)(2,1)S(1)}, u32[]{:S(2)}, u32[]{:S(2)}) %collective-permute-start.33) | collective-permute-done | bytes 786464 | tf_op jit(solution)/shard_map/ppermute | solution.py:24
  223.6 13.2 %collective-permute-done.35 = bf16[256,1536]{1,0:T(8,128)(2,1)S(1)} collective-permute-done((bf16[256,1536]{1,0:T(8,128)(2,1)}, bf16[256,1536]{1,0:T(8,128)(2,1)S(1)}, u32[]{:S(2)}, u32[]{:S(2)}) %collective-permute-start.35) | collective-permute-done | bytes 786464 | tf_op jit(solution)/shard_map/ppermute | solution.py:24
  241.2 4.6 collective-permute-done.37
  252.3 13.2 %ffn.2 = (bf16[2048,512]{1,0:T(8,128)(2,1)}, bf16[2048,1024]{1,0:T(8,128)(2,1)}, bf16[4,256,1536]{2,1,0:T(8,128)(2,1)}) custom-call(bf16[2048,1536]{1,0:T(8,128)(2,1)} %constant_dynamic-update-slice_fusion.h_ref, bf16[2048,1536]{1,0:T(8,128)(2,1)} %constant_dynamic-update-slice_fusion.10.e_ref, bf16[1536,1024]{1,0:T(8,128)(2,1)} %bitcast.198, ...), custom_call_target="tpu_custom_call" | custom-call | flops 8053063680 | bytes 12582912 | tf_op jit(solution)/shard_map/ffn/pallas_call | solution.py:576
  265.5 13.1 %ffn.3 = (bf16[2048,512]{1,0:T(8,128)(2,1)}, bf16[2048,1024]{1,0:T(8,128)(2,1)}, bf16[4,256,1536]{2,1,0:T(8,128)(2,1)}) custom-call(bf16[2048,1536]{1,0:T(8,128)(2,1)} %constant_dynamic-update-slice_fusion.h_ref, bf16[2048,1536]{1,0:T(8,128)(2,1)} %constant_dynamic-update-slice_fusion.10.e_ref, ...), custom_call_target="tpu_custom_call", output_to_operand_aliasing={{0}: (4, {}), {1}: (5, {})} | custom-call | flops 8053063680 | bytes 12582912 | tf_op jit(solution)/shard_map/ffn/pallas_call | solution.py:576
  284.9 8.9 %fusion.51 = bf16[1536,1024]{1,0:T(8,128)(2,1)S(1)} fusion(bf16[2048,1536]{1,0:T(8,128)(2,1)} %constant_dynamic-update-slice_fusion.h_ref, bf16[2048,1024]{1,0:T(8,128)(2,1)S(1)} %copy-done.64), kind=kOutput, calls=%fused_computation.184 | convolution fusion | flops 6442450944 | bytes 13631488 | tf_op jit(solution)/shard_map/dot_general | solution.py:19
  301.6 6.3 %fusion.52 = bf16[512,1536]{1,0:T(8,128)(2,1)S(1)} fusion(bf16[2048,512]{1,0:T(8,128)(2,1)S(1)} %copy-done.17, bf16[2048,1536]{1,0:T(8,128)(2,1)} %constant_dynamic-update-slice_fusion.10.e_ref), kind=kOutput, calls=%fused_computation.185 | convolution fusion | flops 3221225472 | bytes 9961472 | tf_op jit(solution)/shard_map/dot_general | solution.py:19
  310.8 7.9 %collective-permute-done.52.refs_5_ = bf16[256,1536]{1,0:T(8,128)(2,1)S(1)} collective-permute-done((bf16[256,1536]{1,0:T(8,128)(2,1)}, bf16[256,1536]{1,0:T(8,128)(2,1)S(1)}, u32[]{:S(2)}, u32[]{:S(2)}) %collective-permute-start.52) | collective-permute-done | bytes 786464 | tf_op jit(solution)/shard_map/ppermute | solution.py:24
  319.8 5.2 norm_back.2
  336.2 7.4 %collective-permute-done.54.refs_1_.refs_9_ = bf16[256,1536]{1,0:T(8,128)(2,1)} collective-permute-done((bf16[256,1536]{1,0:T(8,128)(2,1)}, bf16[256,1536]{1,0:T(8,128)(2,1)}, u32[]{:S(2)}, u32[]{:S(2)}) %collective-permute-start.54) | collective-permute-done | bytes 786464 | tf_op jit(solution)/shard_map/ppermute | solution.py:24
  349.0 8.1 %collective-permute-done.59.refs_3_ = bf16[128,1536]{1,0:T(8,128)(2,1)S(1)} collective-permute-done((bf16[128,1536]{1,0:T(8,128)(2,1)S(1)}, bf16[128,1536]{1,0:T(8,128)(2,1)S(1)}, u32[]{:S(2)}, u32[]{:S(2)}) %collective-permute-start.59) | collective-permute-done | bytes 393248 | tf_op jit(solution)/shard_map/ppermute | solution.py:24
  366.5 25.1 %attend_back.2 = (bf16[2048,896]{1,0:T(8,128)(2,1)}, bf16[4,128,1536]{2,1,0:T(8,128)(2,1)}, bf16[4,128,1536]{2,1,0:T(8,128)(2,1)}, f32[8,128]{1,0:T(8,128)}, bf16[192,1536]{1,0:T(8,128)(2,1)}) custom-call(s32[32]{0:T(128)} %get-tuple-element.299.table, bf16[256,1536]{1,0:T(8,128)(2,1)} %get-tuple-element.300.refs_0_.refs_8_, ...), custom_call_target="tpu_custom_call" | custom-call | flops 20000000000 | bytes 10000000 | tf_op jit(solution)/shard_map/attend_back/pallas_call | solution.py:502
  401.9 21.1 %attend_back.3 = (bf16[2048,896]{1,0:T(8,128)(2,1)}, bf16[4,128,1536]{2,1,0:T(8,128)(2,1)}, bf16[4,128,1536]{2,1,0:T(8,128)(2,1)}, f32[8,128]{1,0:T(8,128)}) custom-call(s32[32]{0:T(128)} %get-tuple-element.324.table, bf16[256,1536]{1,0:T(8,128)(2,1)} %get-tuple-element.300.refs_0_.refs_8_, ...), custom_call_target="tpu_custom_call", output_to_operand_aliasing={{0}: (18, {})} | custom-call | flops 20000000000 | bytes 10000000 | tf_op jit(solution)/shard_map/attend_back/pallas_call | solution.py:502
  424.6 11.1 %fusion.53 = bf16[1536,896]{1,0:T(8,128)(2,1)} fusion(bf16[2048,1536]{1,0:T(8,128)(2,1)} %get-tuple-element.339, bf16[2048,896]{1,0:T(8,128)(2,1)} %get-tuple-element.340), kind=kOutput, calls=%fused_computation.186 | convolution fusion | flops 5637144576 | bytes 12713984 | tf_op jit(solution)/shard_map/dot_general | solution.py:19
  465.8 12.4 %collective-permute-done.74.refs_7_ = bf16[256,1536]{1,0:T(8,128)(2,1)S(1)} collective-permute-done((bf16[256,1536]{1,0:T(8,128)(2,1)}, bf16[256,1536]{1,0:T(8,128)(2,1)S(1)}, u32[]{:S(2)}, u32[]{:S(2)}) %collective-permute-start.74) | collective-permute-done | bytes 786464 | tf_op jit(solution)/shard_map/ppermute | solution.py:24
  479.6 4.8 norm_back.3
  494.0 4.5 collective-permute-start.81
  500.5 9.4 %collective-permute-done.77 = bf16[4,32,1536]{2,1,0:T(8,128)(2,1)S(1)} collective-permute-done((bf16[4,32,1536]{2,1,0:T(8,128)(2,1)S(1)}, bf16[4,32,1536]{2,1,0:T(8,128)(2,1)S(1)}, u32[]{:S(2)}, u32[]{:S(2)}) %collective-permute-start.77) | collective-permute-done | bytes 393248 | tf_op jit(solution)/shard_map/ppermute | solution.py:24
  509.9 10.8 %collective-permute-done.79 = bf16[4,32,1536]{2,1,0:T(8,128)(2,1)} collective-permute-done((bf16[4,32,1536]{2,1,0:T(8,128)(2,1)S(1)}, bf16[4,32,1536]{2,1,0:T(8,128)(2,1)}, u32[]{:S(2)}, u32[]{:S(2)}) %collective-permute-start.79) | collective-permute-done | bytes 393248 | tf_op jit(solution)/shard_map/ppermute | solution.py:24
  520.7 4.2 all-to-all-start.4
  529.9 6.0 %all-to-all-done.4.x_ref = bf16[8,48,896]{2,1,0:T(8,128)(2,1)S(1)} async-done(((bf16[8,48,896]{2,1,0:T(8,128)(2,1)}), bf16[8,48,896]{2,1,0:T(8,128)(2,1)S(1)}, u32[]{:S(2)}, u32[]{:S(2)}) %all-to-all-start.4) | async-done | bytes 688160 | tf_op jit(solution)/shard_map/all_to_all | solution.py:689
  550.8 7.2 %collective-permute-done.83 = bf16[4,32,1536]{2,1,0:T(8,128)(2,1)S(1)} collective-permute-done((bf16[4,32,1536]{2,1,0:T(8,128)(2,1)S(1)}, bf16[4,32,1536]{2,1,0:T(8,128)(2,1)S(1)}, u32[]{:S(2)}, u32[]{:S(2)}) %collective-permute-start.83) | collective-permute-done | bytes 393248 | tf_op jit(solution)/shard_map/ppermute | solution.py:33
  (423 shorter events, 249.1 us)
Async XLA Ops:
  32.2 24.6 %all-to-all-start = ((bf16[8,48,896]{2,1,0:T(8,128)(2,1)}), bf16[8,48,896]{2,1,0:T(8,128)(2,1)S(1)}, u32[]{:S(2)}, u32[]{:S(2)}) async-start(bf16[8,48,896]{2,1,0:T(8,128)(2,1)} %layout.4), calls=%async_computation | async-start | bytes 1376256 | tf_op jit(solution)/shard_map/all_to_all | solution.py:689
  35.9 83.0 %all-gather.7.cloned.1.call-start = ((), (), s32[]{:S(2)}) async-start(), calls=%async_computation.12 | async-start | bytes 3440640 | tf_op jit(solution)/shard_map/all_gather | solution.py:772
  57.8 20.6 %collective-permute-start.9 = (bf16[256,1536]{1,0:T(8,128)(2,1)S(1)}, bf16[256,1536]{1,0:T(8,128)(2,1)}, u32[]{:S(2)}, u32[]{:S(2)}) collective-permute-start(bf16[256,1536]{1,0:T(8,128)(2,1)S(1)} %bitcast.148), channel_id=1, source_target_pairs={{0,1},{1,0},{2,3},{3,2},{4,5},{5,4},{6,7},{7,6},{8,9},{9,8},{10,11... | collective-permute-start | bytes 2359304 | tf_op jit(solution)/shard_map/ppermute | solution.py:24
  59.5 23.6 %collective-permute-start.10 = (bf16[256,1536]{1,0:T(8,128)(2,1)S(1)}, bf16[256,1536]{1,0:T(8,128)(2,1)}, u32[]{:S(2)}, u32[]{:S(2)}) collective-permute-start(bf16[256,1536]{1,0:T(8,128)(2,1)S(1)} %bitcast.149), channel_id=1, source_target_pairs={{0,2},{2,0},{1,3},{3,1},{4,6},{6,4},{5,7},{7,5},{8,10},{10,8},{9,1... | collective-permute-start | bytes 2359304 | tf_op jit(solution)/shard_map/ppermute | solution.py:24
  61.0 27.1 %all-to-all-start.1 = ((bf16[4,48,1536]{2,1,0:T(8,128)(2,1)}), bf16[4,48,1536]{2,1,0:T(8,128)(2,1)S(1)}, u32[]{:S(2)}, u32[]{:S(2)}) async-start(bf16[4,48,1536]{2,1,0:T(8,128)(2,1)} %pad_maximum_fusion.9), calls=%async_computation.1 | async-start | bytes 1179648 | tf_op jit(solution)/shard_map/all_to_all | solution.py:689
  64.5 23.5 %collective-permute-start.24 = (s32[2,4]{1,0:T(2,128)S(1)}, s32[2,4]{1,0:T(2,128)S(1)}, u32[]{:S(2)}, u32[]{:S(2)}) collective-permute-start(s32[2,4]{1,0:T(2,128)S(1)} %bitcast.206), channel_id=1, source_target_pairs={{0,0},{8,1},{16,2},{24,3},{4,4},{12,5},{20,6},{28,7},{1,8},{9,9},{... | collective-permute-start | bytes 104 | tf_op jit(solution)/shard_map/ppermute | solution.py:784
  84.9 21.3 %collective-permute-start.14 = (bf16[256,1536]{1,0:T(8,128)(2,1)}, bf16[256,1536]{1,0:T(8,128)(2,1)}, u32[]{:S(2)}, u32[]{:S(2)}) collective-permute-start(bf16[256,1536]{1,0:T(8,128)(2,1)} %collective-permute-done.9.refs_1_), channel_id=1, source_target_pairs={{0,4},{4,0},{1,5},{5,1},{2,6},{6,2},{3,7},{7,3},{8,12},{12,8},{9,1... | collective-permute-start | bytes 2359304 | tf_op jit(solution)/shard_map/ppermute | solution.py:24
  86.0 20.2 %collective-permute-start.15 = (bf16[256,1536]{1,0:T(8,128)(2,1)}, bf16[256,1536]{1,0:T(8,128)(2,1)}, u32[]{:S(2)}, u32[]{:S(2)}) collective-permute-start(bf16[256,1536]{1,0:T(8,128)(2,1)} %collective-permute-done.10.refs_2_), channel_id=1, source_target_pairs={{0,4},{4,0},{1,5},{5,1},{2,6},{6,2},{3,7},{7,3},{8,12},{12,8},{9,1... | collective-permute-start | bytes 2359304 | tf_op jit(solution)/shard_map/ppermute | solution.py:24
  91.7 160.7 %all-gather.11.cloned.1.call-start = ((), (), s32[]{:S(2)}) async-start(), calls=%async_computation.14 | async-start | bytes 1966080 | tf_op jit(solution)/shard_map/all_gather | solution.py:817
  119.0 19.8 %collective-permute-start.23 = (bf16[2,32,1536]{2,1,0:T(8,128)(2,1)S(1)}, bf16[2,32,1536]{2,1,0:T(8,128)(2,1)S(1)}, u32[]{:S(2)}, u32[]{:S(2)}) collective-permute-start(bf16[2,32,1536]{2,1,0:T(8,128)(2,1)S(1)} %get-tuple-element.418), channel_id=1, source_target_pairs={{0,24},{8,16},{16,8},{24,0},{1,25},{9,17},{17,9},{25,1},{2,26},{10... | collective-permute-start | bytes 589832 | tf_op jit(solution)/shard_map/ppermute | solution.py:24
  140.7 111.6 %all-gather.9.cloned.1.call-start = ((), (), s32[]{:S(2)}) async-start(), calls=%async_computation.13 | async-start | bytes 3932160 | tf_op jit(solution)/shard_map/all_gather | solution.py:816
  168.8 271.6 %reduce-scatter.4.cloned.1.call-start = ((), (), s32[]{:S(2)}) async-start(), calls=%async_computation.9 | async-start | bytes 5898240 | tf_op jit(solution)/shard_map/reduce_scatter | solution.py:693
  172.5 24.5 %collective-permute-start.44 = (bf16[256,1536]{1,0:T(8,128)(2,1)}, bf16[256,1536]{1,0:T(8,128)(2,1)S(1)}, u32[]{:S(2)}, u32[]{:S(2)}) collective-permute-start(bf16[256,1536]{1,0:T(8,128)(2,1)} %bitcast.158), channel_id=1, source_target_pairs={{0,4},{4,0},{1,5},{5,1},{2,6},{6,2},{3,7},{7,3},{8,12},{12,8},{9,1... | collective-permute-start | bytes 2359304 | tf_op jit(solution)/shard_map/ppermute | solution.py:24
  172.5 25.5 %collective-permute-start.45 = (bf16[256,1536]{1,0:T(8,128)(2,1)}, bf16[256,1536]{1,0:T(8,128)(2,1)S(1)}, u32[]{:S(2)}, u32[]{:S(2)}) collective-permute-start(bf16[256,1536]{1,0:T(8,128)(2,1)} %copy-done.20), channel_id=1, source_target_pairs={{0,4},{4,0},{1,5},{5,1},{2,6},{6,2},{3,7},{7,3},{8,12},{12,8},{9,1... | collective-permute-start | bytes 2359304 | tf_op jit(solution)/shard_map/ppermute | solution.py:24
  179.8 40.4 %collective-permute-start.46 = (bf16[256,1536]{1,0:T(8,128)(2,1)S(1)}, bf16[256,1536]{1,0:T(8,128)(2,1)S(1)}, u32[]{:S(2)}, u32[]{:S(2)}) collective-permute-start(bf16[256,1536]{1,0:T(8,128)(2,1)S(1)} %copy-done.19), channel_id=1, source_target_pairs={{0,4},{4,0},{1,5},{5,1},{2,6},{6,2},{3,7},{7,3},{8,12},{12,8},{9,1... | collective-permute-start | bytes 2359304 | tf_op jit(solution)/shard_map/ppermute | solution.py:24
  197.1 24.0 %collective-permute-start.47 = (bf16[128,1536]{1,0:T(8,128)(2,1)S(1)}, bf16[128,1536]{1,0:T(8,128)(2,1)S(1)}, u32[]{:S(2)}, u32[]{:S(2)}) collective-permute-start(bf16[128,1536]{1,0:T(8,128)(2,1)S(1)} %copy-done.41), channel_id=1, source_target_pairs={{0,4},{4,0},{1,5},{5,1},{2,6},{6,2},{3,7},{7,3},{8,12},{12,8},{9,1... | collective-permute-start | bytes 1179656 | tf_op jit(solution)/shard_map/ppermute | solution.py:24
  198.0 23.8 %collective-permute-start.48 = (bf16[128,1536]{1,0:T(8,128)(2,1)S(1)}, bf16[128,1536]{1,0:T(8,128)(2,1)S(1)}, u32[]{:S(2)}, u32[]{:S(2)}) collective-permute-start(bf16[128,1536]{1,0:T(8,128)(2,1)S(1)} %collective-permute-done.28), channel_id=1, source_target_pairs={{0,4},{4,0},{1,5},{5,1},{2,6},{6,2},{3,7},{7,3},{8,12},{12,8},{9,1... | collective-permute-start | bytes 1179656 | tf_op jit(solution)/shard_map/ppermute | solution.py:24
  222.6 25.3 %collective-permute-start.39 = (bf16[256,1536]{1,0:T(8,128)(2,1)S(1)}, bf16[256,1536]{1,0:T(8,128)(2,1)S(1)}, u32[]{:S(2)}, u32[]{:S(2)}) collective-permute-start(bf16[256,1536]{1,0:T(8,128)(2,1)S(1)} %copy-done.29), channel_id=1, source_target_pairs={{0,4},{4,0},{1,5},{5,1},{2,6},{6,2},{3,7},{7,3},{8,12},{12,8},{9,1... | collective-permute-start | bytes 2359304 | tf_op jit(solution)/shard_map/ppermute | solution.py:24
  363.4 28.2 %collective-permute-start.57 = (bf16[128,1536]{1,0:T(8,128)(2,1)}, bf16[128,1536]{1,0:T(8,128)(2,1)S(1)}, u32[]{:S(2)}, u32[]{:S(2)}) collective-permute-start(bf16[128,1536]{1,0:T(8,128)(2,1)} %get-tuple-element.297), channel_id=1, source_target_pairs={{0,2},{2,0},{1,3},{3,1},{4,6},{6,4},{5,7},{7,5},{8,10},{10,8},{9,1... | collective-permute-start | bytes 1179656 | tf_op jit(solution)/shard_map/ppermute | solution.py:24
  364.5 27.2 %collective-permute-start.58 = (bf16[128,1536]{1,0:T(8,128)(2,1)}, bf16[128,1536]{1,0:T(8,128)(2,1)S(1)}, u32[]{:S(2)}, u32[]{:S(2)}) collective-permute-start(bf16[128,1536]{1,0:T(8,128)(2,1)} %get-tuple-element.298), channel_id=1, source_target_pairs={{0,1},{1,0},{2,3},{3,2},{4,5},{5,4},{6,7},{7,6},{8,9},{9,8},{10,11... | collective-permute-start | bytes 1179656 | tf_op jit(solution)/shard_map/ppermute | solution.py:24
  396.0 27.0 %collective-permute-start.66 = (bf16[256,1536]{1,0:T(8,128)(2,1)}, bf16[256,1536]{1,0:T(8,128)(2,1)S(1)}, u32[]{:S(2)}, u32[]{:S(2)}) collective-permute-start(bf16[256,1536]{1,0:T(8,128)(2,1)} %get-tuple-element.321), channel_id=1, source_target_pairs={{0,1},{1,0},{2,3},{3,2},{4,5},{5,4},{6,7},{7,6},{8,9},{9,8},{10,11... | collective-permute-start | bytes 2359304 | tf_op jit(solution)/shard_map/ppermute | solution.py:24
  397.3 25.8 %collective-permute-start.67 = (bf16[256,1536]{1,0:T(8,128)(2,1)}, bf16[256,1536]{1,0:T(8,128)(2,1)}, u32[]{:S(2)}, u32[]{:S(2)}) collective-permute-start(bf16[256,1536]{1,0:T(8,128)(2,1)} %get-tuple-element.322), channel_id=1, source_target_pairs={{0,2},{2,0},{1,3},{3,1},{4,6},{6,4},{5,7},{7,5},{8,10},{10,8},{9,1... | collective-permute-start | bytes 2359304 | tf_op jit(solution)/shard_map/ppermute | solution.py:24
  398.2 24.9 %all-to-all-start.3 = ((bf16[4,48,1536]{2,1,0:T(8,128)(2,1)}), bf16[4,48,1536]{2,1,0:T(8,128)(2,1)S(1)}, u32[]{:S(2)}, u32[]{:S(2)}) async-start(bf16[4,48,1536]{2,1,0:T(8,128)(2,1)} %bitcast.60), calls=%async_computation.3 | async-start | bytes 1179648 | tf_op jit(solution)/shard_map/all_to_all | solution.py:689
  401.6 119.1 %reduce-scatter.6.cloned.1.call-start = ((), (), s32[]{:S(2)}) async-start(), calls=%async_computation.10 | async-start | bytes 3440640 | tf_op jit(solution)/shard_map/reduce_scatter | solution.py:693
  401.9 33.9 %collective-permute-start.68 = (bf16[4,128,1536]{2,1,0:T(8,128)(2,1)}, bf16[4,128,1536]{2,1,0:T(8,128)(2,1)S(1)}, u32[]{:S(2)}, u32[]{:S(2)}) collective-permute-start(bf16[4,128,1536]{2,1,0:T(8,128)(2,1)} %get-tuple-element.337), channel_id=1, source_target_pairs={{0,4},{4,0},{1,5},{5,1},{2,6},{6,2},{3,7},{7,3},{8,12},{12,8},{9,1... | collective-permute-start | bytes 4718600 | tf_op jit(solution)/shard_map/ppermute | solution.py:24
  457.6 20.7 %collective-permute-start.74 = (bf16[256,1536]{1,0:T(8,128)(2,1)}, bf16[256,1536]{1,0:T(8,128)(2,1)S(1)}, u32[]{:S(2)}, u32[]{:S(2)}) collective-permute-start(bf16[256,1536]{1,0:T(8,128)(2,1)} %get-tuple-element.367), channel_id=1, source_target_pairs={{0,1},{1,0},{2,3},{3,2},{4,5},{5,4},{6,7},{7,6},{8,9},{9,8},{10,11... | collective-permute-start | bytes 2359304 | tf_op jit(solution)/shard_map/ppermute | solution.py:24
  459.0 20.6 %collective-permute-start.75 = (bf16[256,1536]{1,0:T(8,128)(2,1)}, bf16[256,1536]{1,0:T(8,128)(2,1)}, u32[]{:S(2)}, u32[]{:S(2)}) collective-permute-start(bf16[256,1536]{1,0:T(8,128)(2,1)} %get-tuple-element.368), channel_id=1, source_target_pairs={{0,2},{2,0},{1,3},{3,1},{4,6},{6,4},{5,7},{7,5},{8,10},{10,8},{9,1... | collective-permute-start | bytes 2359304 | tf_op jit(solution)/shard_map/ppermute | solution.py:24
  462.3 58.4 %all-to-all-start.5 = ((bf16[8,48,1024]{2,1,0:T(8,128)(2,1)}), bf16[8,48,1024]{2,1,0:T(8,128)(2,1)S(1)}, u32[]{:S(2)}, u32[]{:S(2)}) async-start(bf16[8,48,1024]{2,1,0:T(8,128)(2,1)} %bitcast.84), calls=%async_computation.8 | async-start | bytes 1572864 | tf_op jit(solution)/shard_map/all_to_all | solution.py:689
  485.8 24.1 %collective-permute-start.77 = (bf16[4,32,1536]{2,1,0:T(8,128)(2,1)S(1)}, bf16[4,32,1536]{2,1,0:T(8,128)(2,1)S(1)}, u32[]{:S(2)}, u32[]{:S(2)}) collective-permute-start(bf16[4,32,1536]{2,1,0:T(8,128)(2,1)S(1)} %get-tuple-element.413), channel_id=1, source_target_pairs={{0,8},{8,0},{16,24},{24,16},{1,9},{9,1},{17,25},{25,17},{2,10},{10... | collective-permute-start | bytes 1179656 | tf_op jit(solution)/shard_map/ppermute | solution.py:24
  485.9 24.0 %collective-permute-start.78 = (bf16[4,32,1536]{2,1,0:T(8,128)(2,1)S(1)}, bf16[4,32,1536]{2,1,0:T(8,128)(2,1)}, u32[]{:S(2)}, u32[]{:S(2)}) collective-permute-start(bf16[4,32,1536]{2,1,0:T(8,128)(2,1)S(1)} %get-tuple-element.412), channel_id=1, source_target_pairs={{0,16},{8,24},{16,0},{24,8},{1,17},{9,25},{17,1},{25,9},{2,18},{10... | collective-permute-start | bytes 1179656 | tf_op jit(solution)/shard_map/ppermute | solution.py:24
  488.7 32.0 %collective-permute-start.79 = (bf16[4,32,1536]{2,1,0:T(8,128)(2,1)S(1)}, bf16[4,32,1536]{2,1,0:T(8,128)(2,1)}, u32[]{:S(2)}, u32[]{:S(2)}) collective-permute-start(bf16[4,32,1536]{2,1,0:T(8,128)(2,1)S(1)} %get-tuple-element.411), channel_id=1, source_target_pairs={{0,24},{8,16},{16,8},{24,0},{1,25},{9,17},{17,9},{25,1},{2,26},{10... | collective-permute-start | bytes 1179656 | tf_op jit(solution)/shard_map/ppermute | solution.py:24
  524.9 33.5 %reduce-scatter.8.cloned.1.call-start = ((), (), s32[]{:S(2)}) async-start(), calls=%async_computation.11 | async-start | bytes 737280 | tf_op jit(solution)/shard_map/reduce_scatter | solution.py:693
  (131 other events, 1470.3 us)
Sparse Core Ops, SparseCore 0:
  57.9 57.4 all-gather.6
  140.8 36.4 all-gather.10
  178.9 62.3 all-gather.8
  328.3 84.2 reduce-scatter.3
  440.5 64.3 reduce-scatter.5
  527.8 27.1 reduce-scatter.7

commit v6 on v5

--- a/solution.py
+++ b/solution.py
@@ -758,7 +758,8 @@
     for number, gain in enumerate((norm1_gain, norm2_gain)):
         first_lanes = jnp.where(lane_of % 128 == 2 * own_heads + number, gain[:, None], first_lanes)
     packed = pack_heads(first_lanes, (w_query, w_key, w_value, w_outgate), nf, columns)
-    own = rows_to_layer(rows_to_plane(inputs[:, 0]))
+    own, w_out = tie(rows_to_plane(inputs[:, 0]), w_out)
+    own = rows_to_layer(own)
     packed, own[1] = tie(packed, own[1])
     packed = all_to_all(packed, members)
     if aligned:

time: 576 us -> 576 us (level)
    ppermute x75, waiting for transfers between devices: 157 us -> 148 us  [xor_permute(): return lax.ppermute(x, axis, [(i, i ^ step) for i in range(n)])]
  transfers between devices with their start and end apart: 97 -> 97, of which waited for: 43 -> 45; matrix products, arithmetic and copies ran while one was open for 15% -> 14% of each run, Pallas kernels for 24% -> 24%
where the time goes in v6:
time: 576 us; the launch traced here: 567 us
  waiting for transfers between devices  184 us (32%)
  Pallas kernels  161 us (28%)
  starting transfers between devices  106 us (18%)
  local copies, waits for them, and re-layouts  48.5 us (8%)
  matrix products  36.3 us (6%)
  other arithmetic  16.2 us (3%)
  between operations  15.4 us (3%)
    ppermute x75, waiting for transfers between devices, xor_permute(): return lax.ppermute(x, axis, [(i, i ^ step) for i in range(n)])  148 us
    ppermute x75, starting transfers between devices, xor_permute(): return lax.ppermute(x, axis, [(i, i ^ step) for i in range(n)])  70 us
    pallas_call x2, Pallas kernels, attend_back(): pl.pallas_call(functools.partial(attend_back_kernel, heads, depth, chunk,...  46.2 us
    pallas_call x12, Pallas kernels, rows_kernel(): pl.pallas_call(kernel, grid=(1,), in_specs=[spec for _, spec in operands]...  41.7 us
    dot_general x6, matrix products, dot(): lax.dot_general(left, right, (contract, ((), ())), preferred_element_type...  34.7 us
    unnamed x148, local copies, waits for them, and re-layouts  32.6 us
    pallas_call x2, Pallas kernels, attend(): pl.pallas_call(functools.partial(attend_kernel, heads, depth, chunk, memb...  30.5 us
    pallas_call x2, Pallas kernels, ffn(): pl.pallas_call(ffn_kernel, grid=(count,), in_specs=[blocks(width, first),...  26.3 us
  transfers between devices with their start and end apart: 97, of which 45 were waited for; matrix products, arithmetic and copies ran while one was open for 14% of the time, Pallas kernels for 24%

profile of v6, /device:TPU:0, one launch (start us, length us, event | category | flops | bytes accessed | tf_op | source)
XLA Modules:
  0.0 567.3 jit_solution(12498461142696930918)
XLA Ops:
  30.7 7.0 %collective-permute-start.4 = (bf16[2,32,1536]{2,1,0:T(8,128)(2,1)S(1)}, bf16[2,32,1536]{2,1,0:T(8,128)(2,1)S(1)}, u32[]{:S(2)}, u32[]{:S(2)}) collective-permute-start(bf16[2,32,1536]{2,1,0:T(8,128)(2,1)S(1)} %get-tuple-element.431), channel_id=1, source_target_pairs={{0,16},{8,24},{16,0},{24,8},{1,17},{9,25},{17,1},{25,9},{2,18},{10... | collective-permute-start | bytes 589832 | tf_op jit(solution)/shard_map/ppermute | solution.py:24
  45.8 9.3 %collective-permute-done.4 = bf16[2,32,1536]{2,1,0:T(8,128)(2,1)S(1)} collective-permute-done((bf16[2,32,1536]{2,1,0:T(8,128)(2,1)S(1)}, bf16[2,32,1536]{2,1,0:T(8,128)(2,1)S(1)}, u32[]{:S(2)}, u32[]{:S(2)}) %collective-permute-start.4) | collective-permute-done | bytes 196640 | tf_op jit(solution)/shard_map/ppermute | solution.py:24
  64.8 12.3 %collective-permute-done.9.refs_1_ = bf16[256,1536]{1,0:T(8,128)(2,1)} collective-permute-done((bf16[256,1536]{1,0:T(8,128)(2,1)S(1)}, bf16[256,1536]{1,0:T(8,128)(2,1)}, u32[]{:S(2)}, u32[]{:S(2)}) %collective-permute-start.9) | collective-permute-done | bytes 786464 | tf_op jit(solution)/shard_map/ppermute | solution.py:24
  77.1 4.3 collective-permute-done.10.refs_2_
  85.5 4.3 all-to-all-start.2
  92.1 5.0 collective-permute-done.11.refs_3_
  98.5 6.0 %all-to-all-done.2 = bf16[8,48,1024]{2,1,0:T(8,128)(2,1)S(1)} async-done(((bf16[8,48,1024]{2,1,0:T(8,128)(2,1)}), bf16[8,48,1024]{2,1,0:T(8,128)(2,1)S(1)}, u32[]{:S(2)}, u32[]{:S(2)}) %all-to-all-start.2) | async-done | bytes 786464 | tf_op jit(solution)/shard_map/all_to_all | solution.py:689
  121.7 15.4 %attend.2 = (bf16[2048,1536]{1,0:T(8,128)(2,1)}, bf16[1024,576]{1,0:T(8,128)(2,1)}, f32[1024,192]{1,0:T(8,128)}, f32[1024,128]{1,0:T(8,128)}, f32[1024,192]{1,0:...) custom-call(s32[32]{0:T(128)} %get-tuple-element.303.table, ...), custom_call_target="tpu_custom_call" | custom-call | flops 14000000000 | bytes 10000000 | tf_op jit(solution)/shard_map/attend/pallas_call | solution.py:464
  139.9 15.2 %attend.3 = (bf16[2048,1536]{1,0:T(8,128)(2,1)}, bf16[1024,576]{1,0:T(8,128)(2,1)}, f32[1024,192]{1,0:T(8,128)}, f32[1024,128]{1,0:T(8,128)}, f32[1024,192]{1,0:...) custom-call(s32[32]{0:T(128)} %get-tuple-element.328.table, ...), custom_call_target="tpu_custom_call", output_to_operand_aliasing={{0}: (12, {})} | custom-call | flops 14000000000 | bytes 10000000 | tf_op jit(solution)/shard_map/attend/pallas_call | solution.py:464
  180.5 7.5 %collective-permute-done.31.refs_8_ = bf16[128,1536]{1,0:T(8,128)(2,1)S(1)} collective-permute-done((bf16[128,1536]{1,0:T(8,128)(2,1)}, bf16[128,1536]{1,0:T(8,128)(2,1)S(1)}, u32[]{:S(2)}, u32[]{:S(2)}) %collective-permute-start.31) | collective-permute-done | bytes 393248 | tf_op jit(solution)/shard_map/ppermute | solution.py:24
  199.2 12.7 %collective-permute-done.33.refs_6_ = bf16[256,1536]{1,0:T(8,128)(2,1)S(1)} collective-permute-done((bf16[256,1536]{1,0:T(8,128)(2,1)}, bf16[256,1536]{1,0:T(8,128)(2,1)S(1)}, u32[]{:S(2)}, u32[]{:S(2)}) %collective-permute-start.33) | collective-permute-done | bytes 786464 | tf_op jit(solution)/shard_map/ppermute | solution.py:24
  223.4 13.3 %collective-permute-done.35 = bf16[256,1536]{1,0:T(8,128)(2,1)S(1)} collective-permute-done((bf16[256,1536]{1,0:T(8,128)(2,1)}, bf16[256,1536]{1,0:T(8,128)(2,1)S(1)}, u32[]{:S(2)}, u32[]{:S(2)}) %collective-permute-start.35) | collective-permute-done | bytes 786464 | tf_op jit(solution)/shard_map/ppermute | solution.py:24
  241.0 4.7 collective-permute-done.37
  252.2 13.2 %ffn.2 = (bf16[2048,512]{1,0:T(8,128)(2,1)}, bf16[2048,1024]{1,0:T(8,128)(2,1)}, bf16[4,256,1536]{2,1,0:T(8,128)(2,1)}) custom-call(bf16[2048,1536]{1,0:T(8,128)(2,1)} %constant_dynamic-update-slice_fusion.h_ref, bf16[2048,1536]{1,0:T(8,128)(2,1)} %constant_dynamic-update-slice_fusion.10.e_ref, bf16[1536,1024]{1,0:T(8,128)(2,1)} %bitcast.198, ...), custom_call_target="tpu_custom_call" | custom-call | flops 8053063680 | bytes 12582912 | tf_op jit(solution)/shard_map/ffn/pallas_call | solution.py:576
  265.4 13.1 %ffn.3 = (bf16[2048,512]{1,0:T(8,128)(2,1)}, bf16[2048,1024]{1,0:T(8,128)(2,1)}, bf16[4,256,1536]{2,1,0:T(8,128)(2,1)}) custom-call(bf16[2048,1536]{1,0:T(8,128)(2,1)} %constant_dynamic-update-slice_fusion.h_ref, bf16[2048,1536]{1,0:T(8,128)(2,1)} %constant_dynamic-update-slice_fusion.10.e_ref, ...), custom_call_target="tpu_custom_call", output_to_operand_aliasing={{0}: (4, {}), {1}: (5, {})} | custom-call | flops 8053063680 | bytes 12582912 | tf_op jit(solution)/shard_map/ffn/pallas_call | solution.py:576
  284.8 8.9 %fusion.51 = bf16[1536,1024]{1,0:T(8,128)(2,1)S(1)} fusion(bf16[2048,1536]{1,0:T(8,128)(2,1)} %constant_dynamic-update-slice_fusion.h_ref, bf16[2048,1024]{1,0:T(8,128)(2,1)S(1)} %copy-done.64), kind=kOutput, calls=%fused_computation.184 | convolution fusion | flops 6442450944 | bytes 13631488 | tf_op jit(solution)/shard_map/dot_general | solution.py:19
  301.4 6.3 %fusion.52 = bf16[512,1536]{1,0:T(8,128)(2,1)S(1)} fusion(bf16[2048,512]{1,0:T(8,128)(2,1)S(1)} %copy-done.17, bf16[2048,1536]{1,0:T(8,128)(2,1)} %constant_dynamic-update-slice_fusion.10.e_ref), kind=kOutput, calls=%fused_computation.185 | convolution fusion | flops 3221225472 | bytes 9961472 | tf_op jit(solution)/shard_map/dot_general | solution.py:19
  310.7 8.0 %collective-permute-done.52.refs_5_ = bf16[256,1536]{1,0:T(8,128)(2,1)S(1)} collective-permute-done((bf16[256,1536]{1,0:T(8,128)(2,1)}, bf16[256,1536]{1,0:T(8,128)(2,1)S(1)}, u32[]{:S(2)}, u32[]{:S(2)}) %collective-permute-start.52) | collective-permute-done | bytes 786464 | tf_op jit(solution)/shard_map/ppermute | solution.py:24
  319.6 5.2 norm_back.2
  335.7 7.7 %collective-permute-done.54.refs_1_.refs_9_ = bf16[256,1536]{1,0:T(8,128)(2,1)} collective-permute-done((bf16[256,1536]{1,0:T(8,128)(2,1)}, bf16[256,1536]{1,0:T(8,128)(2,1)}, u32[]{:S(2)}, u32[]{:S(2)}) %collective-permute-start.54) | collective-permute-done | bytes 786464 | tf_op jit(solution)/shard_map/ppermute | solution.py:24
  348.3 8.7 %collective-permute-done.59.refs_3_ = bf16[128,1536]{1,0:T(8,128)(2,1)S(1)} collective-permute-done((bf16[128,1536]{1,0:T(8,128)(2,1)S(1)}, bf16[128,1536]{1,0:T(8,128)(2,1)S(1)}, u32[]{:S(2)}, u32[]{:S(2)}) %collective-permute-start.59) | collective-permute-done | bytes 393248 | tf_op jit(solution)/shard_map/ppermute | solution.py:24
  366.4 25.1 %attend_back.2 = (bf16[2048,896]{1,0:T(8,128)(2,1)}, bf16[4,128,1536]{2,1,0:T(8,128)(2,1)}, bf16[4,128,1536]{2,1,0:T(8,128)(2,1)}, f32[8,128]{1,0:T(8,128)}, bf16[192,1536]{1,0:T(8,128)(2,1)}) custom-call(s32[32]{0:T(128)} %get-tuple-element.303.table, bf16[256,1536]{1,0:T(8,128)(2,1)} %get-tuple-element.304.refs_0_.refs_8_, ...), custom_call_target="tpu_custom_call" | custom-call | flops 20000000000 | bytes 10000000 | tf_op jit(solution)/shard_map/attend_back/pallas_call | solution.py:502
  401.1 21.1 %attend_back.3 = (bf16[2048,896]{1,0:T(8,128)(2,1)}, bf16[4,128,1536]{2,1,0:T(8,128)(2,1)}, bf16[4,128,1536]{2,1,0:T(8,128)(2,1)}, f32[8,128]{1,0:T(8,128)}) custom-call(s32[32]{0:T(128)} %get-tuple-element.328.table, bf16[256,1536]{1,0:T(8,128)(2,1)} %get-tuple-element.304.refs_0_.refs_8_, ...), custom_call_target="tpu_custom_call", output_to_operand_aliasing={{0}: (18, {})} | custom-call | flops 20000000000 | bytes 10000000 | tf_op jit(solution)/shard_map/attend_back/pallas_call | solution.py:502
  423.9 11.1 %fusion.53 = bf16[1536,896]{1,0:T(8,128)(2,1)} fusion(bf16[2048,1536]{1,0:T(8,128)(2,1)} %get-tuple-element.343, bf16[2048,896]{1,0:T(8,128)(2,1)} %get-tuple-element.344), kind=kOutput, calls=%fused_computation.186 | convolution fusion | flops 5637144576 | bytes 12713984 | tf_op jit(solution)/shard_map/dot_general | solution.py:19
  465.3 12.2 %collective-permute-done.74.refs_7_ = bf16[256,1536]{1,0:T(8,128)(2,1)S(1)} collective-permute-done((bf16[256,1536]{1,0:T(8,128)(2,1)}, bf16[256,1536]{1,0:T(8,128)(2,1)S(1)}, u32[]{:S(2)}, u32[]{:S(2)}) %collective-permute-start.74) | collective-permute-done | bytes 786464 | tf_op jit(solution)/shard_map/ppermute | solution.py:24
  478.9 4.8 norm_back.3
  493.1 5.0 collective-permute-start.81
  500.1 9.3 %collective-permute-done.77 = bf16[4,32,1536]{2,1,0:T(8,128)(2,1)S(1)} collective-permute-done((bf16[4,32,1536]{2,1,0:T(8,128)(2,1)S(1)}, bf16[4,32,1536]{2,1,0:T(8,128)(2,1)S(1)}, u32[]{:S(2)}, u32[]{:S(2)}) %collective-permute-start.77) | collective-permute-done | bytes 393248 | tf_op jit(solution)/shard_map/ppermute | solution.py:24
  509.4 10.8 %collective-permute-done.79 = bf16[4,32,1536]{2,1,0:T(8,128)(2,1)} collective-permute-done((bf16[4,32,1536]{2,1,0:T(8,128)(2,1)S(1)}, bf16[4,32,1536]{2,1,0:T(8,128)(2,1)}, u32[]{:S(2)}, u32[]{:S(2)}) %collective-permute-start.79) | collective-permute-done | bytes 393248 | tf_op jit(solution)/shard_map/ppermute | solution.py:24
  520.2 4.2 all-to-all-start.4
  529.4 6.0 %all-to-all-done.4.x_ref = bf16[8,48,896]{2,1,0:T(8,128)(2,1)S(1)} async-done(((bf16[8,48,896]{2,1,0:T(8,128)(2,1)}), bf16[8,48,896]{2,1,0:T(8,128)(2,1)S(1)}, u32[]{:S(2)}, u32[]{:S(2)}) %all-to-all-start.4) | async-done | bytes 688160 | tf_op jit(solution)/shard_map/all_to_all | solution.py:689
  550.2 7.2 %collective-permute-done.83 = bf16[4,32,1536]{2,1,0:T(8,128)(2,1)S(1)} collective-permute-done((bf16[4,32,1536]{2,1,0:T(8,128)(2,1)S(1)}, bf16[4,32,1536]{2,1,0:T(8,128)(2,1)S(1)}, u32[]{:S(2)}, u32[]{:S(2)}) %collective-permute-start.83) | collective-permute-done | bytes 393248 | tf_op jit(solution)/shard_map/ppermute | solution.py:33
  (423 shorter events, 247.0 us)
Async XLA Ops:
  30.7 24.5 %collective-permute-start.4 = (bf16[2,32,1536]{2,1,0:T(8,128)(2,1)S(1)}, bf16[2,32,1536]{2,1,0:T(8,128)(2,1)S(1)}, u32[]{:S(2)}, u32[]{:S(2)}) collective-permute-start(bf16[2,32,1536]{2,1,0:T(8,128)(2,1)S(1)} %get-tuple-element.431), channel_id=1, source_target_pairs={{0,16},{8,24},{16,0},{24,8},{1,17},{9,25},{17,1},{25,9},{2,18},{10... | collective-permute-start | bytes 589832 | tf_op jit(solution)/shard_map/ppermute | solution.py:24
  44.8 72.4 %all-gather.7.cloned.1.call-start = ((), (), s32[]{:S(2)}) async-start(), calls=%async_computation.12 | async-start | bytes 3440640 | tf_op jit(solution)/shard_map/all_gather | solution.py:773
  56.6 20.5 %collective-permute-start.9 = (bf16[256,1536]{1,0:T(8,128)(2,1)S(1)}, bf16[256,1536]{1,0:T(8,128)(2,1)}, u32[]{:S(2)}, u32[]{:S(2)}) collective-permute-start(bf16[256,1536]{1,0:T(8,128)(2,1)S(1)} %bitcast.148), channel_id=1, source_target_pairs={{0,1},{1,0},{2,3},{3,2},{4,5},{5,4},{6,7},{7,6},{8,9},{9,8},{10,11... | collective-permute-start | bytes 2359304 | tf_op jit(solution)/shard_map/ppermute | solution.py:24
  57.8 23.7 %collective-permute-start.10 = (bf16[256,1536]{1,0:T(8,128)(2,1)S(1)}, bf16[256,1536]{1,0:T(8,128)(2,1)}, u32[]{:S(2)}, u32[]{:S(2)}) collective-permute-start(bf16[256,1536]{1,0:T(8,128)(2,1)S(1)} %bitcast.149), channel_id=1, source_target_pairs={{0,2},{2,0},{1,3},{3,1},{4,6},{6,4},{5,7},{7,5},{8,10},{10,8},{9,1... | collective-permute-start | bytes 2359304 | tf_op jit(solution)/shard_map/ppermute | solution.py:24
  58.3 27.2 %all-to-all-start.1 = ((bf16[4,48,1536]{2,1,0:T(8,128)(2,1)}), bf16[4,48,1536]{2,1,0:T(8,128)(2,1)S(1)}, u32[]{:S(2)}, u32[]{:S(2)}) async-start(bf16[4,48,1536]{2,1,0:T(8,128)(2,1)} %pad_maximum_fusion.9), calls=%async_computation.1 | async-start | bytes 1179648 | tf_op jit(solution)/shard_map/all_to_all | solution.py:689
  61.8 23.6 %collective-permute-start.24 = (s32[2,4]{1,0:T(2,128)S(1)}, s32[2,4]{1,0:T(2,128)S(1)}, u32[]{:S(2)}, u32[]{:S(2)}) collective-permute-start(s32[2,4]{1,0:T(2,128)S(1)} %bitcast.206), channel_id=1, source_target_pairs={{0,0},{8,1},{16,2},{24,3},{4,4},{12,5},{20,6},{28,7},{1,8},{9,9},{... | collective-permute-start | bytes 104 | tf_op jit(solution)/shard_map/ppermute | solution.py:785
  83.2 21.3 %collective-permute-start.14 = (bf16[256,1536]{1,0:T(8,128)(2,1)}, bf16[256,1536]{1,0:T(8,128)(2,1)}, u32[]{:S(2)}, u32[]{:S(2)}) collective-permute-start(bf16[256,1536]{1,0:T(8,128)(2,1)} %collective-permute-done.9.refs_1_), channel_id=1, source_target_pairs={{0,4},{4,0},{1,5},{5,1},{2,6},{6,2},{3,7},{7,3},{8,12},{12,8},{9,1... | collective-permute-start | bytes 2359304 | tf_op jit(solution)/shard_map/ppermute | solution.py:24
  84.3 20.2 %collective-permute-start.15 = (bf16[256,1536]{1,0:T(8,128)(2,1)}, bf16[256,1536]{1,0:T(8,128)(2,1)}, u32[]{:S(2)}, u32[]{:S(2)}) collective-permute-start(bf16[256,1536]{1,0:T(8,128)(2,1)} %collective-permute-done.10.refs_2_), channel_id=1, source_target_pairs={{0,4},{4,0},{1,5},{5,1},{2,6},{6,2},{3,7},{7,3},{8,12},{12,8},{9,1... | collective-permute-start | bytes 2359304 | tf_op jit(solution)/shard_map/ppermute | solution.py:24
  89.8 162.4 %all-gather.11.cloned.1.call-start = ((), (), s32[]{:S(2)}) async-start(), calls=%async_computation.14 | async-start | bytes 1966080 | tf_op jit(solution)/shard_map/all_gather | solution.py:818
  117.3 19.8 %collective-permute-start.23 = (bf16[2,32,1536]{2,1,0:T(8,128)(2,1)S(1)}, bf16[2,32,1536]{2,1,0:T(8,128)(2,1)S(1)}, u32[]{:S(2)}, u32[]{:S(2)}) collective-permute-start(bf16[2,32,1536]{2,1,0:T(8,128)(2,1)S(1)} %get-tuple-element.422), channel_id=1, source_target_pairs={{0,24},{8,16},{16,8},{24,0},{1,25},{9,17},{17,9},{25,1},{2,26},{10... | collective-permute-start | bytes 589832 | tf_op jit(solution)/shard_map/ppermute | solution.py:24
  139.5 112.8 %all-gather.9.cloned.1.call-start = ((), (), s32[]{:S(2)}) async-start(), calls=%async_computation.13 | async-start | bytes 3932160 | tf_op jit(solution)/shard_map/all_gather | solution.py:817
  168.3 271.3 %reduce-scatter.4.cloned.1.call-start = ((), (), s32[]{:S(2)}) async-start(), calls=%async_computation.9 | async-start | bytes 5898240 | tf_op jit(solution)/shard_map/reduce_scatter | solution.py:693
  172.1 24.7 %collective-permute-start.44 = (bf16[256,1536]{1,0:T(8,128)(2,1)}, bf16[256,1536]{1,0:T(8,128)(2,1)S(1)}, u32[]{:S(2)}, u32[]{:S(2)}) collective-permute-start(bf16[256,1536]{1,0:T(8,128)(2,1)} %bitcast.158), channel_id=1, source_target_pairs={{0,4},{4,0},{1,5},{5,1},{2,6},{6,2},{3,7},{7,3},{8,12},{12,8},{9,1... | collective-permute-start | bytes 2359304 | tf_op jit(solution)/shard_map/ppermute | solution.py:24
  172.1 25.7 %collective-permute-start.45 = (bf16[256,1536]{1,0:T(8,128)(2,1)}, bf16[256,1536]{1,0:T(8,128)(2,1)S(1)}, u32[]{:S(2)}, u32[]{:S(2)}) collective-permute-start(bf16[256,1536]{1,0:T(8,128)(2,1)} %copy-done.20), channel_id=1, source_target_pairs={{0,4},{4,0},{1,5},{5,1},{2,6},{6,2},{3,7},{7,3},{8,12},{12,8},{9,1... | collective-permute-start | bytes 2359304 | tf_op jit(solution)/shard_map/ppermute | solution.py:24
  179.5 40.4 %collective-permute-start.46 = (bf16[256,1536]{1,0:T(8,128)(2,1)S(1)}, bf16[256,1536]{1,0:T(8,128)(2,1)S(1)}, u32[]{:S(2)}, u32[]{:S(2)}) collective-permute-start(bf16[256,1536]{1,0:T(8,128)(2,1)S(1)} %copy-done.19), channel_id=1, source_target_pairs={{0,4},{4,0},{1,5},{5,1},{2,6},{6,2},{3,7},{7,3},{8,12},{12,8},{9,1... | collective-permute-start | bytes 2359304 | tf_op jit(solution)/shard_map/ppermute | solution.py:24
  196.8 24.0 %collective-permute-start.47 = (bf16[128,1536]{1,0:T(8,128)(2,1)S(1)}, bf16[128,1536]{1,0:T(8,128)(2,1)S(1)}, u32[]{:S(2)}, u32[]{:S(2)}) collective-permute-start(bf16[128,1536]{1,0:T(8,128)(2,1)S(1)} %copy-done.41), channel_id=1, source_target_pairs={{0,4},{4,0},{1,5},{5,1},{2,6},{6,2},{3,7},{7,3},{8,12},{12,8},{9,1... | collective-permute-start | bytes 1179656 | tf_op jit(solution)/shard_map/ppermute | solution.py:24
  197.8 23.8 %collective-permute-start.48 = (bf16[128,1536]{1,0:T(8,128)(2,1)S(1)}, bf16[128,1536]{1,0:T(8,128)(2,1)S(1)}, u32[]{:S(2)}, u32[]{:S(2)}) collective-permute-start(bf16[128,1536]{1,0:T(8,128)(2,1)S(1)} %collective-permute-done.28), channel_id=1, source_target_pairs={{0,4},{4,0},{1,5},{5,1},{2,6},{6,2},{3,7},{7,3},{8,12},{12,8},{9,1... | collective-permute-start | bytes 1179656 | tf_op jit(solution)/shard_map/ppermute | solution.py:24
  222.4 25.4 %collective-permute-start.39 = (bf16[256,1536]{1,0:T(8,128)(2,1)S(1)}, bf16[256,1536]{1,0:T(8,128)(2,1)S(1)}, u32[]{:S(2)}, u32[]{:S(2)}) collective-permute-start(bf16[256,1536]{1,0:T(8,128)(2,1)S(1)} %copy-done.29), channel_id=1, source_target_pairs={{0,4},{4,0},{1,5},{5,1},{2,6},{6,2},{3,7},{7,3},{8,12},{12,8},{9,1... | collective-permute-start | bytes 2359304 | tf_op jit(solution)/shard_map/ppermute | solution.py:24
  362.6 28.9 %collective-permute-start.57 = (bf16[128,1536]{1,0:T(8,128)(2,1)}, bf16[128,1536]{1,0:T(8,128)(2,1)S(1)}, u32[]{:S(2)}, u32[]{:S(2)}) collective-permute-start(bf16[128,1536]{1,0:T(8,128)(2,1)} %get-tuple-element.301), channel_id=1, source_target_pairs={{0,2},{2,0},{1,3},{3,1},{4,6},{6,4},{5,7},{7,5},{8,10},{10,8},{9,1... | collective-permute-start | bytes 1179656 | tf_op jit(solution)/shard_map/ppermute | solution.py:24
  364.3 27.3 %collective-permute-start.58 = (bf16[128,1536]{1,0:T(8,128)(2,1)}, bf16[128,1536]{1,0:T(8,128)(2,1)S(1)}, u32[]{:S(2)}, u32[]{:S(2)}) collective-permute-start(bf16[128,1536]{1,0:T(8,128)(2,1)} %get-tuple-element.302), channel_id=1, source_target_pairs={{0,1},{1,0},{2,3},{3,2},{4,5},{5,4},{6,7},{7,6},{8,9},{9,8},{10,11... | collective-permute-start | bytes 1179656 | tf_op jit(solution)/shard_map/ppermute | solution.py:24
  395.9 26.7 %collective-permute-start.66 = (bf16[256,1536]{1,0:T(8,128)(2,1)}, bf16[256,1536]{1,0:T(8,128)(2,1)S(1)}, u32[]{:S(2)}, u32[]{:S(2)}) collective-permute-start(bf16[256,1536]{1,0:T(8,128)(2,1)} %get-tuple-element.325), channel_id=1, source_target_pairs={{0,1},{1,0},{2,3},{3,2},{4,5},{5,4},{6,7},{7,6},{8,9},{9,8},{10,11... | collective-permute-start | bytes 2359304 | tf_op jit(solution)/shard_map/ppermute | solution.py:24
  397.1 25.6 %collective-permute-start.67 = (bf16[256,1536]{1,0:T(8,128)(2,1)}, bf16[256,1536]{1,0:T(8,128)(2,1)}, u32[]{:S(2)}, u32[]{:S(2)}) collective-permute-start(bf16[256,1536]{1,0:T(8,128)(2,1)} %get-tuple-element.326), channel_id=1, source_target_pairs={{0,2},{2,0},{1,3},{3,1},{4,6},{6,4},{5,7},{7,5},{8,10},{10,8},{9,1... | collective-permute-start | bytes 2359304 | tf_op jit(solution)/shard_map/ppermute | solution.py:24
  397.4 25.3 %all-to-all-start.3 = ((bf16[4,48,1536]{2,1,0:T(8,128)(2,1)}), bf16[4,48,1536]{2,1,0:T(8,128)(2,1)S(1)}, u32[]{:S(2)}, u32[]{:S(2)}) async-start(bf16[4,48,1536]{2,1,0:T(8,128)(2,1)} %bitcast.60), calls=%async_computation.3 | async-start | bytes 1179648 | tf_op jit(solution)/shard_map/all_to_all | solution.py:689
  400.8 119.4 %reduce-scatter.6.cloned.1.call-start = ((), (), s32[]{:S(2)}) async-start(), calls=%async_computation.10 | async-start | bytes 3440640 | tf_op jit(solution)/shard_map/reduce_scatter | solution.py:693
  401.1 33.9 %collective-permute-start.68 = (bf16[4,128,1536]{2,1,0:T(8,128)(2,1)}, bf16[4,128,1536]{2,1,0:T(8,128)(2,1)S(1)}, u32[]{:S(2)}, u32[]{:S(2)}) collective-permute-start(bf16[4,128,1536]{2,1,0:T(8,128)(2,1)} %get-tuple-element.341), channel_id=1, source_target_pairs={{0,4},{4,0},{1,5},{5,1},{2,6},{6,2},{3,7},{7,3},{8,12},{12,8},{9,1... | collective-permute-start | bytes 4718600 | tf_op jit(solution)/shard_map/ppermute | solution.py:24
  456.8 20.7 %collective-permute-start.74 = (bf16[256,1536]{1,0:T(8,128)(2,1)}, bf16[256,1536]{1,0:T(8,128)(2,1)S(1)}, u32[]{:S(2)}, u32[]{:S(2)}) collective-permute-start(bf16[256,1536]{1,0:T(8,128)(2,1)} %get-tuple-element.371), channel_id=1, source_target_pairs={{0,1},{1,0},{2,3},{3,2},{4,5},{5,4},{6,7},{7,6},{8,9},{9,8},{10,11... | collective-permute-start | bytes 2359304 | tf_op jit(solution)/shard_map/ppermute | solution.py:24
  458.2 20.6 %collective-permute-start.75 = (bf16[256,1536]{1,0:T(8,128)(2,1)}, bf16[256,1536]{1,0:T(8,128)(2,1)}, u32[]{:S(2)}, u32[]{:S(2)}) collective-permute-start(bf16[256,1536]{1,0:T(8,128)(2,1)} %get-tuple-element.372), channel_id=1, source_target_pairs={{0,2},{2,0},{1,3},{3,1},{4,6},{6,4},{5,7},{7,5},{8,10},{10,8},{9,1... | collective-permute-start | bytes 2359304 | tf_op jit(solution)/shard_map/ppermute | solution.py:24
  461.7 58.5 %all-to-all-start.5 = ((bf16[8,48,1024]{2,1,0:T(8,128)(2,1)}), bf16[8,48,1024]{2,1,0:T(8,128)(2,1)S(1)}, u32[]{:S(2)}, u32[]{:S(2)}) async-start(bf16[8,48,1024]{2,1,0:T(8,128)(2,1)} %bitcast.84), calls=%async_computation.8 | async-start | bytes 1572864 | tf_op jit(solution)/shard_map/all_to_all | solution.py:689
  485.1 24.4 %collective-permute-start.77 = (bf16[4,32,1536]{2,1,0:T(8,128)(2,1)S(1)}, bf16[4,32,1536]{2,1,0:T(8,128)(2,1)S(1)}, u32[]{:S(2)}, u32[]{:S(2)}) collective-permute-start(bf16[4,32,1536]{2,1,0:T(8,128)(2,1)S(1)} %get-tuple-element.417), channel_id=1, source_target_pairs={{0,8},{8,0},{16,24},{24,16},{1,9},{9,1},{17,25},{25,17},{2,10},{10... | collective-permute-start | bytes 1179656 | tf_op jit(solution)/shard_map/ppermute | solution.py:24
  485.3 24.2 %collective-permute-start.78 = (bf16[4,32,1536]{2,1,0:T(8,128)(2,1)S(1)}, bf16[4,32,1536]{2,1,0:T(8,128)(2,1)}, u32[]{:S(2)}, u32[]{:S(2)}) collective-permute-start(bf16[4,32,1536]{2,1,0:T(8,128)(2,1)S(1)} %get-tuple-element.416), channel_id=1, source_target_pairs={{0,16},{8,24},{16,0},{24,8},{1,17},{9,25},{17,1},{25,9},{2,18},{10... | collective-permute-start | bytes 1179656 | tf_op jit(solution)/shard_map/ppermute | solution.py:24
  488.2 32.0 %collective-permute-start.79 = (bf16[4,32,1536]{2,1,0:T(8,128)(2,1)S(1)}, bf16[4,32,1536]{2,1,0:T(8,128)(2,1)}, u32[]{:S(2)}, u32[]{:S(2)}) collective-permute-start(bf16[4,32,1536]{2,1,0:T(8,128)(2,1)S(1)} %get-tuple-element.415), channel_id=1, source_target_pairs={{0,24},{8,16},{16,8},{24,0},{1,25},{9,17},{17,9},{25,1},{2,26},{10... | collective-permute-start | bytes 1179656 | tf_op jit(solution)/shard_map/ppermute | solution.py:24
  524.4 33.5 %reduce-scatter.8.cloned.1.call-start = ((), (), s32[]{:S(2)}) async-start(), calls=%async_computation.11 | async-start | bytes 737280 | tf_op jit(solution)/shard_map/reduce_scatter | solution.py:693
  (131 other events, 1476.4 us)
Sparse Core Ops, SparseCore 0:
  56.7 56.8 all-gather.6
  139.6 37.1 all-gather.10
  178.3 62.3 all-gather.8
  327.8 84.0 reduce-scatter.3
  439.7 64.6 reduce-scatter.5
  527.2 27.2 reduce-scatter.7
